TPU v7x, 32 devices: a whole 2x2x4 slice. The times are simulated.
32 devices in a mesh: teacher: 4 (over x, core), vocab: 8 (over z, y).
Axes of the slice: x: 2, y: 2, z: 4, core: 2. Of those that a mesh axis runs over, the one named last changes fastest.
Arguments:
- teacher_hidden: bfloat16 [4, 512, 4096], P('teacher', 'vocab'), may hold values from -28 to 28
- teacher_gain: float32 [4, 4096], P('teacher'), may hold values from 0.25 to 1.75
- teacher_head: bfloat16 [4, 4096, 77824], P('teacher', None, 'vocab'), may hold values from -2 to 2
- student_hidden: bfloat16 [512, 896], P(('teacher', 'vocab')), may hold values from -10 to 10
- student_head: bfloat16 [896, 77824], P(None, 'vocab'), may hold values from -2 to 2
- targets: int32 [512], P(('teacher', 'vocab')), may hold values from 0 to 77823
Outputs:
- row_loss: float32 [512], P(('teacher', 'vocab'))
- grad_hidden: bfloat16 [512, 896], P(('teacher', 'vocab'))
- grad_head: float32 [896, 77824], P('teacher', 'vocab')
All inputs are finite; a program needn't handle non-finite values.
Results may differ from a plain program's by a relative error of at most 0.0098.
The roundings to bfloat16 on the way count: a program that leaves them out, or rounds other values in their place, can miss the bound.
Values may be sent and summed in bfloat16 or wider, within the bound.
No kernel may reach another device: no remote copies, remote signals or barrier semaphores. Data moves between devices by JAX's collectives and lax.ppermute only.
A program may use at most 256 MiB of HBM per device.

v0:
```python
import jax
import jax.numpy as jnp
from jax import lax
from jax.sharding import PartitionSpec as P

EPSILON = 1e-06
LABEL_WEIGHT = 0.5


def joined(shard, axis, combine):
    everything = jax.tree.map(lambda part: lax.all_gather(part, axis), shard)
    first = jax.tree.map(lambda part: part[0], everything)

    def turn(k, so_far):
        return combine(so_far, jax.tree.map(lambda part: part[k], everything))

    return lax.fori_loop(1, lax.axis_size(axis), turn, first)


def normed_logits(block_rows, gain_row, head_cols, weight):
    hidden = block_rows.astype(jnp.float32)
    scale_rows = lax.rsqrt(jnp.mean(hidden * hidden, axis=1, keepdims=True) + EPSILON)
    normed = (hidden * scale_rows * gain_row[None, :]).astype(jnp.bfloat16)
    return jnp.dot(normed, head_cols, preferred_element_type=jnp.float32) * weight


def rescale_factors(first_peak, second_peak):
    joined_peak = jnp.maximum(first_peak, second_peak)
    return (joined_peak, jnp.exp(first_peak - joined_peak), jnp.exp(second_peak - joined_peak))


def combine_apart(first, second):
    target_peak, first_factor, second_factor = rescale_factors(first[0], second[0])
    student_peak, first_scale, second_scale = rescale_factors(first[2], second[2])
    return (
        target_peak,
        first[1] * first_factor + second[1] * second_factor,
        student_peak,
        first[3] * first_scale + second[3] * second_scale,
    )


def on_device(teacher_hidden, teacher_gain, teacher_head, student_hidden, student_head, targets):
    teachers = lax.axis_size("teacher")
    weight = 1.0 / teachers
    gain_row = teacher_gain[0]
    head_cols = teacher_head[0]
    own_rows = teacher_hidden[0]
    gathered = lax.all_gather(own_rows, "vocab", axis=0, tiled=True)
    mean_logits = lax.psum_scatter(
        normed_logits(gathered, gain_row, head_cols, weight),
        "teacher",
        scatter_dimension=0,
        tiled=True,
    )
    student_rows, target_rows = (
        lax.all_gather(student_hidden, "vocab", axis=0, tiled=True),
        lax.all_gather(targets, "vocab", axis=0, tiled=True),
    )
    student_logits = jnp.dot(student_rows, student_head, preferred_element_type=jnp.float32)
    vocab_slice = student_head.shape[1]
    columns = lax.axis_index("vocab") * vocab_slice + lax.broadcasted_iota(
        jnp.int32, (1, vocab_slice), 1
    )
    is_target = target_rows[:, None] == columns
    target_peak = jnp.max(mean_logits, axis=1)
    target_exp = jnp.exp(mean_logits - target_peak[:, None])
    target_total = jnp.sum(target_exp, axis=1)
    student_peak = jnp.max(student_logits, axis=1)
    student_exp = jnp.exp(student_logits - student_peak[:, None])
    student_total = jnp.sum(student_exp, axis=1)
    merged = joined(
        (target_peak, target_total, student_peak, student_total), "vocab", combine_apart
    )
    target_norm = merged[0] + jnp.log(merged[1])
    student_norm = merged[2] + jnp.log(merged[3])
    log_target = mean_logits - target_norm[:, None]
    log_student = student_logits - student_norm[:, None]
    target_prob = target_exp * jnp.exp(target_peak - target_norm)[:, None]
    student_prob = student_exp * jnp.exp(student_peak - student_norm)[:, None]
    partial_value = jnp.sum(
        target_prob * (log_target - log_student), axis=1
    ) - LABEL_WEIGHT * jnp.sum(jnp.where(is_target, log_student, 0.0), axis=1)
    row_loss = lax.psum_scatter(partial_value, "vocab", scatter_dimension=0, tiled=True)
    grad_logits = (
        (1.0 + LABEL_WEIGHT) * student_prob
        - target_prob
        - LABEL_WEIGHT * is_target.astype(jnp.float32)
    ).astype(jnp.bfloat16)
    grad_hidden = lax.psum_scatter(
        lax.dot_general(
            grad_logits, student_head, (((1,), (1,)), ((), ())), preferred_element_type=jnp.float32
        ),
        "vocab",
        scatter_dimension=0,
        tiled=True,
    ).astype(jnp.bfloat16)
    grad_head = lax.psum_scatter(
        lax.dot_general(
            student_rows, grad_logits, (((0,), (0,)), ((), ())), preferred_element_type=jnp.float32
        ),
        "teacher",
        scatter_dimension=0,
        tiled=True,
    )
    return (row_loss, grad_hidden, grad_head)


def solution(mesh):
    return jax.shard_map(
        on_device,
        mesh=mesh,
        in_specs=(
            P("teacher", "vocab", None),
            P("teacher", None),
            P("teacher", None, "vocab"),
            P(("teacher", "vocab"), None),
            P(None, "vocab"),
            P(("teacher", "vocab")),
        ),
        out_specs=(P(("teacher", "vocab")), P(("teacher", "vocab"), None), P("teacher", "vocab")),
        check_vma=False,
    )
```

profile of v0, /device:TPU:0, one launch (start us, length us, event | category | flops | bytes accessed | tf_op | source)
XLA Modules:
  0.0 659.6 jit_solution(13611442912253352236)
XLA Ops:
  7.2 0.0 all-gather.11.cloned.1.call-start
  7.2 0.7 all-gather.11.cloned.1.call-update
  7.9 0.0 reduce-scatter.6.cloned.1.call-start
  7.9 78.3 %all-gather.11.cloned.1.call-done = bf16[1,512,4096]{2,1,0:T(8,128)(2,1)} async-done(((bf16[1,64,4096]{2,1,0:T(8,128)(2,1)}), bf16[1,512,4096]{2,1,0:T(8,128)(2,1)}) %all-gather.11.cloned.1.call-update) | async-done | bytes 4194320 | tf_op jit(solution)/shard_map/all_gather | solution.py:49
  86.3 3.1 fusion.15
  89.3 51.8 %fusion.12 = f32[512,9728]{1,0:T(8,128)} fusion(bf16[1,4096,9728]{2,1,0:T(8,128)(2,1)} %param.10, bf16[1,512,4096]{2,1,0:T(8,128)(2,1)} %all-gather.11.cloned.1.call-done, f32[4096]{0:T(1024)} %bitcast.79, f32[512]{0:T(512)S(1)} %add_rsqrt_fusion), kind=kOutput, calls=%fused_computation.17 | convolution fusion | flops 40815558656 | bytes 103827456 | tf_op jit(solution)/shard_map/dot_general | solution.py:24
  141.1 0.0 copy-start.2
  141.1 0.0 copy-start.3
  141.1 0.0 copy-start.1
  141.1 0.0 reduce-scatter.6.cloned.1.call-update
  141.2 0.0 reduce-scatter.8.cloned.1.call-start
  141.2 0.6 copy-done.2
  141.8 0.6 fusion.29
  143.0 0.0 copy-done.3
  143.0 0.2 dynamic-update-slice
  143.3 9.6 %all-reduce = s32[128]{0:T(128)S(1)} all-reduce(s32[128]{0:T(128)S(1)} %dynamic-update-slice), channel_id=1, replica_groups=mesh['teacher'=4,'vocab'=8] {'vocab'}, use_global_device_ids=true, to_apply=%add | all-reduce | flops 128 | bytes 1024
  152.9 0.0 copy-done.1
  152.9 30.7 %all_gather.38 = bf16[128,896]{1,0:T(8,128)(2,1)S(1)} all-gather(bf16[16,896]{1,0:T(8,128)(2,1)S(1)} %copy-done.1), channel_id=1, replica_groups=mesh['teacher'=4,'vocab'=8] {'vocab'}, dimensions={0}, use_global_device_ids=true | all-gather | bytes 258048 | tf_op jit(solution)/shard_map/all_gather | solution.py:57
  183.6 7.8 %fusion.30 = (f32[128]{0:T(128)S(1)}, f32[128,9728]{1,0:T(8,128)S(1)}) fusion(bf16[128,896]{1,0:T(8,128)(2,1)S(1)} %all_gather.38, bf16[896,9728]{1,0:T(8,128)(2,1)} %param.12), kind=kOutput, calls=%fused_computation.48 | convolution fusion | flops 2232614912 | bytes 22643200 | tf_op jit(solution)/shard_map/dot_general | solution.py:60
  191.4 0.0 copy-start
  191.4 2.3 copy-done
  193.7 0.9 fusion.22
  194.6 18.6 %all-gather.8 = f32[8,1,128]{2,1,0:T(1,128)S(1)} all-gather(f32[1,1,128]{2,1,0:T(1,128)S(1)} %bitcast.77), channel_id=6, replica_groups=mesh['teacher'=4,'vocab'=8] {'vocab'}, dimensions={0}, use_global_device_ids=true | all-gather | bytes 4608 | tf_op jit(solution)/shard_map/all_gather | solution.py:11
  213.1 16.1 %all-gather.7 = f32[8,1,128]{2,1,0:T(1,128)S(1)} all-gather(f32[1,1,128]{2,1,0:T(1,128)S(1)} %bitcast.71), channel_id=5, replica_groups=mesh['teacher'=4,'vocab'=8] {'vocab'}, dimensions={0}, use_global_device_ids=true | all-gather | bytes 4608 | tf_op jit(solution)/shard_map/all_gather | solution.py:11
  229.3 56.6 %reduce-scatter.6.cloned.1.call-done = f32[128,9728]{1,0:T(8,128)} async-done(((f32[512,9728]{1,0:T(8,128)}), f32[128,9728]{1,0:T(8,128)}) %reduce-scatter.6.cloned.1.call-update) | async-done | bytes 4980752 | tf_op jit(solution)/shard_map/reduce_scatter | solution.py:50
  285.9 2.7 reduce_max.18
  288.6 3.2 fusion.21
  291.8 20.4 %all-gather.6 = f32[8,1,128]{2,1,0:T(1,128)S(1)} all-gather(f32[1,1,128]{2,1,0:T(1,128)S(1)} %bitcast.78), channel_id=4, replica_groups=mesh['teacher'=4,'vocab'=8] {'vocab'}, dimensions={0}, use_global_device_ids=true | all-gather | bytes 4608 | tf_op jit(solution)/shard_map/all_gather | solution.py:11
  312.2 16.3 %all-gather.5 = f32[8,1,128]{2,1,0:T(1,128)S(1)} all-gather(f32[1,1,128]{2,1,0:T(1,128)S(1)} %bitcast.72), channel_id=3, replica_groups=mesh['teacher'=4,'vocab'=8] {'vocab'}, dimensions={0}, use_global_device_ids=true | all-gather | bytes 4608 | tf_op jit(solution)/shard_map/all_gather | solution.py:11
  328.5 0.3 while.21
  328.9 7.2 %fusion.18 = (f32[128]{0:T(128)S(1)}, f32[128]{0:T(128)S(1)}, bf16[128,9728]{1,0:T(8,128)(2,1)S(1)}) fusion(f32[128,9728]{1,0:T(8,128)} %copy-done, s32[9728]{0:T(1024)S(1)} %iota_add_fusion, f32[128]{0:T(128)S(1)} %get-tuple-element.261, s32[128]{0:T(128)S(1)} %all-reduce, f32[128,9728]{1,0:T(8,128)} %reduce-scatter.6.cloned.1.call-done, ...), kind=kLoop, calls=%fused_computation.25 | loop fusion | flops 21167872 | bytes 12495360 | tf_op jit(solution)/shard_map/reduce_sum | solution.py:83
  336.1 12.2 %fusion.31 = f32[128,896]{1,0:T(8,128)} fusion(bf16[128,9728]{1,0:T(8,128)(2,1)S(1)} %get-tuple-element.266, bf16[896,9728]{1,0:T(8,128)(2,1)} %param.12), kind=kOutput, calls=%fused_computation.49 | convolution fusion | flops 2231369728 | bytes 20381696 | tf_op jit(solution)/shard_map/dot_general | solution.py:91
  348.4 0.0 reduce-scatter.8.cloned.1.call-update
  348.4 0.0 reduce-scatter.10.cloned.1.call-start
  348.4 13.7 %convolution_bitcast_fusion = f32[896,9728]{0,1:T(8,128)} fusion(bf16[128,9728]{1,0:T(8,128)(2,1)S(1)} %get-tuple-element.266, bf16[128,896]{1,0:T(8,128)(2,1)S(1)} %all_gather.38), kind=kOutput, calls=%fused_computation.16 | convolution fusion | flops 2231369728 | bytes 37584896 | tf_op jit(solution)/shard_map/dot_general | solution.py:99
  362.1 36.4 %copy.11 = f32[896,9728]{1,0:T(8,128)} copy(f32[896,9728]{0,1:T(8,128)} %convolution_bitcast_fusion) | data formatting | bytes 69730304
  398.6 0.0 reduce-scatter.10.cloned.1.call-update
  399.3 19.2 %all-reduce.1 = f32[128]{0:T(128)S(1)} all-reduce(f32[128]{0:T(128)S(1)} %multiply_subtract_fusion), channel_id=8, replica_groups=mesh['teacher'=4,'vocab'=8] {'vocab'}, use_global_device_ids=true, to_apply=%region_10.11.clone | all-reduce | flops 128 | bytes 1024
  418.4 0.6 dynamic-slice.2
  419.0 0.0 reduce-scatter.8.cloned.1.call-done
  419.0 1.4 convert_element_type.16
  420.4 232.6 %reduce-scatter.10.cloned.1.call-done = f32[224,9728]{1,0:T(8,128)} async-done(((f32[896,9728]{1,0:T(8,128)}), f32[224,9728]{1,0:T(8,128)}) %reduce-scatter.10.cloned.1.call-update) | async-done | bytes 8716304
  (16 shorter events, 0.2 us)
Async XLA Ops:
  7.2 79.1 %all-gather.11.cloned.1.call-start = ((), (), s32[]{:S(2)}) async-start(), calls=%async_computation.5 | async-start | bytes 4718592 | tf_op jit(solution)/shard_map/all_gather | solution.py:49
  7.9 278.0 %reduce-scatter.6.cloned.1.call-start = ((), (), s32[]{:S(2)}) async-start(), calls=%async_computation.3 | async-start | bytes 24903680 | tf_op jit(solution)/shard_map/reduce_scatter | solution.py:50
  141.1 0.7 copy-start.2
  141.1 1.9 copy-start.3
  141.1 11.7 %copy-start.1 = (bf16[16,896]{1,0:T(8,128)(2,1)S(1)}, bf16[16,896]{1,0:T(8,128)(2,1)}, u32[]{:S(2)}) copy-start(bf16[16,896]{1,0:T(8,128)(2,1)} %param.11) | copy-start | bytes 86020
  141.2 277.8 %reduce-scatter.8.cloned.1.call-start = ((), (), s32[]{:S(2)}) async-start(), calls=%async_computation.4 | async-start | bytes 516096 | tf_op jit(solution)/shard_map/reduce_scatter | solution.py:90
  191.4 2.3 copy-start
  348.4 304.7 %reduce-scatter.10.cloned.1.call-start = ((), (), s32[]{:S(2)}) async-start(), calls=%async_computation.6 | async-start | bytes 43581440
Sparse Core Ops, SparseCore 0:
  10.1 76.0 all-gather.10
  141.3 144.5 reduce-scatter.5
  348.5 59.5 reduce-scatter.7
  411.2 241.8 reduce-scatter.9
where the time goes:
time: 661 us; the launch traced here: 660 us
  waiting for transfers between devices  368 us (56%)
  blocking collectives  131 us (20%)
  matrix products  85.5 us (13%)
  local copies, waits for them, and re-layouts  40.7 us (6%)
  other arithmetic  18.8 us (3%)
  between operations  15.2 us (2%)
    unnamed x5, waiting for transfers between devices  233 us
    all_gather x1, waiting for transfers between devices, on_device(): gathered = lax.all_gather(own_rows, 'vocab', axis=0, tiled=True)  78.3 us
    all_gather x4, blocking collectives, joined(): everything = jax.tree.map(lambda part: lax.all_gather(part, axis), shard)  71.4 us
    reduce_scatter x1, waiting for transfers between devices, on_device(): lax.psum_scatter(normed_logits(gathered, gain_row, head_cols, weight), 't...  56.6 us
    dot_general x1, matrix products, normed_logits(): jnp.dot(normed, head_cols, preferred_element_type=jnp.float32) * weight  51.8 us
    unnamed x13, local copies, waits for them, and re-layouts  40.7 us
    all_gather x1, blocking collectives, on_device(): lax.all_gather(student_hidden, 'vocab', axis=0, tiled=True)  30.7 us
    unnamed x2, blocking collectives  28.7 us
  transfers between devices with their start and end apart: 4, of which 3 were waited for; matrix products, arithmetic and copies ran while one was open for 9% of the time, Pallas kernels for 0%

commit v1 on v0

v1 whole, which is shorter than its diff:
```python
import functools

import jax
import jax.numpy as jnp
from jax import lax
from jax.experimental import pallas as pl
from jax.experimental.pallas import tpu as pltpu
from jax.sharding import PartitionSpec as P

EPSILON = 1e-06
LABEL_WEIGHT = 0.5
VMEM_LIMIT = 48 * 2**20


def column_plan(columns, parts):
    tile = next((w for w in (512, 256, 128) if columns % w == 0), columns)
    tiles = columns // tile
    parts = min(parts, tiles)
    edges = [(tiles * k + parts - 1) // parts for k in range(parts + 1)]
    return tile, [(a, b - a) for a, b in zip(edges[:-1], edges[1:])]


def teacher_kernel(half, weight, x_ref, w_ref, sibling_ref, own_ref):
    sums = jnp.dot(x_ref[...], w_ref[0], preferred_element_type=jnp.float32) * weight
    sibling_ref[...] = sums[:half]
    own_ref[...] = sums[half:]


def teacher_chunk(x, head, weight, tile, first, count):
    rows, depth = x.shape
    half = rows // 2
    return pl.pallas_call(
        functools.partial(teacher_kernel, half, weight),
        grid=(count,),
        in_specs=[
            pl.BlockSpec((rows, depth), lambda i: (0, 0)),
            pl.BlockSpec((1, depth, tile), lambda i: (0, 0, i + first)),
        ],
        out_specs=[pl.BlockSpec((half, tile), lambda i: (0, i))] * 2,
        out_shape=[jax.ShapeDtypeStruct((half, tile * count), jnp.float32)] * 2,
        compiler_params=pltpu.CompilerParams(vmem_limit_bytes=VMEM_LIMIT),
        cost_estimate=pl.CostEstimate(
            flops=2 * rows * depth * tile * count,
            bytes_accessed=2 * depth * tile * count + 4 * rows * tile * count,
            transcendentals=0,
        ),
    )(x, head)


def head_grad_kernel(parts, *refs):
    h_refs, g_refs, out_ref = refs[:parts], refs[parts : 2 * parts], refs[-1]
    total = None
    for h_ref, g_ref in zip(h_refs, g_refs):
        term = jnp.dot(h_ref[...], g_ref[...], preferred_element_type=jnp.float32)
        total = term if total is None else total + term
    out_ref[...] = total


def head_grad_chunk(h_parts, g_parts, so_far, columns, tile, first, count):
    parts, features, rows = len(h_parts), h_parts[0].shape[0], h_parts[0].shape[1]
    in_specs = [pl.BlockSpec((features, rows), lambda i: (0, 0))] * parts
    in_specs += [pl.BlockSpec((rows, tile), lambda i: (0, i))] * parts
    operands = list(h_parts) + list(g_parts)
    alias = {}
    if so_far is not None:
        alias = {len(operands): 0}
        in_specs.append(pl.BlockSpec(memory_space=pl.ANY))
        operands.append(so_far)
    return pl.pallas_call(
        functools.partial(head_grad_kernel, parts),
        grid=(count,),
        in_specs=in_specs,
        out_specs=pl.BlockSpec((features, tile), lambda i: (0, i + first)),
        out_shape=jax.ShapeDtypeStruct((features, columns), jnp.float32),
        input_output_aliases=alias,
        compiler_params=pltpu.CompilerParams(vmem_limit_bytes=VMEM_LIMIT),
        cost_estimate=pl.CostEstimate(
            flops=2 * features * rows * parts * tile * count,
            bytes_accessed=(2 * rows * parts + 4 * features) * tile * count,
            transcendentals=0,
        ),
    )(*operands)


class Vocab:
    def __init__(self):
        self.n = lax.axis_size("vocab")
        self.me = lax.axis_index("vocab")
        self.ring = self.n // 2 if self.n in (4, 8) else 0

    def from_ahead(self, a, k):
        n = self.ring
        pairs = [(v, 2 * ((v // 2 - k) % n) + v % 2) for v in range(self.n)]
        return lax.ppermute(a, "vocab", pairs)

    def to_ahead(self, a, k):
        n = self.ring
        pairs = [(v, 2 * ((v // 2 + k) % n) + v % 2) for v in range(self.n)]
        return lax.ppermute(a, "vocab", pairs)

    def across(self, a):
        return lax.ppermute(a, "vocab", [(v, v ^ 1) for v in range(self.n)])

    def slot_of(self, v):
        if not self.ring:
            return v
        return 2 * ((v // 2 - self.me // 2) % self.ring) + ((v % 2) ^ (self.me % 2))

    def holder_of(self, slot):
        if not self.ring:
            return slot
        return 2 * ((slot // 2 + self.me // 2) % self.ring) + ((slot % 2) ^ (self.me % 2))

    def turned(self, a, way):
        if not self.ring:
            return a
        pairs = a.reshape((self.ring, 2) + a.shape[1:])
        start = (way * (self.me // 2)) % self.ring
        pairs = lax.dynamic_slice_in_dim(
            jnp.concatenate([pairs, pairs]), start, self.ring
        )
        return jnp.where(self.me % 2 == 1, pairs[:, ::-1], pairs).reshape(a.shape)

    def gather(self, arrays):
        if not self.ring:
            gathered = [lax.all_gather(a, "vocab") for a in arrays]
            return [[g[k] for k in range(self.n)] for g in gathered]
        slots = [[None] * self.n for _ in arrays]
        now = list(arrays)
        for step in range(self.ring):
            later = [self.from_ahead(a, 1) for a in now] if step < self.ring - 1 else []
            other = [self.across(a) for a in now]
            for s, a, b in zip(slots, now, other):
                s[2 * step], s[2 * step + 1] = a, b
            if later:
                later, other = lax.optimization_barrier((later, other))
                for s, b in zip(slots, other):
                    s[2 * step + 1] = b
            now = later
        return slots

    def log_sum(self, peak, total):
        def merge(peaks, totals):
            top = functools.reduce(jnp.maximum, peaks)
            return top, sum(t * jnp.exp(p - top) for p, t in zip(peaks, totals))

        both = jnp.stack([peak, total])
        if not self.ring:
            every = lax.all_gather(both, "vocab")
            top = jnp.max(every[:, 0], axis=0)
            return top + jnp.log(jnp.sum(every[:, 1] * jnp.exp(every[:, 0] - top), axis=0))
        every = [both] + [self.from_ahead(both, k) for k in range(1, self.ring)]
        peak, total = merge([e[0] for e in every], [e[1] for e in every])
        both = jnp.stack([peak, total])
        other = self.across(both)
        peak, total = merge([both[0], other[0]], [both[1], other[1]])
        return peak + jnp.log(total)

    def sum_scatter(self, a):
        if not self.ring:
            return lax.psum_scatter(a, "vocab", scatter_dimension=0)
        pairs = a.reshape((self.ring, 2) + a.shape[1:])
        mine = pairs[:, 0] + self.across(pairs[:, 1])
        return mine[0] + sum(self.to_ahead(mine[k], k) for k in range(1, self.ring))


def on_device(teacher_hidden, teacher_gain, teacher_head, student_hidden, student_head, targets):
    f32, bf16, f16 = jnp.float32, jnp.bfloat16, jnp.float16
    teachers = lax.axis_size("teacher")
    t = lax.axis_index("teacher")
    vocab = Vocab()
    nv, v = vocab.n, vocab.me
    weight = 1.0 / teachers
    features, columns = student_head.shape
    block, depth = teacher_hidden.shape[1:]
    piece = block // teachers
    rows = nv * piece

    def sibling(a):
        return lax.ppermute(a, "teacher", [(k, k ^ 1) for k in range(teachers)])

    def facing(a):
        return lax.ppermute(a, "teacher", [(k, k ^ 2) for k in range(teachers)])

    owners = t ^ jnp.array([3, 1, 2, 0], jnp.int32)

    hidden = teacher_hidden[0].astype(f32)
    scale_rows = lax.rsqrt(jnp.mean(hidden * hidden, axis=1, keepdims=True) + EPSILON)
    normed = (hidden * scale_rows * teacher_gain[0][None, :]).astype(bf16)
    normed = normed.reshape(teachers, piece, depth)
    normed = jnp.stack(
        [lax.dynamic_index_in_dim(normed, owners[k], keepdims=False) for k in range(teachers)]
    )

    low = targets % 128
    middle = (targets // 128) % 128
    high = targets // 16384
    digits = jnp.stack([low, middle, high], axis=1).astype(bf16)
    lanes = -features % 128 + 128
    digits = jnp.pad(digits, ((0, 0), (0, lanes - 3)))
    student_block = jnp.concatenate([student_hidden, digits], axis=1)

    normed_slots, student_slots = vocab.gather([normed, student_block])
    x = jnp.stack(normed_slots, axis=1).reshape(teachers * rows, depth)

    students = jnp.stack(student_slots)
    students = jnp.stack([students, sibling(students)])
    students = jnp.concatenate([students, facing(students)])
    token_block = teachers * vocab.holder_of(jnp.arange(nv))[None, :] + owners[:, None]
    where = (t ^ (token_block // nv)) * nv + vocab.slot_of(token_block % nv)
    token = piece * where.reshape(-1)[:, None] + jnp.arange(piece)[None, :]
    moved = token.reshape(-1)[:, None] == jnp.arange(teachers * rows)[None, :]
    students = jnp.dot(
        moved.astype(bf16),
        students.reshape(teachers * rows, -1),
        preferred_element_type=f32,
    )
    students = students.astype(bf16).reshape(teachers, rows, -1)
    h_rows = students[..., :features]
    digits = students[2:, :, features : features + 3].astype(jnp.int32)
    target_rows = digits[..., 0] + 128 * digits[..., 1] + 16384 * digits[..., 2]

    share = features // teachers
    h_share = lax.dynamic_slice_in_dim(h_rows, t * share, share, axis=2)
    h_share = jnp.swapaxes(h_share, 1, 2)

    student_logits = jnp.dot(
        h_rows[2:].reshape(2 * rows, features), student_head, preferred_element_type=f32
    ).reshape(2, rows, columns)

    def by_holder(a):
        return vocab.turned(a.reshape(nv, piece), -1)

    def by_slot(a):
        return vocab.turned(a, 1).reshape(rows)

    near_student = student_logits[1]
    student_peak = jnp.max(near_student, axis=1)
    student_total = jnp.sum(jnp.exp(near_student - student_peak[:, None]), axis=1)
    student_norm = by_slot(vocab.log_sum(by_holder(student_peak), by_holder(student_total)))

    tile, chunks = column_plan(columns, 4)
    near, far, peaks, totals = [], [], [], []
    for first, count in chunks:
        for_sibling, for_own = teacher_chunk(x, teacher_head, weight, tile, first, count)
        from_sibling = sibling(for_sibling)
        to_face = (for_own[:rows] + from_sibling[:rows]).astype(f16)
        kept = (for_own[rows:] + from_sibling[rows:]).astype(f16)
        near_logits = kept.astype(f32) + facing(to_face).astype(f32)
        far_logits = (to_face, facing(kept))
        peak = jnp.max(near_logits, axis=1)
        peaks.append(peak)
        totals.append(jnp.sum(jnp.exp(near_logits - peak[:, None]), axis=1))
        near.append(near_logits)
        far.append(far_logits)

    target_peak = functools.reduce(jnp.maximum, peaks)
    target_total = sum(s * jnp.exp(p - target_peak) for p, s in zip(peaks, totals))
    target_norm = by_slot(vocab.log_sum(by_holder(target_peak), by_holder(target_total)))
    norms = jnp.stack([target_norm, student_norm])
    far_norms = facing(norms)

    def probabilities(mean_logits, logits, norm, wanted, first_column):
        log_target = mean_logits - norm[0][:, None]
        log_student = logits - norm[1][:, None]
        place = v * columns + first_column
        is_target = wanted[:, None] == place + lax.broadcasted_iota(
            jnp.int32, (1, logits.shape[1]), 1
        )
        target_prob = jnp.exp(log_target)
        grad = (
            (1.0 + LABEL_WEIGHT) * jnp.exp(log_student)
            - target_prob
            - LABEL_WEIGHT * is_target.astype(f32)
        ).astype(bf16)
        return log_target, log_student, is_target, target_prob, grad

    losses, hidden_terms, near_grads = [], [], []
    for k, (first, count) in enumerate(chunks):
        a, b = first * tile, (first + count) * tile
        log_target, log_student, is_target, target_prob, grad = probabilities(
            near[k], student_logits[1, :, a:b], norms, target_rows[1], a
        )
        losses.append(
            jnp.sum(target_prob * (log_target - log_student), axis=1)
            - LABEL_WEIGHT * jnp.sum(jnp.where(is_target, log_student, 0.0), axis=1)
        )
        near_grads.append(grad)
        hidden_terms.append(
            lax.dot_general(
                grad, student_head[:, a:b], (((1,), (1,)), ((), ())), preferred_element_type=f32
            )
        )
    own_terms = jnp.concatenate(
        [sum(hidden_terms), jnp.broadcast_to(sum(losses)[:, None], (rows, lanes))], axis=1
    )
    own_sums = vocab.sum_scatter(own_terms.reshape(nv, piece, features + lanes))
    devices = teachers * nv
    own_sums = lax.ppermute(
        own_sums,
        ("teacher", "vocab"),
        [(k, teachers * (k % nv) + k // nv) for k in range(devices)],
    )
    grad_hidden = own_sums[:, :features].astype(bf16)
    row_loss = own_sums[:, features]

    grad_head = None
    for k, (first, count) in enumerate(chunks):
        a, b = first * tile, (first + count) * tile
        far_mean = far[k][0].astype(f32) + far[k][1].astype(f32)
        far_grad = probabilities(
            far_mean, student_logits[0, :, a:b], far_norms, target_rows[0], a
        )[-1]
        g_parts = [sibling(far_grad), sibling(near_grads[k]), far_grad, near_grads[k]]
        grad_head = head_grad_chunk(
            list(h_share), g_parts, grad_head, columns, tile, first, count
        )
    return (row_loss, grad_hidden, grad_head)


def solution(mesh):
    return jax.shard_map(
        on_device,
        mesh=mesh,
        in_specs=(
            P("teacher", "vocab", None),
            P("teacher", None),
            P("teacher", None, "vocab"),
            P(("teacher", "vocab"), None),
            P(None, "vocab"),
            P(("teacher", "vocab")),
        ),
        out_specs=(P(("teacher", "vocab")), P(("teacher", "vocab"), None), P("teacher", "vocab")),
        check_vma=False,
    )
```

time: 661 us -> 365 us (0.55)
  waiting for transfers between devices: 368 us -> 119 us
  blocking collectives: 131 us -> 0 us
  Pallas kernels: 0 us -> 83 us
  matrix products: 85.5 us -> 25.4 us
  starting transfers between devices: 0.16 us -> 55.3 us
  other arithmetic: 18.8 us -> 46.9 us
  local copies, waits for them, and re-layouts: 40.7 us -> 21.4 us
    unnamed x5 -> x0, waiting for transfers between devices: 233 us -> none
    ppermute x0 -> x50, waiting for transfers between devices: none -> 119 us  [the longest x10 66 us: facing(): return lax.ppermute(a, 'teacher', [(k, k ^ 2) for k in range(teachers)])]
    all_gather x5 -> x0, blocking collectives: 102 us -> none  [the longest x4 71.4 us: joined(): everything = jax.tree.map(lambda part: lax.all_gather(part, axis), shard)]
    pallas_call x0 -> x8, Pallas kernels: none -> 83 us  [the longest x4 62.8 us: teacher_chunk(): pl.pallas_call(functools.partial(teacher_kernel, half, weight), grid=(cou...]
    all_gather x1 -> x0, waiting for transfers between devices: 78.3 us -> none  [on_device(): gathered = lax.all_gather(own_rows, 'vocab', axis=0, tiled=True)]
    dot_general x4 -> x6, matrix products: 85.5 us -> 25.4 us  [the longest x4 15.3 us: on_device(): lax.dot_general(grad, student_head[:, a:b], (((1,), (1,)), ((), ())), pre...]
    reduce_scatter x2 -> x0, waiting for transfers between devices: 56.6 us -> none  [the longest x1 56.6 us: on_device(): lax.psum_scatter(normed_logits(gathered, gain_row, head_cols, weight), 't...]
    ppermute x0 -> x50, starting transfers between devices: none -> 55.3 us  [the longest x12 19.2 us: from_ahead(): return lax.ppermute(a, 'vocab', pairs)]
  transfers between devices with their start and end apart: 4 -> 50, of which waited for: 3 -> 21; matrix products, arithmetic and copies ran while one was open for 9% -> 24% of each run, Pallas kernels for 0% -> 22%
where the time goes in v1:
time: 365 us; the launch traced here: 360 us
  waiting for transfers between devices  119 us (33%)
  Pallas kernels  83 us (23%)
  starting transfers between devices  55.3 us (15%)
  other arithmetic  46.9 us (13%)
  matrix products  25.4 us (7%)
  local copies, waits for them, and re-layouts  21.4 us (6%)
  between operations  8.85 us (2%)
    ppermute x10, waiting for transfers between devices, facing(): return lax.ppermute(a, 'teacher', [(k, k ^ 2) for k in range(teachers)])  66 us
    pallas_call x4, Pallas kernels, teacher_chunk(): pl.pallas_call(functools.partial(teacher_kernel, half, weight), grid=(cou...  62.8 us
    ppermute x11, waiting for transfers between devices, across(): return lax.ppermute(a, 'vocab', [(v, v ^ 1) for v in range(self.n)])  39 us
    pallas_call x4, Pallas kernels, head_grad_chunk(): pl.pallas_call(functools.partial(head_grad_kernel, parts), grid=(count,),...  20.2 us
    ppermute x12, starting transfers between devices, from_ahead(): return lax.ppermute(a, 'vocab', pairs)  19.2 us
    dot_general x4, matrix products, on_device(): lax.dot_general(grad, student_head[:, a:b], (((1,), (1,)), ((), ())), pre...  15.3 us
    unnamed x54, local copies, waits for them, and re-layouts  13 us
    ppermute x10, starting transfers between devices, facing(): return lax.ppermute(a, 'teacher', [(k, k ^ 2) for k in range(teachers)])  12.2 us
  transfers between devices with their start and end apart: 50, of which 21 were waited for; matrix products, arithmetic and copies ran while one was open for 24% of the time, Pallas kernels for 22%

profile of v1, /device:TPU:0, one launch (start us, length us, event | category | flops | bytes accessed | tf_op | source)
XLA Modules:
  0.0 360.0 jit_solution(14159512527738293103)
XLA Ops:
  2.2 5.0 %collective-permute-start.1 = (bf16[16,1024]{1,0:T(8,128)(2,1)S(1)}, bf16[16,1024]{1,0:T(8,128)(2,1)S(1)}, u32[]{:S(2)}, u32[]{:S(2)}) collective-permute-start(bf16[16,1024]{1,0:T(8,128)(2,1)S(1)} %fusion.75), channel_id=1, source_target_pairs={{0,6},{1,7},{2,0},{3,1},{4,2},{5,3},{6,4},{7,5},{8,14},{9,15},{10,... | collective-permute-start | bytes 98312 | tf_op jit(solution)/shard_map/ppermute | solution.py:94
  7.2 1.5 collective-permute-start.3
  22.6 10.9 %collective-permute-done.2 = bf16[4,16,4096]{2,1,0:T(8,128)(2,1)S(1)} collective-permute-done((bf16[4,16,4096]{2,1,0:T(8,128)(2,1)S(1)}, bf16[4,16,4096]{2,1,0:T(8,128)(2,1)S(1)}, u32[]{:S(2)}, u32[]{:S(2)}) %collective-permute-start.2) | collective-permute-done | bytes 524320 | tf_op jit(solution)/shard_map/ppermute | solution.py:102
  33.7 1.5 collective-permute-start.7
  35.2 2.2 collective-permute-start.5
  39.7 9.3 %collective-permute-done.6 = bf16[4,16,4096]{2,1,0:T(8,128)(2,1)S(1)} collective-permute-done((bf16[4,16,4096]{2,1,0:T(8,128)(2,1)S(1)}, bf16[4,16,4096]{2,1,0:T(8,128)(2,1)S(1)}, u32[]{:S(2)}, u32[]{:S(2)}) %collective-permute-start.6) | collective-permute-done | bytes 524320 | tf_op jit(solution)/shard_map/ppermute | solution.py:102
  49.4 1.8 collective-permute-start.11
  51.2 1.8 collective-permute-start.9
  55.5 9.0 %collective-permute-done.10 = bf16[4,16,4096]{2,1,0:T(8,128)(2,1)S(1)} collective-permute-done((bf16[4,16,4096]{2,1,0:T(8,128)(2,1)S(1)}, bf16[4,16,4096]{2,1,0:T(8,128)(2,1)S(1)}, u32[]{:S(2)}, u32[]{:S(2)}) %collective-permute-start.10) | collective-permute-done | bytes 524320 | tf_op jit(solution)/shard_map/ppermute | solution.py:102
  67.4 1.5 collective-permute-done.12
  70.5 1.6 collective-permute-start.14
  72.1 3.4 collective-permute-done.19
  76.3 13.7 %shard_map.97 = (f32[256,2048]{1,0:T(8,128)}, f32[256,2048]{1,0:T(8,128)S(1)}) custom-call(bf16[512,4096]{1,0:T(8,128)(2,1)} %bitcast.274, bf16[1,4096,9728]{2,1,0:T(8,128)(2,1)} %w_ref.7), custom_call_target="tpu_custom_call" | custom-call | flops 8589934592 | bytes 20971520 | tf_op jit(solution)/shard_map/pallas_call | solution.py:32
  91.4 16.1 %shard_map.96 = (f32[256,2560]{1,0:T(8,128)}, f32[256,2560]{1,0:T(8,128)S(1)}) custom-call(bf16[512,4096]{1,0:T(8,128)(2,1)} %bitcast.275, bf16[1,4096,9728]{2,1,0:T(8,128)(2,1)} %w_ref.7), custom_call_target="tpu_custom_call" | custom-call | flops 10737418240 | bytes 26214400 | tf_op jit(solution)/shard_map/pallas_call | solution.py:32
  107.5 17.0 %shard_map.94 = (f32[256,2560]{1,0:T(8,128)}, f32[256,2560]{1,0:T(8,128)S(1)}) custom-call(bf16[512,4096]{1,0:T(8,128)(2,1)} %bitcast.276, bf16[1,4096,9728]{2,1,0:T(8,128)(2,1)} %w_ref.7), custom_call_target="tpu_custom_call" | custom-call | flops 10737418240 | bytes 26214400 | tf_op jit(solution)/shard_map/pallas_call | solution.py:32
  125.0 16.1 %shard_map.95 = (f32[256,2560]{1,0:T(8,128)}, f32[256,2560]{1,0:T(8,128)S(1)}) custom-call(bf16[512,4096]{1,0:T(8,128)(2,1)} %bitcast.277, bf16[1,4096,9728]{2,1,0:T(8,128)(2,1)} %w_ref.7), custom_call_target="tpu_custom_call" | custom-call | flops 10737418240 | bytes 26214400 | tf_op jit(solution)/shard_map/pallas_call | solution.py:32
  142.7 9.3 %fusion.110 = f32[256,9728]{1,0:T(8,128)S(1)} fusion(bf16[256,896]{1,0:T(8,128)(2,1)S(1)} %bitcast.278, bf16[896,9728]{1,0:T(8,128)(2,1)} %param.11), kind=kOutput, calls=%fused_computation.264 | convolution fusion | flops 4462739456 | bytes 27852800 | tf_op jit(solution)/shard_map/dot_general | solution.py:227
  152.3 3.5 copy-done.7
  158.0 2.2 collective-permute-start.16
  160.2 1.8 fusion.66
  162.6 1.5 collective-permute-start.27
  164.2 2.2 collective-permute-start.15
  166.5 1.6 collective-permute-done.15
  168.8 7.1 %collective-permute-done.27 = f16[128,2048]{1,0:T(8,128)(2,1)S(1)} collective-permute-done((f16[128,2048]{1,0:T(8,128)(2,1)S(1)}, f16[128,2048]{1,0:T(8,128)(2,1)S(1)}, u32[]{:S(2)}, u32[]{:S(2)}) %collective-permute-start.27) | collective-permute-done | bytes 524320 | tf_op jit(solution)/shard_map/ppermute | solution.py:183
  175.8 2.4 fusion.68
  178.4 2.7 fusion.37
  181.1 1.5 collective-permute-start.25
  182.6 2.4 fusion.41
  185.6 2.4 fusion.39
  189.4 1.5 collective-permute-start.23
  190.9 8.2 %collective-permute-done.25 = f16[128,2560]{1,0:T(8,128)(2,1)} collective-permute-done((f16[128,2560]{1,0:T(8,128)(2,1)}, f16[128,2560]{1,0:T(8,128)(2,1)}, u32[]{:S(2)}, u32[]{:S(2)}) %collective-permute-start.25) | collective-permute-done | bytes 655392 | tf_op jit(solution)/shard_map/ppermute | solution.py:183
  199.1 2.3 fusion.55
  201.4 1.5 exponential_reduce_fusion.1
  203.0 10.1 %collective-permute-done.21 = f16[128,2560]{1,0:T(8,128)(2,1)} collective-permute-done((f16[128,2560]{1,0:T(8,128)(2,1)}, f16[128,2560]{1,0:T(8,128)(2,1)}, u32[]{:S(2)}, u32[]{:S(2)}) %collective-permute-start.21) | collective-permute-done | bytes 655392 | tf_op jit(solution)/shard_map/ppermute | solution.py:183
  213.1 2.6 fusion.53
  215.8 1.7 exponential_reduce_fusion.3
  217.6 7.0 %collective-permute-done.23 = f16[128,2560]{1,0:T(8,128)(2,1)} collective-permute-done((f16[128,2560]{1,0:T(8,128)(2,1)}, f16[128,2560]{1,0:T(8,128)(2,1)}, u32[]{:S(2)}, u32[]{:S(2)}) %collective-permute-start.23) | collective-permute-done | bytes 655392 | tf_op jit(solution)/shard_map/ppermute | solution.py:183
  224.6 3.1 fusion.54
  227.8 1.7 exponential_reduce_fusion.2
  229.8 2.8 collective-permute-start.30
  233.2 1.8 collective-permute-start.28
  235.3 1.8 collective-permute-done.29
  237.8 1.6 collective-permute-start.38
  239.9 1.5 collective-permute-start.47
  242.5 1.6 collective-permute-start.37
  244.0 4.9 %fusion.10 = (f32[128]{0:T(128)S(1)}, f32[128]{0:T(128)S(1)}, f32[128]{0:T(128)S(1)}, f32[128]{0:T(128)S(1)}, f32[128]{0:T(128)S(1)}, /*index=5*/f32[128]{0:T(12...) fusion(f32[2,128,9728]{2,1,0:T(8,128)} %bitcast.269, ...), kind=kLoop, calls=%fused_computation.21 | loop fusion | flops 15727872 | bytes 9865728 | tf_op jit(solution)/shard_map/reduce_sum | solution.py:286
  249.0 4.0 %fusion = f32[128,896]{1,0:T(8,128)S(1)} fusion(bf16[128,2560]{1,0:T(8,128)(2,1)S(1)} %get-tuple-element.65.refs_7_, bf16[896,9728]{1,0:T(8,128)(2,1)} %param.11), kind=kOutput, calls=%fused_computation.2 | convolution fusion | flops 587202560 | bytes 5701632 | tf_op jit(solution)/shard_map/dot_general | solution.py:290
  253.0 3.9 %fusion.2 = f32[128,896]{1,0:T(8,128)S(1)} fusion(bf16[128,2560]{1,0:T(8,128)(2,1)S(1)} %get-tuple-element.66.refs_7_, bf16[896,9728]{1,0:T(8,128)(2,1)} %param.11), kind=kOutput, calls=%fused_computation.4 | convolution fusion | flops 587202560 | bytes 5701632 | tf_op jit(solution)/shard_map/dot_general | solution.py:290
  256.9 33.6 %collective-permute-done.37 = f32[2,128]{1,0:T(2,128)S(1)} collective-permute-done((f32[2,128]{1,0:T(2,128)S(1)}, f32[2,128]{1,0:T(2,128)S(1)}, u32[]{:S(2)}, u32[]{:S(2)}) %collective-permute-start.37) | collective-permute-done | bytes 1056 | tf_op jit(solution)/shard_map/ppermute | solution.py:183
  290.6 3.3 fusion.58
  293.9 3.5 fusion.6
  297.4 3.9 %fusion.50 = f32[128,896]{1,0:T(8,128)S(1)} fusion(f32[128,896]{1,0:T(8,128)S(1)} %fusion.6, f32[128,896]{1,0:T(8,128)S(1)} %fusion, f32[128,896]{1,0:T(8,128)S(1)} %fusion.2, bf16[128,2560]{1,0:T(8,128)(2,1)S(1)} %get-tuple-element.64.refs_7_, bf16[896,9728]{1,0:T(8,128)(2,1)} %param.11), kind=kOutput, calls=%fused_computation.78 | convolution fusion | flops 587546624 | bytes 7077888 | tf_op jit(solution)/shard_map/dot_general | solution.py:290
  301.5 1.5 collective-permute-start.32
  303.0 4.9 %collective-permute-done.32 = f32[4,16,1024]{2,1,0:T(8,128)S(1)} collective-permute-done((f32[4,16,1024]{2,1,0:T(8,128)S(1)}, f32[4,16,1024]{2,1,0:T(8,128)S(1)}, u32[]{:S(2)}, u32[]{:S(2)}) %collective-permute-start.32) | collective-permute-done | bytes 262176 | tf_op jit(solution)/shard_map/ppermute | solution.py:102
  308.0 4.1 %fusion.22 = (bf16[128,2560]{1,0:T(8,128)(2,1)}, bf16[128,2560]{1,0:T(8,128)(2,1)S(1)}, bf16[128,2560]{1,0:T(8,128)(2,1)S(1)}) fusion(f32[2,128,9728]{2,1,0:T(8,128)S(1)} %bitcast.273, f16[128,2560]{1,0:T(8,128)(2,1)} %collective-permute-done.47, f16[128,2560]{1,0:T(8,128)(2,1)} %fusion.41, f32[128]{0:T(128)S(1)} %get-tuple-element.106, ...), kind=kLoop, calls=%fused_computation.34 | loop fusion | flops 10813440 | bytes 9862656 | tf_op jit(solution)/shard_map/convert_element_type | solution.py:275
  312.7 2.0 collective-permute-start.34
  316.1 3.3 collective-permute-done.34
  320.5 5.1 %collective-permute-done.33 = f32[16,1024]{1,0:T(8,128)S(1)} collective-permute-done((f32[16,1024]{1,0:T(8,128)S(1)}, f32[16,1024]{1,0:T(8,128)S(1)}, u32[]{:S(2)}, u32[]{:S(2)}) %collective-permute-start.33) | collective-permute-done | bytes 65568 | tf_op jit(solution)/shard_map/ppermute | solution.py:99
  326.3 2.9 collective-permute-start.45
  329.2 1.6 collective-permute-start.43
  339.8 5.2 %shard_map.98.refs_8_ = f32[224,9728]{1,0:T(8,128)} custom-call(bf16[224,128]{1,0:T(8,128)(2,1)S(1)} %get-tuple-element.82.refs_0_, bf16[224,128]{1,0:T(8,128)(2,1)S(1)} %get-tuple-element.81.refs_1_, bf16[224,128]{1,0:T(8,128)(2,1)S(1)} %get-tuple-element.80.refs_2_, bf16[224,128]{1,0:T(8,128)(2,1)S(1)} %get-tuple-element.79.refs_3_, ...), custom_call_target="tpu_custom_call" | custom-call | flops 587202560 | bytes 4915200 | tf_op jit(solution)/shard_map/pallas_call | solution.py:69
  345.0 5.2 %shard_map.99.refs_8_ = f32[224,9728]{1,0:T(8,128)} custom-call(bf16[224,128]{1,0:T(8,128)(2,1)S(1)} %get-tuple-element.82.refs_0_, bf16[224,128]{1,0:T(8,128)(2,1)S(1)} %get-tuple-element.81.refs_1_, bf16[224,128]{1,0:T(8,128)(2,1)S(1)} %get-tuple-element.80.refs_2_, ...), custom_call_target="tpu_custom_call", output_to_operand_aliasing={{}: (8, {})} | custom-call | flops 587202560 | bytes 4915200 | tf_op jit(solution)/shard_map/pallas_call | solution.py:69
  350.2 5.2 %shard_map.100.refs_8_ = f32[224,9728]{1,0:T(8,128)} custom-call(bf16[224,128]{1,0:T(8,128)(2,1)S(1)} %get-tuple-element.82.refs_0_, bf16[224,128]{1,0:T(8,128)(2,1)S(1)} %get-tuple-element.81.refs_1_, bf16[224,128]{1,0:T(8,128)(2,1)S(1)} %get-tuple-element.80.refs_2_, ...), custom_call_target="tpu_custom_call", output_to_operand_aliasing={{}: (8, {})} | custom-call | flops 587202560 | bytes 4915200 | tf_op jit(solution)/shard_map/pallas_call | solution.py:69
  355.5 4.5 %shard_map.101 = f32[224,9728]{1,0:T(8,128)} custom-call(bf16[224,128]{1,0:T(8,128)(2,1)S(1)} %get-tuple-element.82.refs_0_, bf16[224,128]{1,0:T(8,128)(2,1)S(1)} %get-tuple-element.81.refs_1_, bf16[224,128]{1,0:T(8,128)(2,1)S(1)} %get-tuple-element.80.refs_2_, bf16[224,128]{1,0:T(8,128)(2,1)S(1)} %get-tuple-element.79.refs_3_, ...), custom_call_target="tpu_custom_call", output_to_operand_aliasing={{}: (8, {})} | custom-call | flops 469762048 | bytes 3932160 | tf_op jit(solution)/shard_map/pallas_call | solution.py:69
  (208 shorter events, 44.6 us)
Async XLA Ops:
  2.2 20.4 %collective-permute-start.1 = (bf16[16,1024]{1,0:T(8,128)(2,1)S(1)}, bf16[16,1024]{1,0:T(8,128)(2,1)S(1)}, u32[]{:S(2)}, u32[]{:S(2)}) collective-permute-start(bf16[16,1024]{1,0:T(8,128)(2,1)S(1)} %fusion.75), channel_id=1, source_target_pairs={{0,6},{1,7},{2,0},{3,1},{4,2},{5,3},{6,4},{7,5},{8,14},{9,15},{10,... | collective-permute-start | bytes 98312 | tf_op jit(solution)/shard_map/ppermute | solution.py:94
  7.2 15.4 %collective-permute-start.3 = (bf16[16,1024]{1,0:T(8,128)(2,1)S(1)}, bf16[16,1024]{1,0:T(8,128)(2,1)S(1)}, u32[]{:S(2)}, u32[]{:S(2)}) collective-permute-start(bf16[16,1024]{1,0:T(8,128)(2,1)S(1)} %fusion.75), channel_id=1, source_target_pairs={{0,1},{1,0},{2,3},{3,2},{4,5},{5,4},{6,7},{7,6},{8,9},{9,8},{10,11... | collective-permute-start | bytes 98312 | tf_op jit(solution)/shard_map/ppermute | solution.py:102
  20.3 13.2 %collective-permute-start.2 = (bf16[4,16,4096]{2,1,0:T(8,128)(2,1)S(1)}, bf16[4,16,4096]{2,1,0:T(8,128)(2,1)S(1)}, u32[]{:S(2)}, u32[]{:S(2)}) collective-permute-start(bf16[4,16,4096]{2,1,0:T(8,128)(2,1)S(1)} %pad_maximum_fusion.1), channel_id=1, source_target_pairs={{0,1},{1,0},{2,3},{3,2},{4,5},{5,4},{6,7},{7,6},{8,9},{9,8},{10,11... | collective-permute-start | bytes 1572872 | tf_op jit(solution)/shard_map/ppermute | solution.py:102
  20.9 12.8 %collective-permute-start = (bf16[4,16,4096]{2,1,0:T(8,128)(2,1)S(1)}, bf16[4,16,4096]{2,1,0:T(8,128)(2,1)S(1)}, u32[]{:S(2)}, u32[]{:S(2)}) collective-permute-start(bf16[4,16,4096]{2,1,0:T(8,128)(2,1)S(1)} %pad_maximum_fusion.1), channel_id=1, source_target_pairs={{0,6},{1,7},{2,0},{3,1},{4,2},{5,3},{6,4},{7,5},{8,14},{9,15},{10,... | collective-permute-start | bytes 1572872 | tf_op jit(solution)/shard_map/ppermute | solution.py:94
  33.7 5.9 %collective-permute-start.7 = (bf16[16,1024]{1,0:T(8,128)(2,1)S(1)}, bf16[16,1024]{1,0:T(8,128)(2,1)S(1)}, u32[]{:S(2)}, u32[]{:S(2)}) collective-permute-start(bf16[16,1024]{1,0:T(8,128)(2,1)S(1)} %collective-permute-done.1), channel_id=1, source_target_pairs={{0,1},{1,0},{2,3},{3,2},{4,5},{5,4},{6,7},{7,6},{8,9},{9,8},{10,11... | collective-permute-start | bytes 98312 | tf_op jit(solution)/shard_map/ppermute | solution.py:102
  35.2 4.4 %collective-permute-start.5 = (bf16[16,1024]{1,0:T(8,128)(2,1)S(1)}, bf16[16,1024]{1,0:T(8,128)(2,1)S(1)}, u32[]{:S(2)}, u32[]{:S(2)}) collective-permute-start(bf16[16,1024]{1,0:T(8,128)(2,1)S(1)} %collective-permute-done.1), channel_id=1, source_target_pairs={{0,6},{1,7},{2,0},{3,1},{4,2},{5,3},{6,4},{7,5},{8,14},{9,15},{10,... | collective-permute-start | bytes 98312 | tf_op jit(solution)/shard_map/ppermute | solution.py:94
  37.5 11.5 %collective-permute-start.6 = (bf16[4,16,4096]{2,1,0:T(8,128)(2,1)S(1)}, bf16[4,16,4096]{2,1,0:T(8,128)(2,1)S(1)}, u32[]{:S(2)}, u32[]{:S(2)}) collective-permute-start(bf16[4,16,4096]{2,1,0:T(8,128)(2,1)S(1)} %collective-permute-done), channel_id=1, source_target_pairs={{0,1},{1,0},{2,3},{3,2},{4,5},{5,4},{6,7},{7,6},{8,9},{9,8},{10,11... | collective-permute-start | bytes 1572872 | tf_op jit(solution)/shard_map/ppermute | solution.py:102
  38.0 11.4 %collective-permute-start.4 = (bf16[4,16,4096]{2,1,0:T(8,128)(2,1)S(1)}, bf16[4,16,4096]{2,1,0:T(8,128)(2,1)S(1)}, u32[]{:S(2)}, u32[]{:S(2)}) collective-permute-start(bf16[4,16,4096]{2,1,0:T(8,128)(2,1)S(1)} %collective-permute-done), channel_id=1, source_target_pairs={{0,6},{1,7},{2,0},{3,1},{4,2},{5,3},{6,4},{7,5},{8,14},{9,15},{10,... | collective-permute-start | bytes 1572872 | tf_op jit(solution)/shard_map/ppermute | solution.py:94
  49.4 5.9 %collective-permute-start.11 = (bf16[16,1024]{1,0:T(8,128)(2,1)S(1)}, bf16[16,1024]{1,0:T(8,128)(2,1)S(1)}, u32[]{:S(2)}, u32[]{:S(2)}) collective-permute-start(bf16[16,1024]{1,0:T(8,128)(2,1)S(1)} %collective-permute-done.5), channel_id=1, source_target_pairs={{0,1},{1,0},{2,3},{3,2},{4,5},{5,4},{6,7},{7,6},{8,9},{9,8},{10,11... | collective-permute-start | bytes 98312 | tf_op jit(solution)/shard_map/ppermute | solution.py:102
  51.2 4.3 %collective-permute-start.9 = (bf16[16,1024]{1,0:T(8,128)(2,1)S(1)}, bf16[16,1024]{1,0:T(8,128)(2,1)S(1)}, u32[]{:S(2)}, u32[]{:S(2)}) collective-permute-start(bf16[16,1024]{1,0:T(8,128)(2,1)S(1)} %collective-permute-done.5), channel_id=1, source_target_pairs={{0,6},{1,7},{2,0},{3,1},{4,2},{5,3},{6,4},{7,5},{8,14},{9,15},{10,... | collective-permute-start | bytes 98312 | tf_op jit(solution)/shard_map/ppermute | solution.py:94
  53.0 11.6 %collective-permute-start.10 = (bf16[4,16,4096]{2,1,0:T(8,128)(2,1)S(1)}, bf16[4,16,4096]{2,1,0:T(8,128)(2,1)S(1)}, u32[]{:S(2)}, u32[]{:S(2)}) collective-permute-start(bf16[4,16,4096]{2,1,0:T(8,128)(2,1)S(1)} %collective-permute-done.4), channel_id=1, source_target_pairs={{0,1},{1,0},{2,3},{3,2},{4,5},{5,4},{6,7},{7,6},{8,9},{9,8},{10,11... | collective-permute-start | bytes 1572872 | tf_op jit(solution)/shard_map/ppermute | solution.py:102
  53.6 11.0 %collective-permute-start.8 = (bf16[4,16,4096]{2,1,0:T(8,128)(2,1)S(1)}, bf16[4,16,4096]{2,1,0:T(8,128)(2,1)S(1)}, u32[]{:S(2)}, u32[]{:S(2)}) collective-permute-start(bf16[4,16,4096]{2,1,0:T(8,128)(2,1)S(1)} %collective-permute-done.4), channel_id=1, source_target_pairs={{0,6},{1,7},{2,0},{3,1},{4,2},{5,3},{6,4},{7,5},{8,14},{9,15},{10,... | collective-permute-start | bytes 1572872 | tf_op jit(solution)/shard_map/ppermute | solution.py:94
  64.6 4.3 %collective-permute-start.12 = (bf16[16,1024]{1,0:T(8,128)(2,1)S(1)}, bf16[16,1024]{1,0:T(8,128)(2,1)S(1)}, u32[]{:S(2)}, u32[]{:S(2)}) collective-permute-start(bf16[16,1024]{1,0:T(8,128)(2,1)S(1)} %collective-permute-done.9), channel_id=1, source_target_pairs={{0,1},{1,0},{2,3},{3,2},{4,5},{5,4},{6,7},{7,6},{8,9},{9,8},{10,11... | collective-permute-start | bytes 98312 | tf_op jit(solution)/shard_map/ppermute | solution.py:102
  65.3 10.2 %collective-permute-start.19 = (bf16[4,16,4096]{2,1,0:T(8,128)(2,1)S(1)}, bf16[4,16,4096]{2,1,0:T(8,128)(2,1)S(1)}, u32[]{:S(2)}, u32[]{:S(2)}) collective-permute-start(bf16[4,16,4096]{2,1,0:T(8,128)(2,1)S(1)} %collective-permute-done.8), channel_id=1, source_target_pairs={{0,1},{1,0},{2,3},{3,2},{4,5},{5,4},{6,7},{7,6},{8,9},{9,8},{10,11... | collective-permute-start | bytes 1572872 | tf_op jit(solution)/shard_map/ppermute | solution.py:102
  68.9 1.5 collective-permute-start.13
  70.5 71.1 %collective-permute-start.14 = (bf16[2,8,16,1024]{3,2,1,0:T(8,128)(2,1)S(1)}, bf16[2,8,16,1024]{3,2,1,0:T(8,128)(2,1)S(1)}, u32[]{:S(2)}, u32[]{:S(2)}) collective-permute-start(bf16[2,8,16,1024]{3,2,1,0:T(8,128)(2,1)S(1)} %pad_maximum_fusion.2), channel_id=1, source_target_pairs={{0,16},{8,24},{16,0},{24,8},{1,17},{9,25},{17,1},{25,9},{2,18},{10... | collective-permute-start | bytes 1572872 | tf_op jit(solution)/shard_map/ppermute | solution.py:183
  107.5 17.0 %copy-start.2 = (f32[256,2560]{1,0:T(8,128)}, f32[256,2560]{1,0:T(8,128)S(1)}, u32[]{:S(2)}) copy-start(f32[256,2560]{1,0:T(8,128)S(1)} %get-tuple-element.39) | copy-start | bytes 7864324
  124.5 33.5 %collective-permute-start.26 = (f32[256,2048]{1,0:T(8,128)}, f32[256,2048]{1,0:T(8,128)}, u32[]{:S(2)}, u32[]{:S(2)}) collective-permute-start(f32[256,2048]{1,0:T(8,128)} %get-tuple-element.42), channel_id=1, source_target_pairs={{0,8},{8,0},{16,24},{24,16},{1,9},{9,1},{17,25},{25,17},{2,10},{10... | collective-permute-start | bytes 6291464 | tf_op jit(solution)/shard_map/ppermute | solution.py:180
  124.5 53.9 %collective-permute-start.24 = (f32[256,2560]{1,0:T(8,128)}, f32[256,2560]{1,0:T(8,128)}, u32[]{:S(2)}, u32[]{:S(2)}) collective-permute-start(f32[256,2560]{1,0:T(8,128)} %get-tuple-element.40), channel_id=1, source_target_pairs={{0,8},{8,0},{16,24},{24,16},{1,9},{9,1},{17,25},{25,17},{2,10},{10... | collective-permute-start | bytes 7864328 | tf_op jit(solution)/shard_map/ppermute | solution.py:180
  125.0 57.6 %collective-permute-start.20 = (f32[256,2560]{1,0:T(8,128)}, f32[256,2560]{1,0:T(8,128)}, u32[]{:S(2)}, u32[]{:S(2)}) collective-permute-start(f32[256,2560]{1,0:T(8,128)} %get-tuple-element.36), channel_id=1, source_target_pairs={{0,8},{8,0},{16,24},{24,16},{1,9},{9,1},{17,25},{25,17},{2,10},{10... | collective-permute-start | bytes 7864328 | tf_op jit(solution)/shard_map/ppermute | solution.py:180
  141.1 44.5 %collective-permute-start.22 = (f32[256,2560]{1,0:T(8,128)}, f32[256,2560]{1,0:T(8,128)}, u32[]{:S(2)}, u32[]{:S(2)}) collective-permute-start(f32[256,2560]{1,0:T(8,128)} %get-tuple-element.38), channel_id=1, source_target_pairs={{0,8},{8,0},{16,24},{24,16},{1,9},{9,1},{17,25},{25,17},{2,10},{10... | collective-permute-start | bytes 7864328 | tf_op jit(solution)/shard_map/ppermute | solution.py:180
  142.6 9.4 %copy-start.14 = (bf16[512,1024]{1,0:T(8,128)(2,1)}, bf16[512,1024]{1,0:T(8,128)(2,1)S(1)}, u32[]{:S(2)}) copy-start(bf16[512,1024]{1,0:T(8,128)(2,1)S(1)} %convolution_convert_fusion) | copy-start | bytes 3145732
  152.0 3.8 %copy-start.7 = (f32[256,9728]{1,0:T(8,128)}, f32[256,9728]{1,0:T(8,128)S(1)}, u32[]{:S(2)}) copy-start(f32[256,9728]{1,0:T(8,128)S(1)} %fusion.110) | copy-start | bytes 29884420
  157.1 5.5 %collective-permute-start.17 = (f32[2,8,16]{2,1,0:T(8,128)S(1)}, f32[2,8,16]{2,1,0:T(8,128)S(1)}, u32[]{:S(2)}, u32[]{:S(2)}) collective-permute-start(f32[2,8,16]{2,1,0:T(8,128)S(1)} %pad_maximum_fusion.4), channel_id=1, source_target_pairs={{0,2},{1,3},{2,4},{3,5},{4,6},{5,7},{6,0},{7,1},{8,10},{9,11},{10,... | collective-permute-start | bytes 3080 | tf_op jit(solution)/shard_map/ppermute | solution.py:94
  158.0 6.2 %collective-permute-start.16 = (f32[2,8,16]{2,1,0:T(8,128)S(1)}, f32[2,8,16]{2,1,0:T(8,128)S(1)}, u32[]{:S(2)}, u32[]{:S(2)}) collective-permute-start(f32[2,8,16]{2,1,0:T(8,128)S(1)} %pad_maximum_fusion.4), channel_id=1, source_target_pairs={{0,4},{1,5},{2,6},{3,7},{4,0},{5,1},{6,2},{7,3},{8,12},{9,13},{10,... | collective-permute-start | bytes 3080 | tf_op jit(solution)/shard_map/ppermute | solution.py:94
  160.2 15.6 %copy-start.4 = (f32[256,2048]{1,0:T(8,128)S(1)}, f32[256,2048]{1,0:T(8,128)}, u32[]{:S(2)}) copy-start(f32[256,2048]{1,0:T(8,128)} %copy-done.3) | copy-start | bytes 6291460
  162.0 6.1 %copy-start.12 = (f16[128,2048]{1,0:T(8,128)(2,1)}, f16[128,2048]{1,0:T(8,128)(2,1)S(1)}, u32[]{:S(2)}) copy-start(f16[128,2048]{1,0:T(8,128)(2,1)S(1)} %fusion.66) | copy-start | bytes 1572868
  162.6 13.3 %collective-permute-start.27 = (f16[128,2048]{1,0:T(8,128)(2,1)S(1)}, f16[128,2048]{1,0:T(8,128)(2,1)S(1)}, u32[]{:S(2)}, u32[]{:S(2)}) collective-permute-start(f16[128,2048]{1,0:T(8,128)(2,1)S(1)} %fusion.66), channel_id=1, source_target_pairs={{0,16},{8,24},{16,0},{24,8},{1,17},{9,25},{17,1},{25,9},{2,18},{10... | collective-permute-start | bytes 1572872 | tf_op jit(solution)/shard_map/ppermute | solution.py:183
  164.2 3.9 %collective-permute-start.15 = (f32[2,8,16]{2,1,0:T(8,128)S(1)}, f32[2,8,16]{2,1,0:T(8,128)S(1)}, u32[]{:S(2)}, u32[]{:S(2)}) collective-permute-start(f32[2,8,16]{2,1,0:T(8,128)S(1)} %pad_maximum_fusion.4), channel_id=1, source_target_pairs={{0,6},{1,7},{2,0},{3,1},{4,2},{5,3},{6,4},{7,5},{8,14},{9,15},{10,... | collective-permute-start | bytes 3080 | tf_op jit(solution)/shard_map/ppermute | solution.py:94
  168.1 66.9 %collective-permute-start.18 = (f32[2,8,16]{2,1,0:T(8,128)S(1)}, f32[2,8,16]{2,1,0:T(8,128)S(1)}, u32[]{:S(2)}, u32[]{:S(2)}) collective-permute-start(f32[2,8,16]{2,1,0:T(8,128)S(1)} %pad_maximum_fusion.5), channel_id=1, source_target_pairs={{0,1},{1,0},{2,3},{3,2},{4,5},{5,4},{6,7},{7,6},{8,9},{9,8},{10,11... | collective-permute-start | bytes 3080 | tf_op jit(solution)/shard_map/ppermute | solution.py:102
  175.8 12.1 %copy-start.9 = (f16[128,2048]{1,0:T(8,128)(2,1)}, f16[128,2048]{1,0:T(8,128)(2,1)S(1)}, u32[]{:S(2)}) copy-start(f16[128,2048]{1,0:T(8,128)(2,1)S(1)} %collective-permute-done.27) | copy-start | bytes 1572868
  181.1 18.0 %collective-permute-start.25 = (f16[128,2560]{1,0:T(8,128)(2,1)}, f16[128,2560]{1,0:T(8,128)(2,1)}, u32[]{:S(2)}, u32[]{:S(2)}) collective-permute-start(f16[128,2560]{1,0:T(8,128)(2,1)} %fusion.37), channel_id=1, source_target_pairs={{0,16},{8,24},{16,0},{24,8},{1,17},{9,25},{17,1},{25,9},{2,18},{10... | collective-permute-start | bytes 1966088 | tf_op jit(solution)/shard_map/ppermute | solution.py:183
  182.6 3.0 copy-start.1
  185.0 28.1 %collective-permute-start.21 = (f16[128,2560]{1,0:T(8,128)(2,1)}, f16[128,2560]{1,0:T(8,128)(2,1)}, u32[]{:S(2)}, u32[]{:S(2)}) collective-permute-start(f16[128,2560]{1,0:T(8,128)(2,1)} %fusion.41), channel_id=1, source_target_pairs={{0,16},{8,24},{16,0},{24,8},{1,17},{9,25},{17,1},{25,9},{2,18},{10... | collective-permute-start | bytes 1966088 | tf_op jit(solution)/shard_map/ppermute | solution.py:183
  189.4 35.2 %collective-permute-start.23 = (f16[128,2560]{1,0:T(8,128)(2,1)}, f16[128,2560]{1,0:T(8,128)(2,1)}, u32[]{:S(2)}, u32[]{:S(2)}) collective-permute-start(f16[128,2560]{1,0:T(8,128)(2,1)} %fusion.39), channel_id=1, source_target_pairs={{0,16},{8,24},{16,0},{24,8},{1,17},{9,25},{17,1},{25,9},{2,18},{10... | collective-permute-start | bytes 1966088 | tf_op jit(solution)/shard_map/ppermute | solution.py:183
  227.7 12.2 %copy-start.8 = (f16[128,2560]{1,0:T(8,128)(2,1)S(1)}, f16[128,2560]{1,0:T(8,128)(2,1)}, u32[]{:S(2)}) copy-start(f16[128,2560]{1,0:T(8,128)(2,1)} %get-tuple-element.57) | copy-start | bytes 1966084
  229.8 5.5 %collective-permute-start.30 = (f32[2,8,16]{2,1,0:T(8,128)S(1)}, f32[2,8,16]{2,1,0:T(8,128)S(1)}, u32[]{:S(2)}, u32[]{:S(2)}) collective-permute-start(f32[2,8,16]{2,1,0:T(8,128)S(1)} %pad_maximum_fusion.6), channel_id=1, source_target_pairs={{0,2},{1,3},{2,4},{3,5},{4,6},{5,7},{6,0},{7,1},{8,10},{9,11},{10,... | collective-permute-start | bytes 3080 | tf_op jit(solution)/shard_map/ppermute | solution.py:94
  232.6 4.5 %collective-permute-start.29 = (f32[2,8,16]{2,1,0:T(8,128)S(1)}, f32[2,8,16]{2,1,0:T(8,128)S(1)}, u32[]{:S(2)}, u32[]{:S(2)}) collective-permute-start(f32[2,8,16]{2,1,0:T(8,128)S(1)} %pad_maximum_fusion.6), channel_id=1, source_target_pairs={{0,4},{1,5},{2,6},{3,7},{4,0},{5,1},{6,2},{7,3},{8,12},{9,13},{10,... | collective-permute-start | bytes 3080 | tf_op jit(solution)/shard_map/ppermute | solution.py:94
  233.2 3.9 %collective-permute-start.28 = (f32[2,8,16]{2,1,0:T(8,128)S(1)}, f32[2,8,16]{2,1,0:T(8,128)S(1)}, u32[]{:S(2)}, u32[]{:S(2)}) collective-permute-start(f32[2,8,16]{2,1,0:T(8,128)S(1)} %pad_maximum_fusion.6), channel_id=1, source_target_pairs={{0,6},{1,7},{2,0},{3,1},{4,2},{5,3},{6,4},{7,5},{8,14},{9,15},{10,... | collective-permute-start | bytes 3080 | tf_op jit(solution)/shard_map/ppermute | solution.py:94
  237.2 4.8 %collective-permute-start.31 = (f32[2,8,16]{2,1,0:T(8,128)S(1)}, f32[2,8,16]{2,1,0:T(8,128)S(1)}, u32[]{:S(2)}, u32[]{:S(2)}) collective-permute-start(f32[2,8,16]{2,1,0:T(8,128)S(1)} %pad_maximum_fusion.7), channel_id=1, source_target_pairs={{0,1},{1,0},{2,3},{3,2},{4,5},{5,4},{6,7},{7,6},{8,9},{9,8},{10,11... | collective-permute-start | bytes 3080 | tf_op jit(solution)/shard_map/ppermute | solution.py:102
  237.8 52.7 %collective-permute-start.38 = (f16[128,2048]{1,0:T(8,128)(2,1)}, f16[128,2048]{1,0:T(8,128)(2,1)}, u32[]{:S(2)}, u32[]{:S(2)}) collective-permute-start(f16[128,2048]{1,0:T(8,128)(2,1)} %get-tuple-element.63), channel_id=1, source_target_pairs={{0,16},{8,24},{16,0},{24,8},{1,17},{9,25},{17,1},{25,9},{2,18},{10... | collective-permute-start | bytes 1572872 | tf_op jit(solution)/shard_map/ppermute | solution.py:183
  239.4 68.6 %collective-permute-start.41 = (f16[128,2560]{1,0:T(8,128)(2,1)S(1)}, f16[128,2560]{1,0:T(8,128)(2,1)}, u32[]{:S(2)}, u32[]{:S(2)}) collective-permute-start(f16[128,2560]{1,0:T(8,128)(2,1)S(1)} %get-tuple-element.61), channel_id=1, source_target_pairs={{0,16},{8,24},{16,0},{24,8},{1,17},{9,25},{17,1},{25,9},{2,18},{10... | collective-permute-start | bytes 1966088 | tf_op jit(solution)/shard_map/ppermute | solution.py:183
  239.9 68.1 %collective-permute-start.47 = (f16[128,2560]{1,0:T(8,128)(2,1)S(1)}, f16[128,2560]{1,0:T(8,128)(2,1)}, u32[]{:S(2)}, u32[]{:S(2)}) collective-permute-start(f16[128,2560]{1,0:T(8,128)(2,1)S(1)} %copy-done.8), channel_id=1, source_target_pairs={{0,16},{8,24},{16,0},{24,8},{1,17},{9,25},{17,1},{25,9},{2,18},{10... | collective-permute-start | bytes 1966088 | tf_op jit(solution)/shard_map/ppermute | solution.py:183
  241.4 66.6 %collective-permute-start.44 = (f16[128,2560]{1,0:T(8,128)(2,1)}, f16[128,2560]{1,0:T(8,128)(2,1)}, u32[]{:S(2)}, u32[]{:S(2)}) collective-permute-start(f16[128,2560]{1,0:T(8,128)(2,1)} %get-tuple-element.59), channel_id=1, source_target_pairs={{0,16},{8,24},{16,0},{24,8},{1,17},{9,25},{17,1},{25,9},{2,18},{10... | collective-permute-start | bytes 1966088 | tf_op jit(solution)/shard_map/ppermute | solution.py:183
  242.5 48.1 %collective-permute-start.37 = (f32[2,128]{1,0:T(2,128)S(1)}, f32[2,128]{1,0:T(2,128)S(1)}, u32[]{:S(2)}, u32[]{:S(2)}) collective-permute-start(f32[2,128]{1,0:T(2,128)S(1)} %pad_maximum_fusion.9), channel_id=1, source_target_pairs={{0,16},{8,24},{16,0},{24,8},{1,17},{9,25},{17,1},{25,9},{2,18},{10... | collective-permute-start | bytes 3080 | tf_op jit(solution)/shard_map/ppermute | solution.py:183
  244.0 46.6 %slice-start = ((s8[9961472]{0:T(1024)(128)(4,1)}), s8[4194304]{0:T(1024)(128)(4,1)S(1)}, s32[]{:S(2)}) async-start(s8[9961472]{0:T(1024)(128)(4,1)} %bitcast.270), calls=%async_computation | async-start | bytes 8388608
  244.0 46.6 %slice-start.1 = ((s8[9961472]{0:T(1024)(128)(4,1)}), s8[4194304]{0:T(1024)(128)(4,1)S(1)}, s32[]{:S(2)}) async-start(s8[9961472]{0:T(1024)(128)(4,1)} %bitcast.270), calls=%async_computation.1 | async-start | bytes 8388608
  249.0 41.6 %slice-start.2 = ((s8[9961472]{0:T(1024)(128)(4,1)}), s8[1572864]{0:T(1024)(128)(4,1)S(1)}, s32[]{:S(2)}) async-start(s8[9961472]{0:T(1024)(128)(4,1)} %bitcast.270), calls=%async_computation.2 | async-start | bytes 3145728
  253.0 37.7 %copy-start.10 = (f16[128,2048]{1,0:T(8,128)(2,1)S(1)}, f16[128,2048]{1,0:T(8,128)(2,1)}, u32[]{:S(2)}) copy-start(f16[128,2048]{1,0:T(8,128)(2,1)} %copy-done.9) | copy-start | bytes 1572868
  253.0 37.7 %copy-start.13 = (f16[128,2048]{1,0:T(8,128)(2,1)S(1)}, f16[128,2048]{1,0:T(8,128)(2,1)}, u32[]{:S(2)}) copy-start(f16[128,2048]{1,0:T(8,128)(2,1)} %copy-done.12) | copy-start | bytes 1572868
  301.3 6.7 %copy-start.11 = (f16[128,2560]{1,0:T(8,128)(2,1)S(1)}, f16[128,2560]{1,0:T(8,128)(2,1)}, u32[]{:S(2)}) copy-start(f16[128,2560]{1,0:T(8,128)(2,1)} %fusion.39) | copy-start | bytes 1966084
  301.5 6.4 %collective-permute-start.32 = (f32[4,16,1024]{2,1,0:T(8,128)S(1)}, f32[4,16,1024]{2,1,0:T(8,128)S(1)}, u32[]{:S(2)}, u32[]{:S(2)}) collective-permute-start(f32[4,16,1024]{2,1,0:T(8,128)S(1)} %slice_bitcast_fusion.8), channel_id=1, source_target_pairs={{0,1},{1,0},{2,3},{3,2},{4,5},{5,4},{6,7},{7,6},{8,9},{9,8},{10,11... | collective-permute-start | bytes 786440 | tf_op jit(solution)/shard_map/ppermute | solution.py:102
  303.0 27.7 %collective-permute-start.49 = (bf16[128,2560]{1,0:T(8,128)(2,1)S(1)}, bf16[128,2560]{1,0:T(8,128)(2,1)S(1)}, u32[]{:S(2)}, u32[]{:S(2)}) collective-permute-start(bf16[128,2560]{1,0:T(8,128)(2,1)S(1)} %get-tuple-element.64.refs_7_), channel_id=1, source_target_pairs={{0,8},{8,0},{16,24},{24,16},{1,9},{9,1},{17,25},{25,17},{2,10},{10... | collective-permute-start | bytes 1966088 | tf_op jit(solution)/shard_map/ppermute | solution.py:180
  307.9 25.5 %collective-permute-start.46 = (bf16[128,2560]{1,0:T(8,128)(2,1)S(1)}, bf16[128,2560]{1,0:T(8,128)(2,1)}, u32[]{:S(2)}, u32[]{:S(2)}) collective-permute-start(bf16[128,2560]{1,0:T(8,128)(2,1)S(1)} %get-tuple-element.66.refs_7_), channel_id=1, source_target_pairs={{0,8},{8,0},{16,24},{24,16},{1,9},{9,1},{17,25},{25,17},{2,10},{10... | collective-permute-start | bytes 1966088 | tf_op jit(solution)/shard_map/ppermute | solution.py:180
  312.1 21.4 %collective-permute-start.48 = (bf16[128,2560]{1,0:T(8,128)(2,1)}, bf16[128,2560]{1,0:T(8,128)(2,1)}, u32[]{:S(2)}, u32[]{:S(2)}) collective-permute-start(bf16[128,2560]{1,0:T(8,128)(2,1)} %get-tuple-element.69.refs_6_), channel_id=1, source_target_pairs={{0,8},{8,0},{16,24},{24,16},{1,9},{9,1},{17,25},{25,17},{2,10},{10... | collective-permute-start | bytes 1966088 | tf_op jit(solution)/shard_map/ppermute | solution.py:180
  312.7 6.7 %collective-permute-start.34 = (f32[16,1024]{1,0:T(8,128)S(1)}, f32[16,1024]{1,0:T(8,128)S(1)}, u32[]{:S(2)}, u32[]{:S(2)}) collective-permute-start(f32[16,1024]{1,0:T(8,128)S(1)} %get-tuple-element.76), channel_id=1, source_target_pairs={{0,4},{1,5},{2,6},{3,7},{4,0},{5,1},{6,2},{7,3},{8,12},{9,13},{10,... | collective-permute-start | bytes 196616 | tf_op jit(solution)/shard_map/ppermute | solution.py:99
  314.7 5.8 %collective-permute-start.35 = (f32[16,1024]{1,0:T(8,128)S(1)}, f32[16,1024]{1,0:T(8,128)S(1)}, u32[]{:S(2)}, u32[]{:S(2)}) collective-permute-start(f32[16,1024]{1,0:T(8,128)S(1)} %get-tuple-element.77), channel_id=1, source_target_pairs={{0,6},{1,7},{2,0},{3,1},{4,2},{5,3},{6,4},{7,5},{8,14},{9,15},{10,... | collective-permute-start | bytes 196616 | tf_op jit(solution)/shard_map/ppermute | solution.py:99
  319.4 6.2 %collective-permute-start.33 = (f32[16,1024]{1,0:T(8,128)S(1)}, f32[16,1024]{1,0:T(8,128)S(1)}, u32[]{:S(2)}, u32[]{:S(2)}) collective-permute-start(f32[16,1024]{1,0:T(8,128)S(1)} %get-tuple-element.78), channel_id=1, source_target_pairs={{0,2},{1,3},{2,4},{3,5},{4,6},{5,7},{6,0},{7,1},{8,10},{9,11},{10,... | collective-permute-start | bytes 196616 | tf_op jit(solution)/shard_map/ppermute | solution.py:99
  325.6 3.6 collective-permute-start.36
  326.3 18.7 %collective-permute-start.45 = (bf16[128,2560]{1,0:T(8,128)(2,1)S(1)}, bf16[128,2560]{1,0:T(8,128)(2,1)}, u32[]{:S(2)}, u32[]{:S(2)}) collective-permute-start(bf16[128,2560]{1,0:T(8,128)(2,1)S(1)} %get-tuple-element.70.refs_6_), channel_id=1, source_target_pairs={{0,8},{8,0},{16,24},{24,16},{1,9},{9,1},{17,25},{25,17},{2,10},{10... | collective-permute-start | bytes 1966088 | tf_op jit(solution)/shard_map/ppermute | solution.py:180
  329.2 21.1 %collective-permute-start.43 = (bf16[128,2560]{1,0:T(8,128)(2,1)S(1)}, bf16[128,2560]{1,0:T(8,128)(2,1)}, u32[]{:S(2)}, u32[]{:S(2)}) collective-permute-start(bf16[128,2560]{1,0:T(8,128)(2,1)S(1)} %get-tuple-element.65.refs_7_), channel_id=1, source_target_pairs={{0,8},{8,0},{16,24},{24,16},{1,9},{9,1},{17,25},{25,17},{2,10},{10... | collective-permute-start | bytes 1966088 | tf_op jit(solution)/shard_map/ppermute | solution.py:180
  331.6 18.6 %collective-permute-start.42 = (bf16[128,2560]{1,0:T(8,128)(2,1)S(1)}, bf16[128,2560]{1,0:T(8,128)(2,1)}, u32[]{:S(2)}, u32[]{:S(2)}) collective-permute-start(bf16[128,2560]{1,0:T(8,128)(2,1)S(1)} %get-tuple-element.71.refs_6_), channel_id=1, source_target_pairs={{0,8},{8,0},{16,24},{24,16},{1,9},{9,1},{17,25},{25,17},{2,10},{10... | collective-permute-start | bytes 1966088 | tf_op jit(solution)/shard_map/ppermute | solution.py:180
  333.5 22.0 %collective-permute-start.40 = (bf16[128,2048]{1,0:T(8,128)(2,1)}, bf16[128,2048]{1,0:T(8,128)(2,1)}, u32[]{:S(2)}, u32[]{:S(2)}) collective-permute-start(bf16[128,2048]{1,0:T(8,128)(2,1)} %get-tuple-element.67.refs_7_), channel_id=1, source_target_pairs={{0,8},{8,0},{16,24},{24,16},{1,9},{9,1},{17,25},{25,17},{2,10},{10... | collective-permute-start | bytes 1572872 | tf_op jit(solution)/shard_map/ppermute | solution.py:180
  333.6 21.9 %collective-permute-start.39 = (bf16[128,2048]{1,0:T(8,128)(2,1)}, bf16[128,2048]{1,0:T(8,128)(2,1)}, u32[]{:S(2)}, u32[]{:S(2)}) collective-permute-start(bf16[128,2048]{1,0:T(8,128)(2,1)} %get-tuple-element.68.refs_6_), channel_id=1, source_target_pairs={{0,8},{8,0},{16,24},{24,16},{1,9},{9,1},{17,25},{25,17},{2,10},{10... | collective-permute-start | bytes 1572872 | tf_op jit(solution)/shard_map/ppermute | solution.py:180
  (6 other events, 7.6 us)

commit v2 on v0

v2 whole, which is shorter than its diff:
```python
import functools

import jax
import jax.numpy as jnp
from jax import lax
from jax.experimental import pallas as pl
from jax.experimental.pallas import tpu as pltpu
from jax.sharding import PartitionSpec as P

EPSILON = 1e-06
LABEL_WEIGHT = 0.5
MIB = 2**20
SMALL_COST = pl.CostEstimate(flops=1, bytes_accessed=1, transcendentals=0)


def column_plan(columns, split):
    tile = next((w for w in (512, 256, 128) if columns % w == 0), columns)
    tiles = columns // tile
    large = 3 * tiles // 8
    if not split or not large:
        return tile, [(0, tiles)], [[0]]
    return tile, [(0, large), (large, large), (2 * large, tiles - 2 * large)], [[0, 1], [2]]


def run_plan(tile, chunks, run):
    chunks = [chunks[c] for c in run]
    first, count = chunks[0]
    wide = tile
    if len(chunks) > 1:
        wide = max(w for w in range(128, 1793, 128) if (tile * count) % w == 0)
    return wide, [(a * tile // wide, b * tile // wide) for a, b in chunks]


def together(tree):
    return lax.optimization_barrier(tree)


def teacher_kernel(weight, slots, *refs):
    x_refs, w_ref, sibling_ref, own_ref = refs[:slots], refs[slots], refs[slots + 1], refs[slots + 2]
    if len(refs) > slots + 3:
        x_ref = refs[-1]
        pieces, rows = x_refs[0].shape[:2]

        @pl.when(pl.program_id(0) == 0)
        def _():
            for p in range(pieces):
                for s in range(slots):
                    at = (p * slots + s) * rows
                    x_ref[at : at + rows, :] = x_refs[s][p]
    else:
        x_ref = x_refs[0]
    sums = jnp.dot(x_ref[...], w_ref[0], preferred_element_type=jnp.float32) * weight
    half = sums.shape[0] // 2
    sibling_ref[...] = sums[:half]
    own_ref[...] = sums[half:]


def teacher_chunk(slots, head, weight, tile, first, count):
    pieces, piece, depth = slots[0].shape
    rows = pieces * piece * len(slots)
    half = rows // 2
    scratch = [pltpu.VMEM((rows, depth), jnp.bfloat16)]
    if piece % 16:
        slots, scratch = [jnp.stack(slots, axis=1).reshape(rows, depth)], []
    return pl.pallas_call(
        functools.partial(teacher_kernel, weight, len(slots)),
        grid=(count,),
        in_specs=[pl.BlockSpec(a.shape, lambda i, a=a: (0,) * a.ndim) for a in slots]
        + [pl.BlockSpec((1, depth, tile), lambda i: (0, 0, i + first))],
        out_specs=[pl.BlockSpec((half, tile), lambda i: (0, i))] * 2,
        out_shape=[jax.ShapeDtypeStruct((half, tile * count), jnp.float32)] * 2,
        scratch_shapes=scratch,
        compiler_params=pltpu.CompilerParams(vmem_limit_bytes=24 * MIB),
        cost_estimate=SMALL_COST,
    )(*slots, head)


def logits_grad_kernel(spans, parts, tile, first, near, *refs):
    mean_refs = refs[: parts * len(spans)]
    h_ref, head_ref, row_ref, grad_ref = refs[len(mean_refs) : len(mean_refs) + 4]
    step = pl.program_id(0)
    if near:
        loss_ref, hidden_ref = refs[len(mean_refs) + 4 :]

        @pl.when(step == 0)
        def _():
            loss_ref[...] = jnp.zeros_like(loss_ref)
            hidden_ref[...] = jnp.zeros_like(hidden_ref)

    def span(means):
        logits = jnp.dot(h_ref[...], head_ref[...], preferred_element_type=jnp.float32)
        at = 0
        for mean_ref in means:
            size = mean_ref.shape[0]
            rows = slice(at, at + size)
            log_target = mean_ref[...] - row_ref[rows, 0:1]
            log_student = logits[rows] - row_ref[rows, 1:2]
            place = (first + step) * tile + lax.broadcasted_iota(jnp.int32, (size, tile), 1)
            is_target = row_ref[rows, 2:3].astype(jnp.int32) == place
            target_prob = jnp.exp(log_target)
            grad = (1.0 + LABEL_WEIGHT) * jnp.exp(log_student) - target_prob
            grad = jnp.where(is_target, grad - LABEL_WEIGHT, grad)
            grad_ref[rows, :] = grad.astype(jnp.bfloat16)
            if near:
                terms = target_prob * (log_target - log_student)
                terms = jnp.where(is_target, terms - LABEL_WEIGHT * log_student, terms)
                loss_ref[rows, :] += jnp.sum(terms, axis=1, keepdims=True)
            at += size

    for k, (start, count) in enumerate(spans):
        pl.when((step >= start) & (step < start + count))(
            functools.partial(span, mean_refs[k * parts : (k + 1) * parts])
        )
    if near:
        hidden_ref[...] += lax.dot_general(
            head_ref[...],
            grad_ref[...],
            (((1,), (1,)), ((), ())),
            preferred_element_type=jnp.float32,
        )


def logits_grad(means, h, head, row_values, near, tile, chunks):
    rows, features = h.shape
    first = chunks[0][0]
    spans = [(start - first, count) for start, count in chunks]
    steps = sum(count for _, count in chunks)
    whole = lambda a: pl.BlockSpec(a.shape, lambda i: (0,) * a.ndim)

    def at_span(start, count):
        return lambda i: (0, jnp.clip(i - start, 0, count - 1))

    out_specs = [pl.BlockSpec((rows, tile), lambda i: (0, i))]
    out_shape = [jax.ShapeDtypeStruct((rows, steps * tile), jnp.bfloat16)]
    if near:
        out_specs += [
            pl.BlockSpec((rows, 1), lambda i: (0, 0)),
            pl.BlockSpec((features, rows), lambda i: (0, 0)),
        ]
        out_shape += [
            jax.ShapeDtypeStruct((rows, 1), jnp.float32),
            jax.ShapeDtypeStruct((features, rows), jnp.float32),
        ]
    return pl.pallas_call(
        functools.partial(logits_grad_kernel, spans, len(means[0]), tile, first, near),
        grid=(steps,),
        in_specs=[
            pl.BlockSpec((m.shape[0], tile), at_span(*span))
            for parts, span in zip(means, spans)
            for m in parts
        ]
        + [whole(h), pl.BlockSpec((features, tile), lambda i: (0, i + first)), whole(row_values)],
        out_specs=out_specs,
        out_shape=out_shape,
        compiler_params=pltpu.CompilerParams(vmem_limit_bytes=48 * MIB),
        cost_estimate=SMALL_COST,
    )(*[m for parts in means for m in parts], h, head, row_values)


def head_grad_kernel(h_ref, a_ref, b_ref, c_ref, d_ref, *refs):
    grads = jnp.concatenate([a_ref[...], b_ref[...], c_ref[...], d_ref[...]], axis=0)
    refs[-1][...] = jnp.dot(h_ref[...], grads, preferred_element_type=jnp.float32)


def head_grad(h, near, far, so_far, columns, tile, chunks):
    features, rows = h.shape
    part = near[0].shape[0]
    first, steps = chunks[0][0], sum(count for _, count in chunks)
    part_spec = pl.BlockSpec((part, tile), lambda i: (0, i))
    in_specs = [pl.BlockSpec((features, rows), lambda i: (0, 0))]
    in_specs += [part_spec] * 4
    operands = [h, far[0], near[0], far[1], near[1]]
    alias = {}
    if so_far is not None:
        alias = {len(operands): 0}
        in_specs.append(pl.BlockSpec(memory_space=pl.ANY))
        operands.append(so_far)
    return pl.pallas_call(
        head_grad_kernel,
        grid=(steps,),
        in_specs=in_specs,
        out_specs=pl.BlockSpec((features, tile), lambda i: (0, i + first)),
        out_shape=jax.ShapeDtypeStruct((features, columns), jnp.float32),
        input_output_aliases=alias,
        compiler_params=pltpu.CompilerParams(vmem_limit_bytes=16 * MIB),
        cost_estimate=SMALL_COST,
    )(*operands)


class Vocab:
    def __init__(self):
        self.n = lax.axis_size("vocab")
        self.me = lax.axis_index("vocab")
        self.ring = self.n // 2 if self.n in (4, 8) else 0

    def from_ahead(self, a, k):
        n = self.ring
        pairs = [(v, 2 * ((v // 2 - k) % n) + v % 2) for v in range(self.n)]
        return lax.ppermute(a, "vocab", pairs)

    def to_ahead(self, a, k):
        n = self.ring
        pairs = [(v, 2 * ((v // 2 + k) % n) + v % 2) for v in range(self.n)]
        return lax.ppermute(a, "vocab", pairs)

    def across(self, a):
        return lax.ppermute(a, "vocab", [(v, v ^ 1) for v in range(self.n)])

    def slot_of(self, v):
        if not self.ring:
            return v
        return 2 * ((v // 2 - self.me // 2) % self.ring) + ((v % 2) ^ (self.me % 2))

    def holder_of(self, slot):
        if not self.ring:
            return slot
        return 2 * ((slot // 2 + self.me // 2) % self.ring) + ((slot % 2) ^ (self.me % 2))

    def turned(self, a, way):
        if not self.ring:
            return a
        pairs = a.reshape((self.ring, 2) + a.shape[1:])
        start = (way * (self.me // 2)) % self.ring
        pairs = lax.dynamic_slice_in_dim(
            jnp.concatenate([pairs, pairs]), start, self.ring
        )
        return jnp.where(self.me % 2 == 1, pairs[:, ::-1], pairs).reshape(a.shape)

    def log_sum(self, peak, total):
        def merge(parts):
            top = functools.reduce(jnp.maximum, [p[0] for p in parts])
            return jnp.stack([top, sum(p[1] * jnp.exp(p[0] - top) for p in parts)])

        if not self.ring:
            every = lax.all_gather(jnp.stack([peak, total]), "vocab")
            merged = merge([every[k] for k in range(self.n)])
        else:
            both = jnp.stack([peak, total])
            merged = merge([both] + [self.from_ahead(both, k) for k in range(1, self.ring)])

        def close(merged):
            if self.ring:
                merged = merge([merged, self.across(merged)])
            return merged[0] + jnp.log(merged[1])

        return merged, close

    def sum_scatter(self, a):
        if not self.ring:
            return [lambda a: lax.psum_scatter(a, "vocab", scatter_dimension=0)]

        def pair(a):
            pairs = a.reshape((self.ring, 2) + a.shape[1:])
            return pairs[:, 0] + self.across(pairs[:, 1])

        def along(a):
            return a[0] + sum(self.to_ahead(a[k], k) for k in range(1, self.ring))

        return [pair, along]


def on_device(teacher_hidden, teacher_gain, teacher_head, student_hidden, student_head, targets):
    f32, bf16, f16 = jnp.float32, jnp.bfloat16, jnp.float16
    teachers = lax.axis_size("teacher")
    t = lax.axis_index("teacher")
    vocab = Vocab()
    nv, v, steps = vocab.n, vocab.me, vocab.ring
    weight = 1.0 / teachers
    features, columns = student_head.shape
    block, depth = teacher_hidden.shape[1:]
    piece = block // teachers
    rows = nv * piece

    def sibling(a):
        return lax.ppermute(a, "teacher", [(k, k ^ 1) for k in range(teachers)])

    def facing(a):
        return lax.ppermute(a, "teacher", [(k, k ^ 2) for k in range(teachers)])

    owners = [t ^ k for k in (3, 1, 2, 0)]

    hidden = teacher_hidden[0].astype(f32)
    scale_rows = lax.rsqrt(jnp.mean(hidden * hidden, axis=1, keepdims=True) + EPSILON)
    normed = (hidden * scale_rows * teacher_gain[0][None, :]).astype(bf16)
    normed = normed.reshape(teachers, piece, depth)
    normed = jnp.stack(
        [lax.dynamic_index_in_dim(normed, owner, keepdims=False) for owner in owners]
    )

    digits = jnp.stack([targets % 128, (targets // 128) % 128, targets // 16384], axis=1)
    lanes = -features % 128 + 128
    digits = jnp.pad(digits.astype(bf16), ((0, 0), (0, lanes - 3)))
    student_block = jnp.concatenate([student_hidden, digits], axis=1)

    tile, chunks, runs = column_plan(columns, steps > 0)
    bounds = [(0, 3), (3, nv)] if steps else [(0, nv)]
    items = [(p, c) for p in range(len(bounds)) for c in range(len(chunks))]

    held = {"slots": [], "sums": {}, "near": {}, "far": {}, "peak": {}, "total": {}}

    def gather_step(step):
        now = held["slots"][2 * step]
        held["slots"].append(vocab.across(now))
        if step < steps - 1:
            held["slots"].append(vocab.from_ahead(now, 1))
        s = held["students"]
        if step == 0:
            s = jnp.stack([s] + [vocab.from_ahead(s, k) for k in range(1, steps)])
        elif step == 1:
            s = jnp.stack([s, vocab.across(s)], axis=1)
            s = s.reshape((nv,) + s.shape[2:])
        elif step == 2:
            s = jnp.stack([s, facing(s)])
        else:
            s = jnp.stack([s, sibling(s)], axis=1)
        held["students"] = s

    def product(p, c):
        a, b = bounds[p]
        held["sums"][p, c] = teacher_chunk(
            held["slots"][a:b], teacher_head, weight, tile, *chunks[c]
        )

    def meet(p, c):
        for_sibling, own = held["sums"][p, c]
        held["sums"][p, c] = (own, sibling(for_sibling))

    def add(p, c):
        own, other = held["sums"][p, c]
        n = own.shape[0] // 2
        held["sums"][p, c] = (
            (own[:n] + other[:n]).astype(f16),
            (own[n:] + other[n:]).astype(f16),
        )

    def cross(p, c, which):
        sums = held["sums"][p, c]
        held["far" if which else "near"][p, c] = (sums[1 - which], facing(sums[which]))

    def arrive(where, p, c):
        own, other = held[where][p, c]
        held[where][p, c] = own.astype(f32) + other.astype(f32)

    def statistics(p, c):
        arrive("near", p, c)
        a = held["near"][p, c]
        held["peak"][p, c] = jnp.max(a, axis=1)
        held["total"][p, c] = jnp.sum(jnp.exp(a - held["peak"][p, c][:, None]), axis=1)

    def by_holder(a):
        return vocab.turned(a.reshape(nv, piece), -1)

    def by_slot(a):
        return vocab.turned(a, 1).reshape(rows)

    def arrange():
        students = held["students"].reshape(teachers * rows, -1)
        token_block = (
            teachers * vocab.holder_of(jnp.arange(nv))[None, :] + jnp.stack(owners)[:, None]
        )
        place = (t ^ (token_block // nv)) * nv + vocab.slot_of(token_block % nv)
        token = piece * place.reshape(-1)[:, None] + jnp.arange(piece)[None, :]
        moved = token.reshape(-1)[:, None] == jnp.arange(teachers * rows)[None, :]
        students = jnp.dot(moved.astype(bf16), students, preferred_element_type=f32).astype(bf16)
        h_rows = students[:, :features]
        digits = students[2 * rows :, features : features + 3].astype(jnp.int32)
        share = features // teachers
        held["wanted"] = (
            digits[:, 0] + 128 * digits[:, 1] + 16384 * digits[:, 2] - v * columns
        ).astype(f32)
        held["share"] = lax.dynamic_slice_in_dim(h_rows, t * share, share, axis=1).T
        held["h"] = (h_rows[2 * rows : 3 * rows], h_rows[3 * rows :])
        logits = jnp.dot(held["h"][1], student_head, preferred_element_type=f32)
        top = jnp.max(logits, axis=1)
        total = jnp.sum(jnp.exp(logits - top[:, None]), axis=1)
        held["student"] = (by_holder(top), by_holder(total))

    if not steps:
        held["slots"] = list(lax.all_gather(normed, "vocab"))
        s = lax.all_gather(student_block, "vocab")
        s = jnp.stack([s, facing(s)])
        held["students"] = jnp.stack([s, sibling(s)], axis=1)
        for item in items:
            product(*item)
            meet(*item)
            add(*item)
            cross(*item, 0)
            cross(*item, 1)
            statistics(*item)
        arrange()
        merged, close_student = vocab.log_sum(*held["student"])
        held["student"] = close_student(merged)
    else:
        held["slots"], held["students"] = [normed], student_block
        gather_step(0)
        held = together(held)
        last = len(items) - 1
        for stage in range(last + 3):
            if stage >= 2:
                add(*items[stage - 2])
            if stage + 1 < steps:
                gather_step(stage + 1)
            if 1 <= stage <= last + 1:
                meet(*items[stage - 1])
            if stage >= 2:
                cross(*items[stage - 2], 0)
                if items[stage - 2][0] == 0:
                    cross(*items[stage - 2], 1)
                if stage == last + 1:
                    cross(*items[len(chunks)], 1)
            if stage <= last:
                product(*items[stage])
            if stage >= 3:
                statistics(*items[stage - 3])
            if stage == last + 1:
                arrange()
            if stage == last + 2:
                held["student"] = close_student(held["student"])
            held = together(held)
            if stage == last + 1:
                held["student"], close_student = vocab.log_sum(*held["student"])

    if steps:
        statistics(*items[-1])
    peak, total = [], []
    for p in range(len(bounds)):
        parts = [held["peak"][p, c] for c in range(len(chunks))]
        top = functools.reduce(jnp.maximum, parts)
        peak.append(top)
        total.append(
            sum(held["total"][p, c] * jnp.exp(a - top) for c, a in enumerate(parts))
        )
    peak, total = jnp.concatenate(peak), jnp.concatenate(total)
    merged, close_target = vocab.log_sum(by_holder(peak), by_holder(total))
    if steps:
        if len(chunks) > 1:
            cross(1, 1, 1)
        held, merged = together((held, merged))
        if len(chunks) > 2:
            cross(1, 2, 1)
    norms = jnp.stack([by_slot(close_target(merged)), by_slot(held["student"])])

    def grads(where, norms, k, run):
        means = [[held[where][p, c] for p in range(len(bounds))] for c in run]
        values = jnp.stack([*norms, held["wanted"][k * rows : (k + 1) * rows]], axis=1)
        return logits_grad(
            means, held["h"][k], student_head, values, where == "near", *run_plan(tile, chunks, run)
        )

    far_norms = facing(norms)
    near_grads, losses, terms = [], 0.0, 0.0
    for run in runs:
        grad, loss, term = grads("near", norms, 1, run)
        near_grads.append(grad)
        losses, terms = losses + loss, terms + term
    terms = jnp.concatenate([terms.T, jnp.broadcast_to(losses, (rows, lanes))], axis=1)
    for p, c in items:
        arrive("far", p, c)
    held, far_norms, near_grads, terms = together((held, far_norms, near_grads, terms))

    sums = terms.reshape(nv, piece, features + lanes)
    hops = vocab.sum_scatter(sums)
    hops += [
        lambda a: lax.ppermute(
            a,
            ("teacher", "vocab"),
            [(k, teachers * (k % nv) + k // nv) for k in range(teachers * nv)],
        )
    ]
    near_others, far_grads, far_others = [], [], []
    for k, run in enumerate(runs):
        near_others.append(sibling(near_grads[k]))
        if far_grads:
            far_others.append(sibling(far_grads[-1]))
        far_grads += grads("far", far_norms, 0, run)
        if len(hops) > 1:
            sums = hops.pop(0)(sums)
        sums, near_others, far_grads, far_others, held = together(
            (sums, near_others, far_grads, far_others, held)
        )
    far_others.append(sibling(far_grads[-1]))
    for hop in hops:
        sums = hop(sums)
    row_loss = sums[:, features]
    grad_hidden = sums[:, :features].astype(bf16)
    grad_head = None
    for k, run in enumerate(runs):
        grad_head = head_grad(
            held["share"],
            [near_others[k], near_grads[k]],
            [far_others[k], far_grads[k]],
            grad_head,
            columns,
            *run_plan(tile, chunks, run),
        )
    return (row_loss, grad_hidden, grad_head)


def solution(mesh):
    return jax.shard_map(
        on_device,
        mesh=mesh,
        in_specs=(
            P("teacher", "vocab", None),
            P("teacher", None),
            P("teacher", None, "vocab"),
            P(("teacher", "vocab"), None),
            P(None, "vocab"),
            P(("teacher", "vocab")),
        ),
        out_specs=(P(("teacher", "vocab")), P(("teacher", "vocab"), None), P("teacher", "vocab")),
        check_vma=False,
    )
```

time: 661 us -> 279 us (0.42)
  waiting for transfers between devices: 368 us -> 30.4 us
  blocking collectives: 131 us -> 0 us
  Pallas kernels: 0 us -> 120 us
  matrix products: 85.5 us -> 11.9 us
  starting transfers between devices: 0.16 us -> 48.4 us
  other arithmetic: 18.8 us -> 42.7 us
  local copies, waits for them, and re-layouts: 40.7 us -> 18.2 us
  between operations: 15.2 us -> 1.66 us
    unnamed x5 -> x0, waiting for transfers between devices: 233 us -> none
    pallas_call x0 -> x12, Pallas kernels: none -> 120 us  [the longest x6 79.8 us: teacher_chunk(): pl.pallas_call(functools.partial(teacher_kernel, weight, len(slots)), gri...]
    all_gather x5 -> x0, blocking collectives: 102 us -> none  [the longest x4 71.4 us: joined(): everything = jax.tree.map(lambda part: lax.all_gather(part, axis), shard)]
    all_gather x1 -> x0, waiting for transfers between devices: 78.3 us -> none  [on_device(): gathered = lax.all_gather(own_rows, 'vocab', axis=0, tiled=True)]
    dot_general x4 -> x2, matrix products: 85.5 us -> 11.9 us  [the longest x1 11 us: arrange(): logits = jnp.dot(held['h'][1], student_head, preferred_element_type=f32)]
    reduce_scatter x2 -> x0, waiting for transfers between devices: 56.6 us -> none  [the longest x1 56.6 us: on_device(): lax.psum_scatter(normed_logits(gathered, gain_row, head_cols, weight), 't...]
    ppermute x0 -> x49, starting transfers between devices: none -> 48.4 us  [the longest x12 20.7 us: from_ahead(): return lax.ppermute(a, 'vocab', pairs)]
    ppermute x0 -> x49, waiting for transfers between devices: none -> 30.4 us  [the longest x14 17.4 us: facing(): return lax.ppermute(a, 'teacher', [(k, k ^ 2) for k in range(teachers)])]
  transfers between devices with their start and end apart: 4 -> 49, of which waited for: 3 -> 12; matrix products, arithmetic and copies ran while one was open for 9% -> 21% of each run, Pallas kernels for 0% -> 42%
where the time goes in v2:
time: 279 us; the launch traced here: 274 us
  Pallas kernels  120 us (43%)
  starting transfers between devices  48.4 us (17%)
  other arithmetic  42.7 us (15%)
  waiting for transfers between devices  30.4 us (11%)
  local copies, waits for them, and re-layouts  18.2 us (7%)
  matrix products  11.9 us (4%)
    pallas_call x6, Pallas kernels, teacher_chunk(): pl.pallas_call(functools.partial(teacher_kernel, weight, len(slots)), gri...  79.8 us
    pallas_call x4, Pallas kernels, logits_grad(): pl.pallas_call(functools.partial(logits_grad_kernel, spans, len(means[0])...  28.9 us
    ppermute x12, starting transfers between devices, from_ahead(): return lax.ppermute(a, 'vocab', pairs)  20.7 us
    ppermute x14, waiting for transfers between devices, facing(): return lax.ppermute(a, 'teacher', [(k, k ^ 2) for k in range(teachers)])  17.4 us
    ppermute x14, starting transfers between devices, facing(): return lax.ppermute(a, 'teacher', [(k, k ^ 2) for k in range(teachers)])  13.7 us
    ppermute x12, waiting for transfers between devices, from_ahead(): return lax.ppermute(a, 'vocab', pairs)  11.7 us
    pallas_call x2, Pallas kernels, head_grad(): pl.pallas_call(head_grad_kernel, grid=(steps,), in_specs=in_specs, out_sp...  11.5 us
    unnamed x105, local copies, waits for them, and re-layouts  11.4 us
  transfers between devices with their start and end apart: 49, of which 12 were waited for; matrix products, arithmetic and copies ran while one was open for 21% of the time, Pallas kernels for 42%

profile of v2, /device:TPU:0, one launch (start us, length us, event | category | flops | bytes accessed | tf_op | source)
XLA Modules:
  0.0 273.5 jit_solution(8688683278088751593)
XLA Ops:
  0.6 1.2 multiply_reduce_fusion
  2.0 1.3 multiply_convert_fusion
  3.4 5.1 %collective-permute-start.1 = (bf16[4,16,4096]{2,1,0:T(8,128)(2,1)S(1)}, bf16[4,16,4096]{2,1,0:T(8,128)(2,1)S(1)}, u32[]{:S(2)}, u32[]{:S(2)}) collective-permute-start(bf16[4,16,4096]{2,1,0:T(8,128)(2,1)S(1)} %pad_maximum_fusion.1.refs_0_), channel_id=1, source_target_pairs={{0,6},{1,7},{2,0},{3,1},{4,2},{5,3},{6,4},{7,5},{8,14},{9,15},{10,... | collective-permute-start | bytes 1572872 | tf_op jit(solution)/shard_map/ppermute | solution.py:199
  8.5 1.5 collective-permute-start
  11.0 1.3 collective-permute-start.4
  12.3 8.8 %collective-permute-done.3 = bf16[16,1024]{1,0:T(8,128)(2,1)S(1)} collective-permute-done((bf16[16,1024]{1,0:T(8,128)(2,1)S(1)}, bf16[16,1024]{1,0:T(8,128)(2,1)S(1)}, u32[]{:S(2)}, u32[]{:S(2)}) %collective-permute-start.3) | collective-permute-done | bytes 32800 | tf_op jit(solution)/shard_map/ppermute | solution.py:199
  21.5 1.2 collective-permute-done.4
  22.8 3.6 %collective-permute-start.6 = (bf16[4,16,4096]{2,1,0:T(8,128)(2,1)S(1)}, bf16[4,16,4096]{2,1,0:T(8,128)(2,1)S(1)}, u32[]{:S(2)}, u32[]{:S(2)}) collective-permute-start(bf16[4,16,4096]{2,1,0:T(8,128)(2,1)S(1)} %collective-permute-done.1.refs_2_), channel_id=1, source_target_pairs={{0,6},{1,7},{2,0},{3,1},{4,2},{5,3},{6,4},{7,5},{8,14},{9,15},{10,... | collective-permute-start | bytes 1572872 | tf_op jit(solution)/shard_map/ppermute | solution.py:199
  26.3 1.4 collective-permute-start.5
  28.4 13.2 %shard_map.85 = (f32[96,3584]{1,0:T(8,128)S(1)}, f32[96,3584]{1,0:T(8,128)S(1)}) custom-call(bf16[4,16,4096]{2,1,0:T(8,128)(2,1)S(1)} %pad_maximum_fusion.1.refs_0_, bf16[4,16,4096]{2,1,0:T(8,128)(2,1)S(1)} %collective-permute-done.refs_1_, bf16[4,16,4096]{2,1,0:T(8,128)(2,1)S(1)} %collective-permute-done.1.refs_2_, bf16[1,4096,9728]{2,1,0:T(8,128)(2,1)} %refs_5_.7), custom_call_target="tpu_custom_call" | custom-call | flops 1 | bytes 1 | tf_op jit(solution)/shard_map/pallas_call | solution.py:65
  41.6 1.1 collective-permute-done.7
  42.8 1.3 collective-permute-start.9
  45.1 1.5 collective-permute-start.10
  47.6 13.2 %shard_map.86 = (f32[96,3584]{1,0:T(8,128)S(1)}, f32[96,3584]{1,0:T(8,128)S(1)}) custom-call(bf16[4,16,4096]{2,1,0:T(8,128)(2,1)S(1)} %pad_maximum_fusion.1.refs_0_, bf16[4,16,4096]{2,1,0:T(8,128)(2,1)S(1)} %copy-done.3, bf16[4,16,4096]{2,1,0:T(8,128)(2,1)S(1)} %collective-permute-done.1.refs_2_, bf16[1,4096,9728]{2,1,0:T(8,128)(2,1)} %refs_5_.7), custom_call_target="tpu_custom_call" | custom-call | flops 1 | bytes 1 | tf_op jit(solution)/shard_map/pallas_call | solution.py:65
  61.0 1.1 collective-permute-start.14
  63.0 1.5 collective-permute-start.13
  64.5 9.9 %shard_map.87 = (f32[96,2560]{1,0:T(8,128)S(1)}, f32[96,2560]{1,0:T(8,128)S(1)}) custom-call(bf16[4,16,4096]{2,1,0:T(8,128)(2,1)S(1)} %pad_maximum_fusion.1.refs_0_, bf16[4,16,4096]{2,1,0:T(8,128)(2,1)S(1)} %copy-done.4, bf16[4,16,4096]{2,1,0:T(8,128)(2,1)S(1)} %copy-done.1, bf16[1,4096,9728]{2,1,0:T(8,128)(2,1)} %refs_5_.7), custom_call_target="tpu_custom_call" | custom-call | flops 1 | bytes 1 | tf_op jit(solution)/shard_map/pallas_call | solution.py:65
  74.4 1.1 pad_maximum_fusion
  75.5 4.7 %collective-permute-done.13 = f16[48,3584]{1,0:T(8,128)(2,1)S(1)} collective-permute-done((f16[48,3584]{1,0:T(8,128)(2,1)S(1)}, f16[48,3584]{1,0:T(8,128)(2,1)S(1)}, u32[]{:S(2)}, u32[]{:S(2)}) %collective-permute-start.13) | collective-permute-done | bytes 344096 | tf_op jit(solution)/shard_map/ppermute | solution.py:278
  81.0 1.5 collective-permute-start.18
  82.5 15.3 %shard_map.88 = (f32[160,3584]{1,0:T(8,128)S(1)}, f32[160,3584]{1,0:T(8,128)S(1)}) custom-call(bf16[4,16,4096]{2,1,0:T(8,128)(2,1)S(1)} %collective-permute-done.5.refs_0_, bf16[4,16,4096]{2,1,0:T(8,128)(2,1)S(1)} %collective-permute-done.6.refs_1_, bf16[4,16,4096]{2,1,0:T(8,128)(2,1)S(1)} %collective-permute-done.8.refs_2_, ...), custom_call_target="tpu_custom_call" | custom-call | flops 1 | bytes 1 | tf_op jit(solution)/shard_map/pallas_call | solution.py:65
  98.0 2.0 exponential_reduce_fusion.5
  100.8 1.5 collective-permute-start.21
  102.3 16.1 %shard_map.89 = (f32[160,3584]{1,0:T(8,128)}, f32[160,3584]{1,0:T(8,128)S(1)}) custom-call(bf16[4,16,4096]{2,1,0:T(8,128)(2,1)S(1)} %collective-permute-done.5.refs_0_, bf16[4,16,4096]{2,1,0:T(8,128)(2,1)S(1)} %collective-permute-done.6.refs_1_, bf16[4,16,4096]{2,1,0:T(8,128)(2,1)S(1)} %collective-permute-done.8.refs_2_, ...), custom_call_target="tpu_custom_call" | custom-call | flops 1 | bytes 1 | tf_op jit(solution)/shard_map/pallas_call | solution.py:65
  118.4 1.4 copy-done.13
  119.9 1.7 exponential_reduce_fusion.4
  122.7 3.6 %add_convert_fusion.2 = (f16[80,3584]{1,0:T(8,128)(2,1)}, f16[80,3584]{1,0:T(8,128)(2,1)}) fusion(f32[160,3584]{1,0:T(8,128)} %collective-permute-done.22, f32[160,3584]{1,0:T(8,128)} %copy-done.15), kind=kLoop, calls=%fused_computation.10 | loop fusion | flops 1146880 | bytes 5734400 | tf_op jit(solution)/shard_map/convert_element_type | solution.py:332
  127.0 12.2 %shard_map.90 = (f32[160,2560]{1,0:T(8,128)}, f32[160,2560]{1,0:T(8,128)S(1)}) custom-call(bf16[4,16,4096]{2,1,0:T(8,128)(2,1)S(1)} %collective-permute-done.5.refs_0_, bf16[4,16,4096]{2,1,0:T(8,128)(2,1)S(1)} %collective-permute-done.6.refs_1_, bf16[4,16,4096]{2,1,0:T(8,128)(2,1)S(1)} %collective-permute-done.8.refs_2_, ...), custom_call_target="tpu_custom_call" | custom-call | flops 1 | bytes 1 | tf_op jit(solution)/shard_map/pallas_call | solution.py:65
  140.3 1.6 collective-permute-done.23
  144.3 2.9 %add_convert_fusion = (f16[80,3584]{1,0:T(8,128)(2,1)}, f16[80,3584]{1,0:T(8,128)(2,1)}) fusion(f32[160,3584]{1,0:T(8,128)} %collective-permute-done.24, f32[160,3584]{1,0:T(8,128)S(1)} %copy-done.14), kind=kLoop, calls=%fused_computation.7 | loop fusion | flops 1146880 | bytes 5734400 | tf_op jit(solution)/shard_map/convert_element_type | solution.py:332
  147.2 1.5 collective-permute-start.26
  148.7 11.0 %fusion.58 = (f32[128]{0:T(128)S(1)}, f32[128,9728]{1,0:T(8,128)}) fusion(bf16[896,9728]{1,0:T(8,128)(2,1)} %refs_3_.9, bf16[512,1024]{0,1:T(8,128)(2,1)S(1)} %convolution_convert_fusion), kind=kOutput, calls=%fused_computation.212 | convolution fusion | flops 2232614912 | bytes 22643200 | tf_op jit(solution)/shard_map/dot_general | solution.py:373
  159.8 3.2 %exponential_reduce_fusion = f32[128]{0:T(128)S(1)} fusion(f32[128,9728]{1,0:T(8,128)} %get-tuple-element.538, f32[128]{0:T(128)S(1)} %get-tuple-element.537), kind=kLoop, calls=%fused_computation | loop fusion | flops 2490240 | bytes 4981760 | tf_op jit(solution)/shard_map/reduce_sum | solution.py:375
  163.3 1.5 fusion.53
  166.2 1.7 exponential_reduce_fusion.2
  167.9 1.3 collective-permute-done.26
  170.2 2.9 %collective-permute-start.29 = (f32[2,8,16]{2,1,0:T(8,128)S(1)}, f32[2,8,16]{2,1,0:T(8,128)S(1)}, u32[]{:S(2)}, u32[]{:S(2)}) collective-permute-start(f32[2,8,16]{2,1,0:T(8,128)S(1)} %pad_maximum_fusion.6), channel_id=1, source_target_pairs={{0,6},{1,7},{2,0},{3,1},{4,2},{5,3},{6,4},{7,5},{8,14},{9,15},{10,... | collective-permute-start | bytes 3080 | tf_op jit(solution)/shard_map/ppermute | solution.py:199
  173.1 1.6 add_convert_fusion.4
  175.3 1.4 fusion.54
  176.7 1.1 collective-permute-start.32
  177.8 2.5 exponential_reduce_fusion.1
  180.5 4.4 %collective-permute-done.28 = f16[80,2560]{1,0:T(8,128)(2,1)S(1)} collective-permute-done((f16[80,2560]{1,0:T(8,128)(2,1)S(1)}, f16[80,2560]{1,0:T(8,128)(2,1)S(1)}, u32[]{:S(2)}, u32[]{:S(2)}) %collective-permute-start.28) | collective-permute-done | bytes 409632 | tf_op jit(solution)/shard_map/ppermute | solution.py:278
  185.1 1.2 exponential_reduce_fusion.3
  188.1 1.3 collective-permute-start.35
  189.3 2.8 %collective-permute-start.34 = (f32[2,8,16]{2,1,0:T(8,128)S(1)}, f32[2,8,16]{2,1,0:T(8,128)S(1)}, u32[]{:S(2)}, u32[]{:S(2)}) collective-permute-start(f32[2,8,16]{2,1,0:T(8,128)S(1)} %pad_maximum_fusion.8), channel_id=1, source_target_pairs={{0,6},{1,7},{2,0},{3,1},{4,2},{5,3},{6,4},{7,5},{8,14},{9,15},{10,... | collective-permute-start | bytes 3080 | tf_op jit(solution)/shard_map/ppermute | solution.py:199
  194.2 5.4 %collective-permute-done.33 = f16[80,3584]{1,0:T(8,128)(2,1)S(1)} collective-permute-done((f16[80,3584]{1,0:T(8,128)(2,1)S(1)}, f16[80,3584]{1,0:T(8,128)(2,1)S(1)}, u32[]{:S(2)}, u32[]{:S(2)}) %collective-permute-start.33) | collective-permute-done | bytes 573472 | tf_op jit(solution)/shard_map/ppermute | solution.py:278
  202.1 1.9 convert_add_fusion.7.refs_0_
  205.8 1.4 convert_add_fusion.1.refs_1_
  207.3 2.3 convert_add_fusion.refs_3_
  210.2 1.6 collective-permute-start.39
  211.9 1.1 copy-done.8
  214.1 7.0 %shard_map.92 = (bf16[128,2560]{1,0:T(8,128)(2,1)}, f32[128,1]{1,0:T(8,128)S(1)}, f32[896,128]{1,0:T(8,128)S(1)}) custom-call(f32[48,2560]{1,0:T(8,128)S(1)} %copy-done.16, f32[80,2560]{1,0:T(8,128)S(1)} %copy-done.8, bf16[128,896]{1,0:T(8,128)(2,1)S(1)} %copy.50.refs_4_.refs_2_, bf16[896,9728]{1,0:T(8,128)(2,1)} %refs_3_.9, f32[128,3]{1,0:T(8,128)S(1)} %copy.51.refs_6_.refs_4_), custom_call_target="tpu_custom_call" | custom-call | flops 1 | bytes 1 | tf_op jit(solution)/shard_map/pallas_call | solution.py:144
  221.1 10.2 %shard_map.91 = (bf16[128,7168]{1,0:T(8,128)(2,1)}, f32[128,1]{1,0:T(8,128)S(1)}, f32[896,128]{1,0:T(8,128)S(1)}) custom-call(f32[48,3584]{1,0:T(8,128)S(1)} %copy-done.11, f32[80,3584]{1,0:T(8,128)S(1)} %get-tuple-element.444.refs_1_, f32[48,3584]{1,0:T(8,128)S(1)} %copy-done.12, f32[80,3584]{1,0:T(8,128)S(1)} %copy-done.6, ...), custom_call_target="tpu_custom_call" | custom-call | flops 1 | bytes 1 | tf_op jit(solution)/shard_map/pallas_call | solution.py:144
  232.4 2.0 convert_add_fusion.4.refs_1_
  236.7 1.3 copy-done.5
  237.9 1.1 copy-done.9
  239.0 1.1 copy-done.10
  240.1 6.8 %shard_map.93.c_ref = bf16[128,7168]{1,0:T(8,128)(2,1)S(1)} custom-call(f32[48,3584]{1,0:T(8,128)S(1)} %copy-done.9, f32[80,3584]{1,0:T(8,128)S(1)} %convert_add_fusion.1.refs_1_, f32[48,3584]{1,0:T(8,128)S(1)} %copy-done.10, f32[80,3584]{1,0:T(8,128)S(1)} %copy-done.5, bf16[128,896]{1,0:T(8,128)(2,1)S(1)} %copy.56.refs_4_, bf16[896,9728]{1,0:T(8,128)(2,1)} %refs_3_.9, ...), custom_call_target="tpu_custom_call" | custom-call | flops 1 | bytes 1 | tf_op jit(solution)/shard_map/pallas_call | solution.py:144
  247.0 1.1 fusion.1
  249.3 1.5 collective-permute-start.43
  250.8 1.4 collective-permute-start.44
  254.2 4.8 %shard_map.94.c_ref = bf16[128,2560]{1,0:T(8,128)(2,1)S(1)} custom-call(f32[48,2560]{1,0:T(8,128)S(1)} %copy-done.17, f32[80,2560]{1,0:T(8,128)S(1)} %copy-done.7, bf16[128,896]{1,0:T(8,128)(2,1)S(1)} %copy.58.refs_2_, bf16[896,9728]{1,0:T(8,128)(2,1)} %refs_3_.9, f32[128,3]{1,0:T(8,128)S(1)} %copy.59.refs_4_), custom_call_target="tpu_custom_call" | custom-call | flops 1 | bytes 1 | tf_op jit(solution)/shard_map/pallas_call | solution.py:144
  260.7 6.6 %shard_map.95.refs_0_ = f32[224,9728]{1,0:T(8,128)} custom-call(bf16[224,512]{1,0:T(8,128)(2,1)S(1)} %dynamic-slice_bitcast_fusion.h_ref, bf16[128,7168]{1,0:T(8,128)(2,1)} %collective-permute-done.46.a_ref, bf16[128,7168]{1,0:T(8,128)(2,1)} %collective-permute-done.41.b_ref, bf16[128,7168]{1,0:T(8,128)(2,1)S(1)} %shard_map.93.c_ref, ...), custom_call_target="tpu_custom_call" | custom-call | flops 1 | bytes 1 | tf_op jit(solution)/shard_map/pallas_call | solution.py:178
  268.6 4.9 %shard_map.96 = f32[224,9728]{1,0:T(8,128)} custom-call(bf16[224,512]{1,0:T(8,128)(2,1)S(1)} %dynamic-slice_bitcast_fusion.h_ref, bf16[128,2560]{1,0:T(8,128)(2,1)S(1)} %collective-permute-done.48.a_ref, bf16[128,2560]{1,0:T(8,128)(2,1)} %collective-permute-done.45.b_ref, bf16[128,2560]{1,0:T(8,128)(2,1)S(1)} %shard_map.94.c_ref, ...), custom_call_target="tpu_custom_call", output_to_operand_aliasing={{}: (5, {})} | custom-call | flops 1 | bytes 1 | tf_op jit(solution)/shard_map/pallas_call | solution.py:178
  (268 shorter events, 35.3 us)
Async XLA Ops:
  2.0 8.0 %copy-start.51 = (s32[16]{0:T(128)S(1)}, s32[16]{0:T(128)}, u32[]{:S(2)}) copy-start(s32[16]{0:T(128)} %param.11) | copy-start | bytes 196
  2.0 8.2 %copy-start.43 = (bf16[16,896]{1,0:T(8,128)(2,1)S(1)}, bf16[16,896]{1,0:T(8,128)(2,1)}, u32[]{:S(2)}) copy-start(bf16[16,896]{1,0:T(8,128)(2,1)} %param.9) | copy-start | bytes 86020
  3.4 19.3 %collective-permute-start.1 = (bf16[4,16,4096]{2,1,0:T(8,128)(2,1)S(1)}, bf16[4,16,4096]{2,1,0:T(8,128)(2,1)S(1)}, u32[]{:S(2)}, u32[]{:S(2)}) collective-permute-start(bf16[4,16,4096]{2,1,0:T(8,128)(2,1)S(1)} %pad_maximum_fusion.1.refs_0_), channel_id=1, source_target_pairs={{0,6},{1,7},{2,0},{3,1},{4,2},{5,3},{6,4},{7,5},{8,14},{9,15},{10,... | collective-permute-start | bytes 1572872 | tf_op jit(solution)/shard_map/ppermute | solution.py:199
  8.5 14.2 %collective-permute-start = (bf16[4,16,4096]{2,1,0:T(8,128)(2,1)S(1)}, bf16[4,16,4096]{2,1,0:T(8,128)(2,1)S(1)}, u32[]{:S(2)}, u32[]{:S(2)}) collective-permute-start(bf16[4,16,4096]{2,1,0:T(8,128)(2,1)S(1)} %pad_maximum_fusion.1.refs_0_), channel_id=1, source_target_pairs={{0,1},{1,0},{2,3},{3,2},{4,5},{5,4},{6,7},{7,6},{8,9},{9,8},{10,11... | collective-permute-start | bytes 1572872 | tf_op jit(solution)/shard_map/ppermute | solution.py:207
  10.2 11.0 %collective-permute-start.3 = (bf16[16,1024]{1,0:T(8,128)(2,1)S(1)}, bf16[16,1024]{1,0:T(8,128)(2,1)S(1)}, u32[]{:S(2)}, u32[]{:S(2)}) collective-permute-start(bf16[16,1024]{1,0:T(8,128)(2,1)S(1)} %get-tuple-element.523), channel_id=1, source_target_pairs={{0,4},{1,5},{2,6},{3,7},{4,0},{5,1},{6,2},{7,3},{8,12},{9,13},{10,... | collective-permute-start | bytes 98312 | tf_op jit(solution)/shard_map/ppermute | solution.py:199
  10.3 11.3 %collective-permute-start.2 = (bf16[16,1024]{1,0:T(8,128)(2,1)S(1)}, bf16[16,1024]{1,0:T(8,128)(2,1)S(1)}, u32[]{:S(2)}, u32[]{:S(2)}) collective-permute-start(bf16[16,1024]{1,0:T(8,128)(2,1)S(1)} %get-tuple-element.523), channel_id=1, source_target_pairs={{0,6},{1,7},{2,0},{3,1},{4,2},{5,3},{6,4},{7,5},{8,14},{9,15},{10,... | collective-permute-start | bytes 98312 | tf_op jit(solution)/shard_map/ppermute | solution.py:199
  11.0 11.7 %collective-permute-start.4 = (bf16[16,1024]{1,0:T(8,128)(2,1)S(1)}, bf16[16,1024]{1,0:T(8,128)(2,1)S(1)}, u32[]{:S(2)}, u32[]{:S(2)}) collective-permute-start(bf16[16,1024]{1,0:T(8,128)(2,1)S(1)} %get-tuple-element.523), channel_id=1, source_target_pairs={{0,2},{1,3},{2,4},{3,5},{4,6},{5,7},{6,0},{7,1},{8,10},{9,11},{10,... | collective-permute-start | bytes 98312 | tf_op jit(solution)/shard_map/ppermute | solution.py:199
  22.7 23.8 %copy-start = (bf16[4,16,4096]{2,1,0:T(8,128)(2,1)}, bf16[4,16,4096]{2,1,0:T(8,128)(2,1)S(1)}, u32[]{:S(2)}) copy-start(bf16[4,16,4096]{2,1,0:T(8,128)(2,1)S(1)} %collective-permute-done.1.refs_2_) | copy-start | bytes 1572868
  22.8 18.8 %copy-start.2 = (bf16[4,16,4096]{2,1,0:T(8,128)(2,1)}, bf16[4,16,4096]{2,1,0:T(8,128)(2,1)S(1)}, u32[]{:S(2)}) copy-start(bf16[4,16,4096]{2,1,0:T(8,128)(2,1)S(1)} %collective-permute-done.refs_1_) | copy-start | bytes 1572868
  22.8 19.9 %collective-permute-start.6 = (bf16[4,16,4096]{2,1,0:T(8,128)(2,1)S(1)}, bf16[4,16,4096]{2,1,0:T(8,128)(2,1)S(1)}, u32[]{:S(2)}, u32[]{:S(2)}) collective-permute-start(bf16[4,16,4096]{2,1,0:T(8,128)(2,1)S(1)} %collective-permute-done.1.refs_2_), channel_id=1, source_target_pairs={{0,6},{1,7},{2,0},{3,1},{4,2},{5,3},{6,4},{7,5},{8,14},{9,15},{10,... | collective-permute-start | bytes 1572872 | tf_op jit(solution)/shard_map/ppermute | solution.py:199
  26.3 16.3 %collective-permute-start.5 = (bf16[4,16,4096]{2,1,0:T(8,128)(2,1)S(1)}, bf16[4,16,4096]{2,1,0:T(8,128)(2,1)S(1)}, u32[]{:S(2)}, u32[]{:S(2)}) collective-permute-start(bf16[4,16,4096]{2,1,0:T(8,128)(2,1)S(1)} %collective-permute-done.1.refs_2_), channel_id=1, source_target_pairs={{0,1},{1,0},{2,3},{3,2},{4,5},{5,4},{6,7},{7,6},{8,9},{9,8},{10,11... | collective-permute-start | bytes 1572872 | tf_op jit(solution)/shard_map/ppermute | solution.py:207
  27.8 14.8 %collective-permute-start.7 = (bf16[4,16,1024]{2,1,0:T(8,128)(2,1)S(1)}, bf16[4,16,1024]{2,1,0:T(8,128)(2,1)S(1)}, u32[]{:S(2)}, u32[]{:S(2)}) collective-permute-start(bf16[4,16,1024]{2,1,0:T(8,128)(2,1)S(1)} %pad_maximum_fusion.5), channel_id=1, source_target_pairs={{0,1},{1,0},{2,3},{3,2},{4,5},{5,4},{6,7},{7,6},{8,9},{9,8},{10,11... | collective-permute-start | bytes 393224 | tf_op jit(solution)/shard_map/ppermute | solution.py:207
  42.7 18.2 %collective-permute-start.11 = (f32[96,3584]{1,0:T(8,128)S(1)}, f32[96,3584]{1,0:T(8,128)S(1)}, u32[]{:S(2)}, u32[]{:S(2)}) collective-permute-start(f32[96,3584]{1,0:T(8,128)S(1)} %get-tuple-element.257), channel_id=1, source_target_pairs={{0,8},{8,0},{16,24},{24,16},{1,9},{9,1},{17,25},{25,17},{2,10},{10... | collective-permute-start | bytes 4128776 | tf_op jit(solution)/shard_map/ppermute | solution.py:275
  42.8 18.1 %collective-permute-start.9 = (bf16[4,16,4096]{2,1,0:T(8,128)(2,1)S(1)}, bf16[4,16,4096]{2,1,0:T(8,128)(2,1)S(1)}, u32[]{:S(2)}, u32[]{:S(2)}) collective-permute-start(bf16[4,16,4096]{2,1,0:T(8,128)(2,1)S(1)} %collective-permute-done.6.refs_1_), channel_id=1, source_target_pairs={{0,6},{1,7},{2,0},{3,1},{4,2},{5,3},{6,4},{7,5},{8,14},{9,15},{10,... | collective-permute-start | bytes 1572872 | tf_op jit(solution)/shard_map/ppermute | solution.py:199
  44.1 16.8 %collective-permute-start.8 = (bf16[4,16,4096]{2,1,0:T(8,128)(2,1)S(1)}, bf16[4,16,4096]{2,1,0:T(8,128)(2,1)S(1)}, u32[]{:S(2)}, u32[]{:S(2)}) collective-permute-start(bf16[4,16,4096]{2,1,0:T(8,128)(2,1)S(1)} %collective-permute-done.6.refs_1_), channel_id=1, source_target_pairs={{0,1},{1,0},{2,3},{3,2},{4,5},{5,4},{6,7},{7,6},{8,9},{9,8},{10,11... | collective-permute-start | bytes 1572872 | tf_op jit(solution)/shard_map/ppermute | solution.py:207
  45.1 15.7 %collective-permute-start.10 = (bf16[8,16,1024]{2,1,0:T(8,128)(2,1)S(1)}, bf16[8,16,1024]{2,1,0:T(8,128)(2,1)S(1)}, u32[]{:S(2)}, u32[]{:S(2)}) collective-permute-start(bf16[8,16,1024]{2,1,0:T(8,128)(2,1)S(1)} %bitcast.154), channel_id=1, source_target_pairs={{0,16},{8,24},{16,0},{24,8},{1,17},{9,25},{17,1},{25,9},{2,18},{10... | collective-permute-start | bytes 786440 | tf_op jit(solution)/shard_map/ppermute | solution.py:278
  60.9 19.2 %collective-permute-start.16 = (f32[96,3584]{1,0:T(8,128)S(1)}, f32[96,3584]{1,0:T(8,128)S(1)}, u32[]{:S(2)}, u32[]{:S(2)}) collective-permute-start(f32[96,3584]{1,0:T(8,128)S(1)} %get-tuple-element.271), channel_id=1, source_target_pairs={{0,8},{8,0},{16,24},{24,16},{1,9},{9,1},{17,25},{25,17},{2,10},{10... | collective-permute-start | bytes 4128776 | tf_op jit(solution)/shard_map/ppermute | solution.py:275
  61.0 19.1 %collective-permute-start.14 = (bf16[4,16,4096]{2,1,0:T(8,128)(2,1)S(1)}, bf16[4,16,4096]{2,1,0:T(8,128)(2,1)S(1)}, u32[]{:S(2)}, u32[]{:S(2)}) collective-permute-start(bf16[4,16,4096]{2,1,0:T(8,128)(2,1)S(1)} %collective-permute-done.9.refs_3_), channel_id=1, source_target_pairs={{0,1},{1,0},{2,3},{3,2},{4,5},{5,4},{6,7},{7,6},{8,9},{9,8},{10,11... | collective-permute-start | bytes 1572872 | tf_op jit(solution)/shard_map/ppermute | solution.py:207
  62.1 12.3 %collective-permute-start.15 = (bf16[2,8,16,1024]{3,2,1,0:T(8,128)(2,1)S(1)}, bf16[2,8,16,1024]{3,2,1,0:T(8,128)(2,1)S(1)}, u32[]{:S(2)}, u32[]{:S(2)}) collective-permute-start(bf16[2,8,16,1024]{3,2,1,0:T(8,128)(2,1)S(1)} %pad_maximum_fusion.2), channel_id=1, source_target_pairs={{0,8},{8,0},{16,24},{24,16},{1,9},{9,1},{17,25},{25,17},{2,10},{10... | collective-permute-start | bytes 1572872 | tf_op jit(solution)/shard_map/ppermute | solution.py:275
  62.4 13.0 %collective-permute-start.12 = (f16[48,3584]{1,0:T(8,128)(2,1)S(1)}, f16[48,3584]{1,0:T(8,128)(2,1)S(1)}, u32[]{:S(2)}, u32[]{:S(2)}) collective-permute-start(f16[48,3584]{1,0:T(8,128)(2,1)S(1)} %get-tuple-element.278), channel_id=1, source_target_pairs={{0,16},{8,24},{16,0},{24,8},{1,17},{9,25},{17,1},{25,9},{2,18},{10... | collective-permute-start | bytes 1032200 | tf_op jit(solution)/shard_map/ppermute | solution.py:278
  63.0 17.2 %collective-permute-start.13 = (f16[48,3584]{1,0:T(8,128)(2,1)S(1)}, f16[48,3584]{1,0:T(8,128)(2,1)S(1)}, u32[]{:S(2)}, u32[]{:S(2)}) collective-permute-start(f16[48,3584]{1,0:T(8,128)(2,1)S(1)} %get-tuple-element.427), channel_id=1, source_target_pairs={{0,16},{8,24},{16,0},{24,8},{1,17},{9,25},{17,1},{25,9},{2,18},{10... | collective-permute-start | bytes 1032200 | tf_op jit(solution)/shard_map/ppermute | solution.py:278
  80.2 19.8 %collective-permute-start.19 = (f32[96,2560]{1,0:T(8,128)S(1)}, f32[96,2560]{1,0:T(8,128)S(1)}, u32[]{:S(2)}, u32[]{:S(2)}) collective-permute-start(f32[96,2560]{1,0:T(8,128)S(1)} %get-tuple-element.287), channel_id=1, source_target_pairs={{0,8},{8,0},{16,24},{24,16},{1,9},{9,1},{17,25},{25,17},{2,10},{10... | collective-permute-start | bytes 2949128 | tf_op jit(solution)/shard_map/ppermute | solution.py:275
  80.4 17.4 %copy-start.30 = (f16[48,3584]{1,0:T(8,128)(2,1)}, f16[48,3584]{1,0:T(8,128)(2,1)S(1)}, u32[]{:S(2)}) copy-start(f16[48,3584]{1,0:T(8,128)(2,1)S(1)} %get-tuple-element.429) | copy-start | bytes 1032196
  80.4 19.6 %collective-permute-start.17 = (f16[48,3584]{1,0:T(8,128)(2,1)S(1)}, f16[48,3584]{1,0:T(8,128)(2,1)S(1)}, u32[]{:S(2)}, u32[]{:S(2)}) collective-permute-start(f16[48,3584]{1,0:T(8,128)(2,1)S(1)} %get-tuple-element.297), channel_id=1, source_target_pairs={{0,16},{8,24},{16,0},{24,8},{1,17},{9,25},{17,1},{25,9},{2,18},{10... | collective-permute-start | bytes 1032200 | tf_op jit(solution)/shard_map/ppermute | solution.py:278
  81.0 19.0 %collective-permute-start.18 = (f16[48,3584]{1,0:T(8,128)(2,1)S(1)}, f16[48,3584]{1,0:T(8,128)(2,1)S(1)}, u32[]{:S(2)}, u32[]{:S(2)}) collective-permute-start(f16[48,3584]{1,0:T(8,128)(2,1)S(1)} %get-tuple-element.429), channel_id=1, source_target_pairs={{0,16},{8,24},{16,0},{24,8},{1,17},{9,25},{17,1},{25,9},{2,18},{10... | collective-permute-start | bytes 1032200 | tf_op jit(solution)/shard_map/ppermute | solution.py:278
  100.0 18.4 %copy-start.39 = (f16[48,3584]{1,0:T(8,128)(2,1)}, f16[48,3584]{1,0:T(8,128)(2,1)S(1)}, u32[]{:S(2)}) copy-start(f16[48,3584]{1,0:T(8,128)(2,1)S(1)} %collective-permute-done.17) | copy-start | bytes 1032196
  100.0 21.7 %collective-permute-start.22 = (f32[160,3584]{1,0:T(8,128)S(1)}, f32[160,3584]{1,0:T(8,128)}, u32[]{:S(2)}, u32[]{:S(2)}) collective-permute-start(f32[160,3584]{1,0:T(8,128)S(1)} %get-tuple-element.307), channel_id=1, source_target_pairs={{0,8},{8,0},{16,24},{24,16},{1,9},{9,1},{17,25},{25,17},{2,10},{10... | collective-permute-start | bytes 6881288 | tf_op jit(solution)/shard_map/ppermute | solution.py:275
  100.2 18.2 %copy-start.33 = (f16[48,2560]{1,0:T(8,128)(2,1)}, f16[48,2560]{1,0:T(8,128)(2,1)S(1)}, u32[]{:S(2)}) copy-start(f16[48,2560]{1,0:T(8,128)(2,1)S(1)} %get-tuple-element.431) | copy-start | bytes 737284
  100.2 21.4 %collective-permute-start.20 = (f16[48,2560]{1,0:T(8,128)(2,1)S(1)}, f16[48,2560]{1,0:T(8,128)(2,1)S(1)}, u32[]{:S(2)}, u32[]{:S(2)}) collective-permute-start(f16[48,2560]{1,0:T(8,128)(2,1)S(1)} %get-tuple-element.319), channel_id=1, source_target_pairs={{0,16},{8,24},{16,0},{24,8},{1,17},{9,25},{17,1},{25,9},{2,18},{10... | collective-permute-start | bytes 737288 | tf_op jit(solution)/shard_map/ppermute | solution.py:278
  100.8 20.9 %collective-permute-start.21 = (f16[48,2560]{1,0:T(8,128)(2,1)S(1)}, f16[48,2560]{1,0:T(8,128)(2,1)S(1)}, u32[]{:S(2)}, u32[]{:S(2)}) collective-permute-start(f16[48,2560]{1,0:T(8,128)(2,1)S(1)} %get-tuple-element.431), channel_id=1, source_target_pairs={{0,16},{8,24},{16,0},{24,8},{1,17},{9,25},{17,1},{25,9},{2,18},{10... | collective-permute-start | bytes 737288 | tf_op jit(solution)/shard_map/ppermute | solution.py:278
  122.4 19.6 %collective-permute-start.24 = (f32[160,3584]{1,0:T(8,128)}, f32[160,3584]{1,0:T(8,128)}, u32[]{:S(2)}, u32[]{:S(2)}) collective-permute-start(f32[160,3584]{1,0:T(8,128)} %get-tuple-element.332), channel_id=1, source_target_pairs={{0,8},{8,0},{16,24},{24,16},{1,9},{9,1},{17,25},{25,17},{2,10},{10... | collective-permute-start | bytes 6881288 | tf_op jit(solution)/shard_map/ppermute | solution.py:275
  126.3 15.7 %collective-permute-start.23 = (f16[80,3584]{1,0:T(8,128)(2,1)}, f16[80,3584]{1,0:T(8,128)(2,1)}, u32[]{:S(2)}, u32[]{:S(2)}) collective-permute-start(f16[80,3584]{1,0:T(8,128)(2,1)} %get-tuple-element.433), channel_id=1, source_target_pairs={{0,16},{8,24},{16,0},{24,8},{1,17},{9,25},{17,1},{25,9},{2,18},{10... | collective-permute-start | bytes 1720328 | tf_op jit(solution)/shard_map/ppermute | solution.py:278
  142.0 25.9 %collective-permute-start.25 = (f16[80,3584]{1,0:T(8,128)(2,1)}, f16[80,3584]{1,0:T(8,128)(2,1)}, u32[]{:S(2)}, u32[]{:S(2)}) collective-permute-start(f16[80,3584]{1,0:T(8,128)(2,1)} %get-tuple-element.349), channel_id=1, source_target_pairs={{0,16},{8,24},{16,0},{24,8},{1,17},{9,25},{17,1},{25,9},{2,18},{10... | collective-permute-start | bytes 1720328 | tf_op jit(solution)/shard_map/ppermute | solution.py:278
  147.2 22.0 %collective-permute-start.26 = (f16[80,3584]{1,0:T(8,128)(2,1)}, f16[80,3584]{1,0:T(8,128)(2,1)}, u32[]{:S(2)}, u32[]{:S(2)}) collective-permute-start(f16[80,3584]{1,0:T(8,128)(2,1)} %get-tuple-element.435), channel_id=1, source_target_pairs={{0,16},{8,24},{16,0},{24,8},{1,17},{9,25},{17,1},{25,9},{2,18},{10... | collective-permute-start | bytes 1720328 | tf_op jit(solution)/shard_map/ppermute | solution.py:278
  148.7 20.5 %collective-permute-start.27 = (f32[160,2560]{1,0:T(8,128)}, f32[160,2560]{1,0:T(8,128)}, u32[]{:S(2)}, u32[]{:S(2)}) collective-permute-start(f32[160,2560]{1,0:T(8,128)} %get-tuple-element.357), channel_id=1, source_target_pairs={{0,8},{8,0},{16,24},{24,16},{1,9},{9,1},{17,25},{25,17},{2,10},{10... | collective-permute-start | bytes 4915208 | tf_op jit(solution)/shard_map/ppermute | solution.py:275
  166.2 6.9 %copy-start.19 = (f32[160,2560]{1,0:T(8,128)S(1)}, f32[160,2560]{1,0:T(8,128)}, u32[]{:S(2)}) copy-start(f32[160,2560]{1,0:T(8,128)} %copy-done.18) | copy-start | bytes 4915204
  169.2 7.5 %collective-permute-start.31 = (f32[2,8,16]{2,1,0:T(8,128)S(1)}, f32[2,8,16]{2,1,0:T(8,128)S(1)}, u32[]{:S(2)}, u32[]{:S(2)}) collective-permute-start(f32[2,8,16]{2,1,0:T(8,128)S(1)} %pad_maximum_fusion.6), channel_id=1, source_target_pairs={{0,2},{1,3},{2,4},{3,5},{4,6},{5,7},{6,0},{7,1},{8,10},{9,11},{10,... | collective-permute-start | bytes 3080 | tf_op jit(solution)/shard_map/ppermute | solution.py:199
  170.0 6.7 %collective-permute-start.30 = (f32[2,8,16]{2,1,0:T(8,128)S(1)}, f32[2,8,16]{2,1,0:T(8,128)S(1)}, u32[]{:S(2)}, u32[]{:S(2)}) collective-permute-start(f32[2,8,16]{2,1,0:T(8,128)S(1)} %pad_maximum_fusion.6), channel_id=1, source_target_pairs={{0,4},{1,5},{2,6},{3,7},{4,0},{5,1},{6,2},{7,3},{8,12},{9,13},{10,... | collective-permute-start | bytes 3080 | tf_op jit(solution)/shard_map/ppermute | solution.py:199
  170.2 6.5 %collective-permute-start.29 = (f32[2,8,16]{2,1,0:T(8,128)S(1)}, f32[2,8,16]{2,1,0:T(8,128)S(1)}, u32[]{:S(2)}, u32[]{:S(2)}) collective-permute-start(f32[2,8,16]{2,1,0:T(8,128)S(1)} %pad_maximum_fusion.6), channel_id=1, source_target_pairs={{0,6},{1,7},{2,0},{3,1},{4,2},{5,3},{6,4},{7,5},{8,14},{9,15},{10,... | collective-permute-start | bytes 3080 | tf_op jit(solution)/shard_map/ppermute | solution.py:199
  174.7 10.4 %copy-start.23 = (f16[80,2560]{1,0:T(8,128)(2,1)}, f16[80,2560]{1,0:T(8,128)(2,1)S(1)}, u32[]{:S(2)}) copy-start(f16[80,2560]{1,0:T(8,128)(2,1)S(1)} %get-tuple-element.438) | copy-start | bytes 1228804
  174.7 10.1 %collective-permute-start.28 = (f16[80,2560]{1,0:T(8,128)(2,1)S(1)}, f16[80,2560]{1,0:T(8,128)(2,1)S(1)}, u32[]{:S(2)}, u32[]{:S(2)}) collective-permute-start(f16[80,2560]{1,0:T(8,128)(2,1)S(1)} %get-tuple-element.437), channel_id=1, source_target_pairs={{0,16},{8,24},{16,0},{24,8},{1,17},{9,25},{17,1},{25,9},{2,18},{10... | collective-permute-start | bytes 1228808 | tf_op jit(solution)/shard_map/ppermute | solution.py:278
  176.7 3.7 %collective-permute-start.32 = (f32[2,8,16]{2,1,0:T(8,128)S(1)}, f32[2,8,16]{2,1,0:T(8,128)S(1)}, u32[]{:S(2)}, u32[]{:S(2)}) collective-permute-start(f32[2,8,16]{2,1,0:T(8,128)S(1)} %pad_maximum_fusion.7), channel_id=1, source_target_pairs={{0,1},{1,0},{2,3},{3,2},{4,5},{5,4},{6,7},{7,6},{8,9},{9,8},{10,11... | collective-permute-start | bytes 3080 | tf_op jit(solution)/shard_map/ppermute | solution.py:207
  185.1 19.0 %copy-start.34 = (f16[48,2560]{1,0:T(8,128)(2,1)S(1)}, f16[48,2560]{1,0:T(8,128)(2,1)}, u32[]{:S(2)}) copy-start(f16[48,2560]{1,0:T(8,128)(2,1)} %copy-done.33) | copy-start | bytes 737284
  186.3 18.6 %copy-start.31 = (f16[48,3584]{1,0:T(8,128)(2,1)S(1)}, f16[48,3584]{1,0:T(8,128)(2,1)}, u32[]{:S(2)}) copy-start(f16[48,3584]{1,0:T(8,128)(2,1)} %copy-done.30) | copy-start | bytes 1032196
  186.9 12.7 %collective-permute-start.33 = (f16[80,3584]{1,0:T(8,128)(2,1)S(1)}, f16[80,3584]{1,0:T(8,128)(2,1)S(1)}, u32[]{:S(2)}, u32[]{:S(2)}) collective-permute-start(f16[80,3584]{1,0:T(8,128)(2,1)S(1)} %copy-done.21), channel_id=1, source_target_pairs={{0,16},{8,24},{16,0},{24,8},{1,17},{9,25},{17,1},{25,9},{2,18},{10... | collective-permute-start | bytes 1720328 | tf_op jit(solution)/shard_map/ppermute | solution.py:278
  187.5 5.5 %collective-permute-start.36 = (f32[2,8,16]{2,1,0:T(8,128)S(1)}, f32[2,8,16]{2,1,0:T(8,128)S(1)}, u32[]{:S(2)}, u32[]{:S(2)}) collective-permute-start(f32[2,8,16]{2,1,0:T(8,128)S(1)} %pad_maximum_fusion.8), channel_id=1, source_target_pairs={{0,2},{1,3},{2,4},{3,5},{4,6},{5,7},{6,0},{7,1},{8,10},{9,11},{10,... | collective-permute-start | bytes 3080 | tf_op jit(solution)/shard_map/ppermute | solution.py:199
  188.1 4.9 %collective-permute-start.35 = (f32[2,8,16]{2,1,0:T(8,128)S(1)}, f32[2,8,16]{2,1,0:T(8,128)S(1)}, u32[]{:S(2)}, u32[]{:S(2)}) collective-permute-start(f32[2,8,16]{2,1,0:T(8,128)S(1)} %pad_maximum_fusion.8), channel_id=1, source_target_pairs={{0,4},{1,5},{2,6},{3,7},{4,0},{5,1},{6,2},{7,3},{8,12},{9,13},{10,... | collective-permute-start | bytes 3080 | tf_op jit(solution)/shard_map/ppermute | solution.py:199
  189.3 4.2 %collective-permute-start.34 = (f32[2,8,16]{2,1,0:T(8,128)S(1)}, f32[2,8,16]{2,1,0:T(8,128)S(1)}, u32[]{:S(2)}, u32[]{:S(2)}) collective-permute-start(f32[2,8,16]{2,1,0:T(8,128)S(1)} %pad_maximum_fusion.8), channel_id=1, source_target_pairs={{0,6},{1,7},{2,0},{3,1},{4,2},{5,3},{6,4},{7,5},{8,14},{9,15},{10,... | collective-permute-start | bytes 3080 | tf_op jit(solution)/shard_map/ppermute | solution.py:199
  200.4 9.5 %collective-permute-start.38 = (f32[2,8,16]{2,1,0:T(8,128)}, f32[2,8,16]{2,1,0:T(8,128)S(1)}, u32[]{:S(2)}, u32[]{:S(2)}) collective-permute-start(f32[2,8,16]{2,1,0:T(8,128)} %pad_maximum_fusion.9), channel_id=1, source_target_pairs={{0,1},{1,0},{2,3},{3,2},{4,5},{5,4},{6,7},{7,6},{8,9},{9,8},{10,11... | collective-permute-start | bytes 3080 | tf_op jit(solution)/shard_map/ppermute | solution.py:207
  201.5 30.1 %collective-permute-start.37 = (f16[80,2560]{1,0:T(8,128)(2,1)}, f16[80,2560]{1,0:T(8,128)(2,1)}, u32[]{:S(2)}, u32[]{:S(2)}) collective-permute-start(f16[80,2560]{1,0:T(8,128)(2,1)} %copy-done.23), channel_id=1, source_target_pairs={{0,16},{8,24},{16,0},{24,8},{1,17},{9,25},{17,1},{25,9},{2,18},{10... | collective-permute-start | bytes 1228808 | tf_op jit(solution)/shard_map/ppermute | solution.py:278
  210.2 24.1 %collective-permute-start.39 = (f32[2,128]{1,0:T(2,128)S(1)}, f32[2,128]{1,0:T(2,128)S(1)}, u32[]{:S(2)}, u32[]{:S(2)}) collective-permute-start(f32[2,128]{1,0:T(2,128)S(1)} %pad_maximum_fusion.15), channel_id=1, source_target_pairs={{0,16},{8,24},{16,0},{24,8},{1,17},{9,25},{17,1},{25,9},{2,18},{10... | collective-permute-start | bytes 3080 | tf_op jit(solution)/shard_map/ppermute | solution.py:278
  214.1 7.0 %copy-start.6 = (f32[80,3584]{1,0:T(8,128)S(1)}, f32[80,3584]{1,0:T(8,128)}, u32[]{:S(2)}) copy-start(f32[80,3584]{1,0:T(8,128)} %get-tuple-element.445.refs_3_) | copy-start | bytes 3440644
  214.1 7.0 %copy-start.11 = (f32[48,3584]{1,0:T(8,128)S(1)}, f32[48,3584]{1,0:T(8,128)}, u32[]{:S(2)}) copy-start(f32[48,3584]{1,0:T(8,128)} %get-tuple-element.441.refs_0_) | copy-start | bytes 2064388
  214.1 7.0 %copy-start.12 = (f32[48,3584]{1,0:T(8,128)S(1)}, f32[48,3584]{1,0:T(8,128)}, u32[]{:S(2)}) copy-start(f32[48,3584]{1,0:T(8,128)} %get-tuple-element.442.refs_2_) | copy-start | bytes 2064388
  234.3 13.7 %collective-permute-start.41 = (bf16[128,7168]{1,0:T(8,128)(2,1)}, bf16[128,7168]{1,0:T(8,128)(2,1)}, u32[]{:S(2)}, u32[]{:S(2)}) collective-permute-start(bf16[128,7168]{1,0:T(8,128)(2,1)} %get-tuple-element.458.d_ref), channel_id=1, source_target_pairs={{0,8},{8,0},{16,24},{24,16},{1,9},{9,1},{17,25},{25,17},{2,10},{10... | collective-permute-start | bytes 5505032 | tf_op jit(solution)/shard_map/ppermute | solution.py:275
  235.4 11.6 %collective-permute-start.40 = (f32[4,16,1024]{2,1,0:T(8,128)}, f32[4,16,1024]{2,1,0:T(8,128)}, u32[]{:S(2)}, u32[]{:S(2)}) collective-permute-start(f32[4,16,1024]{2,1,0:T(8,128)} %slice_bitcast_fusion), channel_id=1, source_target_pairs={{0,1},{1,0},{2,3},{3,2},{4,5},{5,4},{6,7},{7,6},{8,9},{9,8},{10,11... | collective-permute-start | bytes 786440 | tf_op jit(solution)/shard_map/ppermute | solution.py:207
  240.1 6.9 %copy-start.25 = (f32[128,1024]{1,0:T(8,128)S(1)}, f32[128,1024]{1,0:T(8,128)}, u32[]{:S(2)}) copy-start(f32[128,1024]{1,0:T(8,128)} %copy-done.24) | copy-start | bytes 1572868
  248.1 11.9 %collective-permute-start.46 = (bf16[128,7168]{1,0:T(8,128)(2,1)S(1)}, bf16[128,7168]{1,0:T(8,128)(2,1)}, u32[]{:S(2)}, u32[]{:S(2)}) collective-permute-start(bf16[128,7168]{1,0:T(8,128)(2,1)S(1)} %shard_map.93.c_ref), channel_id=1, source_target_pairs={{0,8},{8,0},{16,24},{24,16},{1,9},{9,1},{17,25},{25,17},{2,10},{10... | collective-permute-start | bytes 5505032 | tf_op jit(solution)/shard_map/ppermute | solution.py:275
  248.4 11.6 %collective-permute-start.45 = (bf16[128,2560]{1,0:T(8,128)(2,1)}, bf16[128,2560]{1,0:T(8,128)(2,1)}, u32[]{:S(2)}, u32[]{:S(2)}) collective-permute-start(bf16[128,2560]{1,0:T(8,128)(2,1)} %get-tuple-element.471.d_ref), channel_id=1, source_target_pairs={{0,8},{8,0},{16,24},{24,16},{1,9},{9,1},{17,25},{25,17},{2,10},{10... | collective-permute-start | bytes 1966088 | tf_op jit(solution)/shard_map/ppermute | solution.py:275
  249.3 9.7 %collective-permute-start.43 = (f32[16,1024]{1,0:T(8,128)}, f32[16,1024]{1,0:T(8,128)S(1)}, u32[]{:S(2)}, u32[]{:S(2)}) collective-permute-start(f32[16,1024]{1,0:T(8,128)} %get-tuple-element.519), channel_id=1, source_target_pairs={{0,4},{1,5},{2,6},{3,7},{4,0},{5,1},{6,2},{7,3},{8,12},{9,13},{10,... | collective-permute-start | bytes 196616 | tf_op jit(solution)/shard_map/ppermute | solution.py:204
  250.8 8.2 %collective-permute-start.44 = (f32[16,1024]{1,0:T(8,128)}, f32[16,1024]{1,0:T(8,128)}, u32[]{:S(2)}, u32[]{:S(2)}) collective-permute-start(f32[16,1024]{1,0:T(8,128)} %get-tuple-element.520), channel_id=1, source_target_pairs={{0,6},{1,7},{2,0},{3,1},{4,2},{5,3},{6,4},{7,5},{8,14},{9,15},{10,... | collective-permute-start | bytes 196616 | tf_op jit(solution)/shard_map/ppermute | solution.py:204
  252.3 6.8 %collective-permute-start.42 = (f32[16,1024]{1,0:T(8,128)}, f32[16,1024]{1,0:T(8,128)}, u32[]{:S(2)}, u32[]{:S(2)}) collective-permute-start(f32[16,1024]{1,0:T(8,128)} %get-tuple-element.521), channel_id=1, source_target_pairs={{0,2},{1,3},{2,4},{3,5},{4,6},{5,7},{6,0},{7,1},{8,10},{9,11},{10,... | collective-permute-start | bytes 196616 | tf_op jit(solution)/shard_map/ppermute | solution.py:204
  260.0 8.6 %collective-permute-start.48 = (bf16[128,2560]{1,0:T(8,128)(2,1)S(1)}, bf16[128,2560]{1,0:T(8,128)(2,1)S(1)}, u32[]{:S(2)}, u32[]{:S(2)}) collective-permute-start(bf16[128,2560]{1,0:T(8,128)(2,1)S(1)} %shard_map.94.c_ref), channel_id=1, source_target_pairs={{0,8},{8,0},{16,24},{24,16},{1,9},{9,1},{17,25},{25,17},{2,10},{10... | collective-permute-start | bytes 1966088 | tf_op jit(solution)/shard_map/ppermute | solution.py:275
  260.1 7.3 %collective-permute-start.47 = (f32[16,1024]{1,0:T(8,128)S(1)}, f32[16,1024]{1,0:T(8,128)S(1)}, u32[]{:S(2)}, u32[]{:S(2)}) collective-permute-start(f32[16,1024]{1,0:T(8,128)S(1)} %bitcast_add_fusion), channel_id=1, source_target_pairs={{0,0},{1,4},{2,8},{3,12},{4,16},{5,20},{6,24},{7,28},{8,1},{9,5},{... | collective-permute-start | bytes 196616 | tf_op jit(solution)/shard_map/ppermute | solution.py:464
  (37 other events, 124.0 us)

commit v3 on v2

--- a/solution.py
+++ b/solution.py
@@ -56,7 +56,8 @@
 
 
 def teacher_chunk(slots, head, weight, tile, first, count):
-    pieces, piece, depth = slots[0].shape
+    pieces, piece = slots[0].shape[:2]
+    depth = head.shape[1]
     rows = pieces * piece * len(slots)
     half = rows // 2
     scratch = [pltpu.VMEM((rows, depth), jnp.bfloat16)]
@@ -65,7 +66,9 @@
     return pl.pallas_call(
         functools.partial(teacher_kernel, weight, len(slots)),
         grid=(count,),
-        in_specs=[pl.BlockSpec(a.shape, lambda i, a=a: (0,) * a.ndim) for a in slots]
+        in_specs=[
+            pl.BlockSpec(a.shape[:-1] + (depth,), lambda i, a=a: (0,) * a.ndim) for a in slots
+        ]
         + [pl.BlockSpec((1, depth, tile), lambda i: (0, 0, i + first))],
         out_specs=[pl.BlockSpec((half, tile), lambda i: (0, i))] * 2,
         out_shape=[jax.ShapeDtypeStruct((half, tile * count), jnp.float32)] * 2,
@@ -152,7 +155,7 @@
         + [whole(h), pl.BlockSpec((features, tile), lambda i: (0, i + first)), whole(row_values)],
         out_specs=out_specs,
         out_shape=out_shape,
-        compiler_params=pltpu.CompilerParams(vmem_limit_bytes=48 * MIB),
+        compiler_params=pltpu.CompilerParams(vmem_limit_bytes=40 * MIB),
         cost_estimate=SMALL_COST,
     )(*[m for parts in means for m in parts], h, head, row_values)
 
@@ -288,7 +291,7 @@
     )
 
     digits = jnp.stack([targets % 128, (targets // 128) % 128, targets // 16384], axis=1)
-    lanes = -features % 128 + 128
+    lanes = -(features + 128) % (128 * teachers) + 128
     digits = jnp.pad(digits.astype(bf16), ((0, 0), (0, lanes - 3)))
     student_block = jnp.concatenate([student_hidden, digits], axis=1)
 
@@ -303,17 +306,17 @@
         held["slots"].append(vocab.across(now))
         if step < steps - 1:
             held["slots"].append(vocab.from_ahead(now, 1))
-        s = held["students"]
-        if step == 0:
-            s = jnp.stack([s] + [vocab.from_ahead(s, k) for k in range(1, steps)])
-        elif step == 1:
-            s = jnp.stack([s, vocab.across(s)], axis=1)
-            s = s.reshape((nv,) + s.shape[2:])
-        elif step == 2:
-            s = jnp.stack([s, facing(s)])
-        else:
-            s = jnp.stack([s, sibling(s)], axis=1)
-        held["students"] = s
+
+    def spread_students(stage):
+        if stage == steps - 1:
+            s = jnp.stack([a[..., depth:] for a in held["slots"]])
+            s = jnp.swapaxes(s, 1, 2).reshape(nv, piece, -1)
+            held["students"] = (s, facing(s))
+        elif stage == steps:
+            s = jnp.stack(held["students"])
+            held["students"] = (s, sibling(s))
+        elif stage == steps + 1:
+            held["students"] = jnp.stack(held["students"], axis=1)
 
     def product(p, c):
         a, b = bounds[p]
@@ -328,17 +331,28 @@
     def add(p, c):
         own, other = held["sums"][p, c]
         n = own.shape[0] // 2
-        held["sums"][p, c] = (
-            (own[:n] + other[:n]).astype(f16),
-            (own[n:] + other[n:]).astype(f16),
-        )
+        if p == 0:
+            held["sums"][p, c] = (own + other).astype(f16)
+        else:
+            held["sums"][p, c] = (
+                (own[:n] + other[:n]).astype(f16),
+                (own[n:] + other[n:]).astype(f16),
+            )
 
     def cross(p, c, which):
         sums = held["sums"][p, c]
         held["far" if which else "near"][p, c] = (sums[1 - which], facing(sums[which]))
 
+    def cross_both(p, c):
+        sums = held["sums"][p, c]
+        held["near"][p, c] = held["far"][p, c] = (sums, facing(sums))
+
     def arrive(where, p, c):
         own, other = held[where][p, c]
+        if p == 0:
+            n = own.shape[0] // 2
+            low, high = slice(0, n), slice(n, 2 * n)
+            own, other = (own[high], other[low]) if where == "near" else (own[low], other[high])
         held[where][p, c] = own.astype(f32) + other.astype(f32)
 
     def statistics(p, c):
@@ -384,14 +398,12 @@
             product(*item)
             meet(*item)
             add(*item)
-            cross(*item, 0)
-            cross(*item, 1)
+            cross_both(*item)
             statistics(*item)
         arrange()
-        merged, close_student = vocab.log_sum(*held["student"])
-        held["student"] = close_student(merged)
     else:
-        held["slots"], held["students"] = [normed], student_block
+        beside = jnp.swapaxes(student_block.reshape(piece, teachers, -1), 0, 1)
+        held["slots"] = [jnp.concatenate([normed, beside], axis=-1)]
         gather_step(0)
         held = together(held)
         last = len(items) - 1
@@ -402,10 +414,12 @@
                 gather_step(stage + 1)
             if 1 <= stage <= last + 1:
                 meet(*items[stage - 1])
+            spread_students(stage)
             if stage >= 2:
-                cross(*items[stage - 2], 0)
                 if items[stage - 2][0] == 0:
-                    cross(*items[stage - 2], 1)
+                    cross_both(*items[stage - 2])
+                else:
+                    cross(*items[stage - 2], 0)
                 if stage == last + 1:
                     cross(*items[len(chunks)], 1)
             if stage <= last:
@@ -414,12 +428,9 @@
                 statistics(*items[stage - 3])
             if stage == last + 1:
                 arrange()
-            if stage == last + 2:
-                held["student"] = close_student(held["student"])
             held = together(held)
-            if stage == last + 1:
-                held["student"], close_student = vocab.log_sum(*held["student"])
-
+
+    ready = []
     if steps:
         statistics(*items[-1])
     peak, total = [], []
@@ -431,14 +442,18 @@
             sum(held["total"][p, c] * jnp.exp(a - top) for c, a in enumerate(parts))
         )
     peak, total = jnp.concatenate(peak), jnp.concatenate(total)
-    merged, close_target = vocab.log_sum(by_holder(peak), by_holder(total))
+    both = [jnp.stack(pair) for pair in zip((by_holder(peak), by_holder(total)), held["student"])]
+    merged, close = vocab.log_sum(*both)
     if steps:
         if len(chunks) > 1:
             cross(1, 1, 1)
+        ready = [(p, c) for p, c in items if p == 0 or c == 0]
+        for p, c in ready:
+            arrive("far", p, c)
         held, merged = together((held, merged))
         if len(chunks) > 2:
             cross(1, 2, 1)
-    norms = jnp.stack([by_slot(close_target(merged)), by_slot(held["student"])])
+    norms = jnp.stack([by_slot(a) for a in close(merged)])
 
     def grads(where, norms, k, run):
         means = [[held[where][p, c] for p in range(len(bounds))] for c in run]
@@ -455,7 +470,8 @@
         losses, terms = losses + loss, terms + term
     terms = jnp.concatenate([terms.T, jnp.broadcast_to(losses, (rows, lanes))], axis=1)
     for p, c in items:
-        arrive("far", p, c)
+        if (p, c) not in ready:
+            arrive("far", p, c)
     held, far_norms, near_grads, terms = together((held, far_norms, near_grads, terms))
 
     sums = terms.reshape(nv, piece, features + lanes)

time: 279 us -> 278 us (level)
  starting transfers between devices: 48.4 us -> 38.9 us
  local copies, waits for them, and re-layouts: 18.2 us -> 22.2 us
    ppermute x12 -> x6, starting transfers between devices: 20.7 us -> 11.6 us  [from_ahead(): return lax.ppermute(a, 'vocab', pairs)]
    unnamed x105 -> x108, local copies, waits for them, and re-layouts: 11.4 us -> 16.3 us
    ppermute x8 -> x6, waiting for transfers between devices: 1.2 us -> 5.63 us  [across(): return lax.ppermute(a, 'vocab', [(v, v ^ 1) for v in range(self.n)])]
    ppermute x12 -> x6, waiting for transfers between devices: 11.7 us -> 10.4 us  [from_ahead(): return lax.ppermute(a, 'vocab', pairs)]
    ppermute x14 -> x11, waiting for transfers between devices: 17.4 us -> 16.7 us  [facing(): return lax.ppermute(a, 'teacher', [(k, k ^ 2) for k in range(teachers)])]
    ppermute x14 -> x11, starting transfers between devices: 13.7 us -> 13 us  [facing(): return lax.ppermute(a, 'teacher', [(k, k ^ 2) for k in range(teachers)])]
    ppermute x8 -> x6, starting transfers between devices: 8.73 us -> 8.14 us  [across(): return lax.ppermute(a, 'vocab', [(v, v ^ 1) for v in range(self.n)])]
    add x6 -> x5, other arithmetic: 9.36 us -> 8.79 us  [arrive(): held[where][p, c] = own.astype(f32) + other.astype(f32)]
  transfers between devices with their start and end apart: 49 -> 38, of which waited for: 12 -> 8; matrix products, arithmetic and copies ran while one was open for 21% -> 19% of each run, Pallas kernels for 42% -> 43%
where the time goes in v3:
time: 278 us; the launch traced here: 273 us
  Pallas kernels  121 us (44%)
  other arithmetic  44.2 us (16%)
  starting transfers between devices  38.9 us (14%)
  waiting for transfers between devices  32.7 us (12%)
  local copies, waits for them, and re-layouts  22.2 us (8%)
  matrix products  12 us (4%)
    pallas_call x6, Pallas kernels, teacher_chunk(): pl.pallas_call(functools.partial(teacher_kernel, weight, len(slots)), gri...  80.8 us
    pallas_call x4, Pallas kernels, logits_grad(): pl.pallas_call(functools.partial(logits_grad_kernel, spans, len(means[0])...  28.9 us
    ppermute x11, waiting for transfers between devices, facing(): return lax.ppermute(a, 'teacher', [(k, k ^ 2) for k in range(teachers)])  16.7 us
    unnamed x108, local copies, waits for them, and re-layouts  16.3 us
    ppermute x11, starting transfers between devices, facing(): return lax.ppermute(a, 'teacher', [(k, k ^ 2) for k in range(teachers)])  13 us
    ppermute x6, starting transfers between devices, from_ahead(): return lax.ppermute(a, 'vocab', pairs)  11.6 us
    pallas_call x2, Pallas kernels, head_grad(): pl.pallas_call(head_grad_kernel, grid=(steps,), in_specs=in_specs, out_sp...  11.5 us
    dot_general x1, matrix products, arrange(): logits = jnp.dot(held['h'][1], student_head, preferred_element_type=f32)  11 us
  transfers between devices with their start and end apart: 38, of which 8 were waited for; matrix products, arithmetic and copies ran while one was open for 19% of the time, Pallas kernels for 43%

profile of v3, /device:TPU:0, one launch (start us, length us, event | category | flops | bytes accessed | tf_op | source)
XLA Modules:
  0.0 272.8 jit_solution(5744513498483703881)
XLA Ops:
  0.6 1.2 multiply_reduce_fusion
  3.6 1.2 multiply_convert_fusion
  4.9 5.1 %collective-permute-start.1 = (bf16[4,16,4352]{2,1,0:T(8,128)(2,1)S(1)}, bf16[4,16,4352]{2,1,0:T(8,128)(2,1)S(1)}, u32[]{:S(2)}, u32[]{:S(2)}) collective-permute-start(bf16[4,16,4352]{2,1,0:T(8,128)(2,1)S(1)} %pad_maximum_fusion.1.refs_0_), channel_id=1, source_target_pairs={{0,6},{1,7},{2,0},{3,1},{4,2},{5,3},{6,4},{7,5},{8,14},{9,15},{10,... | collective-permute-start | bytes 1671176 | tf_op jit(solution)/shard_map/ppermute | solution.py:202
  10.0 1.5 collective-permute-start
  11.5 10.4 %collective-permute-done.1.refs_2_ = bf16[4,16,4352]{2,1,0:T(8,128)(2,1)S(1)} collective-permute-done((bf16[4,16,4352]{2,1,0:T(8,128)(2,1)S(1)}, bf16[4,16,4352]{2,1,0:T(8,128)(2,1)S(1)}, u32[]{:S(2)}, u32[]{:S(2)}) %collective-permute-start.1) | collective-permute-done | bytes 557088 | tf_op jit(solution)/shard_map/ppermute | solution.py:202
  21.9 2.2 collective-permute-done.refs_1_
  24.1 2.1 collective-permute-start.3
  26.2 1.5 collective-permute-start.2
  27.7 13.2 %shard_map.85 = (f32[96,3584]{1,0:T(8,128)S(1)}, f32[96,3584]{1,0:T(8,128)S(1)}) custom-call(bf16[4,16,4352]{2,1,0:T(8,128)(2,1)S(1)} %pad_maximum_fusion.1.refs_0_, bf16[4,16,4352]{2,1,0:T(8,128)(2,1)S(1)} %collective-permute-done.refs_1_, bf16[4,16,4352]{2,1,0:T(8,128)(2,1)S(1)} %collective-permute-done.1.refs_2_, bf16[1,4096,9728]{2,1,0:T(8,128)(2,1)} %refs_5_.7), custom_call_target="tpu_custom_call" | custom-call | flops 1 | bytes 1 | tf_op jit(solution)/shard_map/pallas_call | solution.py:66
  41.5 1.5 collective-permute-start.4
  43.0 13.2 %shard_map.86 = (f32[96,3584]{1,0:T(8,128)S(1)}, f32[96,3584]{1,0:T(8,128)S(1)}) custom-call(bf16[4,16,4352]{2,1,0:T(8,128)(2,1)S(1)} %pad_maximum_fusion.1.refs_0_, bf16[4,16,4352]{2,1,0:T(8,128)(2,1)S(1)} %collective-permute-done.refs_1_, bf16[4,16,4352]{2,1,0:T(8,128)(2,1)S(1)} %collective-permute-done.1.refs_2_, bf16[1,4096,9728]{2,1,0:T(8,128)(2,1)} %refs_5_.7), custom_call_target="tpu_custom_call" | custom-call | flops 1 | bytes 1 | tf_op jit(solution)/shard_map/pallas_call | solution.py:66
  56.5 1.6 collective-permute-start.7
  58.1 1.4 collective-permute-start.8
  59.5 9.9 %shard_map.87 = (f32[96,2560]{1,0:T(8,128)S(1)}, f32[96,2560]{1,0:T(8,128)S(1)}) custom-call(bf16[4,16,4352]{2,1,0:T(8,128)(2,1)S(1)} %pad_maximum_fusion.1.refs_0_, bf16[4,16,4352]{2,1,0:T(8,128)(2,1)S(1)} %collective-permute-done.refs_1_, bf16[4,16,4352]{2,1,0:T(8,128)(2,1)S(1)} %collective-permute-done.1.refs_2_, bf16[1,4096,9728]{2,1,0:T(8,128)(2,1)} %refs_5_.7), custom_call_target="tpu_custom_call" | custom-call | flops 1 | bytes 1 | tf_op jit(solution)/shard_map/pallas_call | solution.py:66
  69.4 3.4 %collective-permute-done.8.refs_4_ = bf16[4,16,4352]{2,1,0:T(8,128)(2,1)S(1)} collective-permute-done((bf16[4,16,4352]{2,1,0:T(8,128)(2,1)S(1)}, bf16[4,16,4352]{2,1,0:T(8,128)(2,1)S(1)}, u32[]{:S(2)}, u32[]{:S(2)}) %collective-permute-start.8) | collective-permute-done | bytes 557088 | tf_op jit(solution)/shard_map/ppermute | solution.py:210
  72.8 1.6 collective-permute-done.7
  74.6 1.6 collective-permute-start.10
  77.0 16.0 %shard_map.88 = (f32[160,3584]{1,0:T(8,128)}, f32[160,3584]{1,0:T(8,128)S(1)}) custom-call(bf16[4,16,4352]{2,1,0:T(8,128)(2,1)S(1)} %collective-permute-done.2.refs_0_, bf16[4,16,4352]{2,1,0:T(8,128)(2,1)S(1)} %collective-permute-done.3.refs_1_, bf16[4,16,4352]{2,1,0:T(8,128)(2,1)S(1)} %collective-permute-done.4.refs_2_, ...), custom_call_target="tpu_custom_call" | custom-call | flops 1 | bytes 1 | tf_op jit(solution)/shard_map/pallas_call | solution.py:66
  93.1 1.4 copy-done.10
  94.5 1.2 exponential_reduce_fusion.5
  95.6 1.7 collective-permute-done.11
  99.2 1.7 add_convert_fusion.6
  100.8 1.6 collective-permute-start.13
  102.8 16.1 %shard_map.89 = (f32[160,3584]{1,0:T(8,128)}, f32[160,3584]{1,0:T(8,128)S(1)}) custom-call(bf16[4,16,4352]{2,1,0:T(8,128)(2,1)S(1)} %collective-permute-done.2.refs_0_, bf16[4,16,4352]{2,1,0:T(8,128)(2,1)S(1)} %collective-permute-done.3.refs_1_, bf16[4,16,4352]{2,1,0:T(8,128)(2,1)S(1)} %collective-permute-done.4.refs_2_, ...), custom_call_target="tpu_custom_call" | custom-call | flops 1 | bytes 1 | tf_op jit(solution)/shard_map/pallas_call | solution.py:66
  118.9 1.5 copy-done.8
  120.6 1.1 exponential_reduce_fusion.4
  123.9 3.4 %add_convert_fusion.4 = (f16[80,3584]{1,0:T(8,128)(2,1)S(1)}, f16[80,3584]{1,0:T(8,128)(2,1)}) fusion(f32[160,3584]{1,0:T(8,128)} %collective-permute-done.15, f32[160,3584]{1,0:T(8,128)} %copy-done.10), kind=kLoop, calls=%fused_computation.12 | loop fusion | flops 1146880 | bytes 5734400 | tf_op jit(solution)/shard_map/convert_element_type | solution.py:338
  128.0 12.3 %shard_map.90 = (f32[160,2560]{1,0:T(8,128)}, f32[160,2560]{1,0:T(8,128)S(1)}) custom-call(bf16[4,16,4352]{2,1,0:T(8,128)(2,1)S(1)} %collective-permute-done.2.refs_0_, bf16[4,16,4352]{2,1,0:T(8,128)(2,1)S(1)} %collective-permute-done.3.refs_1_, bf16[4,16,4352]{2,1,0:T(8,128)(2,1)S(1)} %collective-permute-done.4.refs_2_, ...), custom_call_target="tpu_custom_call" | custom-call | flops 1 | bytes 1 | tf_op jit(solution)/shard_map/pallas_call | solution.py:66
  140.5 1.2 copy-done.23
  143.2 1.6 collective-permute-start.18
  146.5 2.9 %add_convert_fusion.2 = (f16[80,3584]{1,0:T(8,128)(2,1)}, f16[80,3584]{1,0:T(8,128)(2,1)}) fusion(f32[160,3584]{1,0:T(8,128)} %collective-permute-done.17, f32[160,3584]{1,0:T(8,128)S(1)} %copy-done.9), kind=kLoop, calls=%fused_computation.9 | loop fusion | flops 1146880 | bytes 5734400 | tf_op jit(solution)/shard_map/convert_element_type | solution.py:338
  150.0 11.0 %fusion.49 = (f32[128]{0:T(128)S(1)}, f32[128,9728]{1,0:T(8,128)}) fusion(bf16[896,9728]{1,0:T(8,128)(2,1)} %refs_3_.9, bf16[512,1024]{0,1:T(8,128)(2,1)S(1)} %convolution_convert_fusion), kind=kOutput, calls=%fused_computation.202 | convolution fusion | flops 2232614912 | bytes 22643200 | tf_op jit(solution)/shard_map/dot_general | solution.py:387
  161.1 3.2 %exponential_reduce_fusion = f32[128]{0:T(128)S(1)} fusion(f32[128,9728]{1,0:T(8,128)} %get-tuple-element.520, f32[128]{0:T(128)S(1)} %get-tuple-element.519), kind=kLoop, calls=%fused_computation | loop fusion | flops 2490240 | bytes 4981760 | tf_op jit(solution)/shard_map/reduce_sum | solution.py:389
  164.6 1.5 fusion.42
  167.0 1.7 exponential_reduce_fusion.2
  168.8 2.0 collective-permute-done.19
  170.8 2.4 add_convert_fusion.7
  173.2 1.5 collective-permute-start.21
  174.7 1.4 fusion.43
  176.0 2.5 exponential_reduce_fusion.1
  178.5 5.1 %collective-permute-done.21 = f16[80,2560]{1,0:T(8,128)(2,1)S(1)} collective-permute-done((f16[80,2560]{1,0:T(8,128)(2,1)S(1)}, f16[80,2560]{1,0:T(8,128)(2,1)S(1)}, u32[]{:S(2)}, u32[]{:S(2)}) %collective-permute-start.21) | collective-permute-done | bytes 409632 | tf_op jit(solution)/shard_map/ppermute | solution.py:281
  183.6 1.3 fusion.41
  184.9 2.2 exponential_reduce_fusion.3
  187.7 1.5 collective-permute-start.25
  190.3 1.4 collective-permute-start.23
  191.7 1.5 collective-permute-start.22
  193.2 1.4 convert_add_fusion.1.refs_1_
  194.6 2.3 convert_add_fusion.6
  197.9 6.3 %collective-permute-done.22 = f16[80,3584]{1,0:T(8,128)(2,1)S(1)} collective-permute-done((f16[80,3584]{1,0:T(8,128)(2,1)S(1)}, f16[80,3584]{1,0:T(8,128)(2,1)S(1)}, u32[]{:S(2)}, u32[]{:S(2)}) %collective-permute-start.22) | collective-permute-done | bytes 573472 | tf_op jit(solution)/shard_map/ppermute | solution.py:281
  204.2 1.4 collective-permute-start.27
  205.5 1.5 collective-permute-start.26
  207.0 2.2 convert_add_fusion.refs_3_
  210.7 1.1 copy-done.3
  212.9 7.0 %shard_map.92 = (bf16[128,2560]{1,0:T(8,128)(2,1)}, f32[128,1]{1,0:T(8,128)S(1)}, f32[896,128]{1,0:T(8,128)S(1)}) custom-call(f32[48,2560]{1,0:T(8,128)S(1)} %copy-done.11, f32[80,2560]{1,0:T(8,128)S(1)} %copy-done.3, bf16[128,896]{1,0:T(8,128)(2,1)S(1)} %copy.52.refs_4_.refs_2_, bf16[896,9728]{1,0:T(8,128)(2,1)} %refs_3_.9, f32[128,3]{1,0:T(8,128)S(1)} %copy.53.refs_6_.refs_4_), custom_call_target="tpu_custom_call" | custom-call | flops 1 | bytes 1 | tf_op jit(solution)/shard_map/pallas_call | solution.py:147
  219.9 10.2 %shard_map.91 = (bf16[128,7168]{1,0:T(8,128)(2,1)}, f32[128,1]{1,0:T(8,128)S(1)}, f32[896,128]{1,0:T(8,128)S(1)}) custom-call(f32[48,3584]{1,0:T(8,128)S(1)} %copy-done.6, f32[80,3584]{1,0:T(8,128)S(1)} %get-tuple-element.439.refs_1_, f32[48,3584]{1,0:T(8,128)S(1)} %copy-done.7, f32[80,3584]{1,0:T(8,128)S(1)} %copy-done.1, ...), custom_call_target="tpu_custom_call" | custom-call | flops 1 | bytes 1 | tf_op jit(solution)/shard_map/pallas_call | solution.py:147
  231.3 2.0 convert_add_fusion.4.refs_1_
  235.4 1.3 copy-done
  237.7 1.1 copy-done.5
  238.8 6.8 %shard_map.93.c_ref = bf16[128,7168]{1,0:T(8,128)(2,1)S(1)} custom-call(f32[48,3584]{1,0:T(8,128)S(1)} %copy-done.5, f32[80,3584]{1,0:T(8,128)S(1)} %convert_add_fusion.1.refs_1_, f32[48,3584]{1,0:T(8,128)S(1)} %copy-done.4, f32[80,3584]{1,0:T(8,128)S(1)} %copy-done, bf16[128,896]{1,0:T(8,128)(2,1)S(1)} %copy.58.refs_4_, bf16[896,9728]{1,0:T(8,128)(2,1)} %refs_3_.9, ...), custom_call_target="tpu_custom_call" | custom-call | flops 1 | bytes 1 | tf_op jit(solution)/shard_map/pallas_call | solution.py:147
  248.0 2.1 collective-permute-start.32
  250.1 1.1 collective-permute-start.33
  253.5 4.8 %shard_map.94.c_ref = bf16[128,2560]{1,0:T(8,128)(2,1)S(1)} custom-call(f32[48,2560]{1,0:T(8,128)S(1)} %copy-done.12, f32[80,2560]{1,0:T(8,128)S(1)} %copy-done.2, bf16[128,896]{1,0:T(8,128)(2,1)S(1)} %copy.60.refs_2_, bf16[896,9728]{1,0:T(8,128)(2,1)} %refs_3_.9, f32[128,3]{1,0:T(8,128)S(1)} %copy.61.refs_4_), custom_call_target="tpu_custom_call" | custom-call | flops 1 | bytes 1 | tf_op jit(solution)/shard_map/pallas_call | solution.py:147
  260.1 6.6 %shard_map.95.refs_0_ = f32[224,9728]{1,0:T(8,128)} custom-call(bf16[224,512]{1,0:T(8,128)(2,1)S(1)} %dynamic-slice_bitcast_fusion.h_ref, bf16[128,7168]{1,0:T(8,128)(2,1)} %collective-permute-done.35.a_ref, bf16[128,7168]{1,0:T(8,128)(2,1)} %collective-permute-done.30.b_ref, bf16[128,7168]{1,0:T(8,128)(2,1)S(1)} %shard_map.93.c_ref, ...), custom_call_target="tpu_custom_call" | custom-call | flops 1 | bytes 1 | tf_op jit(solution)/shard_map/pallas_call | solution.py:181
  267.9 4.9 %shard_map.96 = f32[224,9728]{1,0:T(8,128)} custom-call(bf16[224,512]{1,0:T(8,128)(2,1)S(1)} %dynamic-slice_bitcast_fusion.h_ref, bf16[128,2560]{1,0:T(8,128)(2,1)S(1)} %collective-permute-done.37.a_ref, bf16[128,2560]{1,0:T(8,128)(2,1)} %collective-permute-done.34.b_ref, bf16[128,2560]{1,0:T(8,128)(2,1)S(1)} %shard_map.94.c_ref, ...), custom_call_target="tpu_custom_call", output_to_operand_aliasing={{}: (5, {})} | custom-call | flops 1 | bytes 1 | tf_op jit(solution)/shard_map/pallas_call | solution.py:181
  (246 shorter events, 30.5 us)
Async XLA Ops:
  4.9 17.0 %collective-permute-start.1 = (bf16[4,16,4352]{2,1,0:T(8,128)(2,1)S(1)}, bf16[4,16,4352]{2,1,0:T(8,128)(2,1)S(1)}, u32[]{:S(2)}, u32[]{:S(2)}) collective-permute-start(bf16[4,16,4352]{2,1,0:T(8,128)(2,1)S(1)} %pad_maximum_fusion.1.refs_0_), channel_id=1, source_target_pairs={{0,6},{1,7},{2,0},{3,1},{4,2},{5,3},{6,4},{7,5},{8,14},{9,15},{10,... | collective-permute-start | bytes 1671176 | tf_op jit(solution)/shard_map/ppermute | solution.py:202
  10.0 14.1 %collective-permute-start = (bf16[4,16,4352]{2,1,0:T(8,128)(2,1)S(1)}, bf16[4,16,4352]{2,1,0:T(8,128)(2,1)S(1)}, u32[]{:S(2)}, u32[]{:S(2)}) collective-permute-start(bf16[4,16,4352]{2,1,0:T(8,128)(2,1)S(1)} %pad_maximum_fusion.1.refs_0_), channel_id=1, source_target_pairs={{0,1},{1,0},{2,3},{3,2},{4,5},{5,4},{6,7},{7,6},{8,9},{9,8},{10,11... | collective-permute-start | bytes 1671176 | tf_op jit(solution)/shard_map/ppermute | solution.py:210
  24.1 16.8 %collective-permute-start.3 = (bf16[4,16,4352]{2,1,0:T(8,128)(2,1)S(1)}, bf16[4,16,4352]{2,1,0:T(8,128)(2,1)S(1)}, u32[]{:S(2)}, u32[]{:S(2)}) collective-permute-start(bf16[4,16,4352]{2,1,0:T(8,128)(2,1)S(1)} %collective-permute-done.1.refs_2_), channel_id=1, source_target_pairs={{0,6},{1,7},{2,0},{3,1},{4,2},{5,3},{6,4},{7,5},{8,14},{9,15},{10,... | collective-permute-start | bytes 1671176 | tf_op jit(solution)/shard_map/ppermute | solution.py:202
  26.2 14.8 %collective-permute-start.2 = (bf16[4,16,4352]{2,1,0:T(8,128)(2,1)S(1)}, bf16[4,16,4352]{2,1,0:T(8,128)(2,1)S(1)}, u32[]{:S(2)}, u32[]{:S(2)}) collective-permute-start(bf16[4,16,4352]{2,1,0:T(8,128)(2,1)S(1)} %collective-permute-done.1.refs_2_), channel_id=1, source_target_pairs={{0,1},{1,0},{2,3},{3,2},{4,5},{5,4},{6,7},{7,6},{8,9},{9,8},{10,11... | collective-permute-start | bytes 1671176 | tf_op jit(solution)/shard_map/ppermute | solution.py:210
  40.9 15.3 %collective-permute-start.6 = (f32[96,3584]{1,0:T(8,128)S(1)}, f32[96,3584]{1,0:T(8,128)S(1)}, u32[]{:S(2)}, u32[]{:S(2)}) collective-permute-start(f32[96,3584]{1,0:T(8,128)S(1)} %get-tuple-element.252), channel_id=1, source_target_pairs={{0,8},{8,0},{16,24},{24,16},{1,9},{9,1},{17,25},{25,17},{2,10},{10... | collective-permute-start | bytes 4128776 | tf_op jit(solution)/shard_map/ppermute | solution.py:278
  41.0 15.2 %collective-permute-start.5 = (bf16[4,16,4352]{2,1,0:T(8,128)(2,1)S(1)}, bf16[4,16,4352]{2,1,0:T(8,128)(2,1)S(1)}, u32[]{:S(2)}, u32[]{:S(2)}) collective-permute-start(bf16[4,16,4352]{2,1,0:T(8,128)(2,1)S(1)} %collective-permute-done.3.refs_1_), channel_id=1, source_target_pairs={{0,6},{1,7},{2,0},{3,1},{4,2},{5,3},{6,4},{7,5},{8,14},{9,15},{10,... | collective-permute-start | bytes 1671176 | tf_op jit(solution)/shard_map/ppermute | solution.py:202
  41.5 14.8 %collective-permute-start.4 = (bf16[4,16,4352]{2,1,0:T(8,128)(2,1)S(1)}, bf16[4,16,4352]{2,1,0:T(8,128)(2,1)S(1)}, u32[]{:S(2)}, u32[]{:S(2)}) collective-permute-start(bf16[4,16,4352]{2,1,0:T(8,128)(2,1)S(1)} %collective-permute-done.3.refs_1_), channel_id=1, source_target_pairs={{0,1},{1,0},{2,3},{3,2},{4,5},{5,4},{6,7},{7,6},{8,9},{9,8},{10,11... | collective-permute-start | bytes 1671176 | tf_op jit(solution)/shard_map/ppermute | solution.py:210
  56.3 18.1 %collective-permute-start.9 = (f32[96,3584]{1,0:T(8,128)S(1)}, f32[96,3584]{1,0:T(8,128)S(1)}, u32[]{:S(2)}, u32[]{:S(2)}) collective-permute-start(f32[96,3584]{1,0:T(8,128)S(1)} %get-tuple-element.265), channel_id=1, source_target_pairs={{0,8},{8,0},{16,24},{24,16},{1,9},{9,1},{17,25},{25,17},{2,10},{10... | collective-permute-start | bytes 4128776 | tf_op jit(solution)/shard_map/ppermute | solution.py:278
  56.5 36.6 %copy-start.18 = (f16[96,3584]{1,0:T(8,128)(2,1)}, f16[96,3584]{1,0:T(8,128)(2,1)S(1)}, u32[]{:S(2)}) copy-start(f16[96,3584]{1,0:T(8,128)(2,1)S(1)} %add_convert_fusion.1) | copy-start | bytes 2064388
  56.5 17.9 %collective-permute-start.7 = (f16[96,3584]{1,0:T(8,128)(2,1)S(1)}, f16[96,3584]{1,0:T(8,128)(2,1)S(1)}, u32[]{:S(2)}, u32[]{:S(2)}) collective-permute-start(f16[96,3584]{1,0:T(8,128)(2,1)S(1)} %add_convert_fusion.1), channel_id=1, source_target_pairs={{0,16},{8,24},{16,0},{24,8},{1,17},{9,25},{17,1},{25,9},{2,18},{10... | collective-permute-start | bytes 2064392 | tf_op jit(solution)/shard_map/ppermute | solution.py:281
  58.1 14.7 %collective-permute-start.8 = (bf16[4,16,4352]{2,1,0:T(8,128)(2,1)S(1)}, bf16[4,16,4352]{2,1,0:T(8,128)(2,1)S(1)}, u32[]{:S(2)}, u32[]{:S(2)}) collective-permute-start(bf16[4,16,4352]{2,1,0:T(8,128)(2,1)S(1)} %collective-permute-done.5.refs_3_), channel_id=1, source_target_pairs={{0,1},{1,0},{2,3},{3,2},{4,5},{5,4},{6,7},{7,6},{8,9},{9,8},{10,11... | collective-permute-start | bytes 1671176 | tf_op jit(solution)/shard_map/ppermute | solution.py:210
  69.4 7.5 %copy-start.15 = (f32[96,2560]{1,0:T(8,128)}, f32[96,2560]{1,0:T(8,128)S(1)}, u32[]{:S(2)}) copy-start(f32[96,2560]{1,0:T(8,128)S(1)} %get-tuple-element.290) | copy-start | bytes 2949124
  74.4 18.7 %copy-start.34 = (f16[96,3584]{1,0:T(8,128)(2,1)}, f16[96,3584]{1,0:T(8,128)(2,1)S(1)}, u32[]{:S(2)}) copy-start(f16[96,3584]{1,0:T(8,128)(2,1)S(1)} %collective-permute-done.7) | copy-start | bytes 2064388
  74.6 46.0 %copy-start.20 = (f16[96,3584]{1,0:T(8,128)(2,1)}, f16[96,3584]{1,0:T(8,128)(2,1)S(1)}, u32[]{:S(2)}) copy-start(f16[96,3584]{1,0:T(8,128)(2,1)S(1)} %add_convert_fusion) | copy-start | bytes 2064388
  74.6 22.7 %collective-permute-start.10 = (f16[96,3584]{1,0:T(8,128)(2,1)S(1)}, f16[96,3584]{1,0:T(8,128)(2,1)S(1)}, u32[]{:S(2)}, u32[]{:S(2)}) collective-permute-start(f16[96,3584]{1,0:T(8,128)(2,1)S(1)} %add_convert_fusion), channel_id=1, source_target_pairs={{0,16},{8,24},{16,0},{24,8},{1,17},{9,25},{17,1},{25,9},{2,18},{10... | collective-permute-start | bytes 2064392 | tf_op jit(solution)/shard_map/ppermute | solution.py:281
  76.1 21.2 %collective-permute-start.12 = (f32[96,2560]{1,0:T(8,128)S(1)}, f32[96,2560]{1,0:T(8,128)S(1)}, u32[]{:S(2)}, u32[]{:S(2)}) collective-permute-start(f32[96,2560]{1,0:T(8,128)S(1)} %get-tuple-element.283), channel_id=1, source_target_pairs={{0,8},{8,0},{16,24},{24,16},{1,9},{9,1},{17,25},{25,17},{2,10},{10... | collective-permute-start | bytes 2949128 | tf_op jit(solution)/shard_map/ppermute | solution.py:278
  76.2 16.9 %copy-start.42 = (bf16[8,4,2,8,256]{4,3,1,2,0:T(8,128)(2,1)}, bf16[8,4,2,8,256]{4,3,1,2,0:T(8,128)(2,1)S(1)}, u32[]{:S(2)}) copy-start(bf16[8,4,2,8,256]{4,3,1,2,0:T(8,128)(2,1)S(1)} %copy.66) | copy-start | bytes 786436
  76.2 21.1 %collective-permute-start.11 = (bf16[8,16,1024]{2,1,0:T(8,128)(2,1)S(1)}, bf16[8,16,1024]{2,1,0:T(8,128)(2,1)S(1)}, u32[]{:S(2)}, u32[]{:S(2)}) collective-permute-start(bf16[8,16,1024]{2,1,0:T(8,128)(2,1)S(1)} %bitcast.138), channel_id=1, source_target_pairs={{0,16},{8,24},{16,0},{24,8},{1,17},{9,25},{17,1},{25,9},{2,18},{10... | collective-permute-start | bytes 786440 | tf_op jit(solution)/shard_map/ppermute | solution.py:281
  99.2 23.4 %collective-permute-start.15 = (f32[160,3584]{1,0:T(8,128)}, f32[160,3584]{1,0:T(8,128)}, u32[]{:S(2)}, u32[]{:S(2)}) collective-permute-start(f32[160,3584]{1,0:T(8,128)} %get-tuple-element.304), channel_id=1, source_target_pairs={{0,8},{8,0},{16,24},{24,16},{1,9},{9,1},{17,25},{25,17},{2,10},{10... | collective-permute-start | bytes 6881288 | tf_op jit(solution)/shard_map/ppermute | solution.py:278
  100.8 18.1 %copy-start.22 = (f16[96,2560]{1,0:T(8,128)(2,1)}, f16[96,2560]{1,0:T(8,128)(2,1)S(1)}, u32[]{:S(2)}) copy-start(f16[96,2560]{1,0:T(8,128)(2,1)S(1)} %add_convert_fusion.6) | copy-start | bytes 1474564
  100.8 20.9 %collective-permute-start.13 = (f16[96,2560]{1,0:T(8,128)(2,1)S(1)}, f16[96,2560]{1,0:T(8,128)(2,1)S(1)}, u32[]{:S(2)}, u32[]{:S(2)}) collective-permute-start(f16[96,2560]{1,0:T(8,128)(2,1)S(1)} %add_convert_fusion.6), channel_id=1, source_target_pairs={{0,16},{8,24},{16,0},{24,8},{1,17},{9,25},{17,1},{25,9},{2,18},{10... | collective-permute-start | bytes 1474568 | tf_op jit(solution)/shard_map/ppermute | solution.py:281
  102.5 16.5 %copy-start.28 = (bf16[2,8,16,1024]{3,2,1,0:T(8,128)(2,1)}, bf16[2,8,16,1024]{3,2,1,0:T(8,128)(2,1)S(1)}, u32[]{:S(2)}) copy-start(bf16[2,8,16,1024]{3,2,1,0:T(8,128)(2,1)S(1)} %pad_maximum_fusion.2) | copy-start | bytes 1572868
  102.5 19.3 %collective-permute-start.14 = (bf16[2,8,16,1024]{3,2,1,0:T(8,128)(2,1)S(1)}, bf16[2,8,16,1024]{3,2,1,0:T(8,128)(2,1)S(1)}, u32[]{:S(2)}, u32[]{:S(2)}) collective-permute-start(bf16[2,8,16,1024]{3,2,1,0:T(8,128)(2,1)S(1)} %pad_maximum_fusion.2), channel_id=1, source_target_pairs={{0,8},{8,0},{16,24},{24,16},{1,9},{9,1},{17,25},{25,17},{2,10},{10... | collective-permute-start | bytes 1572872 | tf_op jit(solution)/shard_map/ppermute | solution.py:278
  102.8 17.6 %copy-start.37 = (f16[96,3584]{1,0:T(8,128)(2,1)S(1)}, f16[96,3584]{1,0:T(8,128)(2,1)}, u32[]{:S(2)}) copy-start(f16[96,3584]{1,0:T(8,128)(2,1)} %copy-done.36) | copy-start | bytes 2064388
  123.3 19.9 %collective-permute-start.17 = (f32[160,3584]{1,0:T(8,128)}, f32[160,3584]{1,0:T(8,128)}, u32[]{:S(2)}, u32[]{:S(2)}) collective-permute-start(f32[160,3584]{1,0:T(8,128)} %get-tuple-element.330), channel_id=1, source_target_pairs={{0,8},{8,0},{16,24},{24,16},{1,9},{9,1},{17,25},{25,17},{2,10},{10... | collective-permute-start | bytes 6881288 | tf_op jit(solution)/shard_map/ppermute | solution.py:278
  127.3 13.0 %copy-start.25 = (f16[80,3584]{1,0:T(8,128)(2,1)}, f16[80,3584]{1,0:T(8,128)(2,1)S(1)}, u32[]{:S(2)}) copy-start(f16[80,3584]{1,0:T(8,128)(2,1)S(1)} %get-tuple-element.397) | copy-start | bytes 1720324
  127.3 15.9 %collective-permute-start.16 = (f16[80,3584]{1,0:T(8,128)(2,1)S(1)}, f16[80,3584]{1,0:T(8,128)(2,1)}, u32[]{:S(2)}, u32[]{:S(2)}) collective-permute-start(f16[80,3584]{1,0:T(8,128)(2,1)S(1)} %get-tuple-element.397), channel_id=1, source_target_pairs={{0,16},{8,24},{16,0},{24,8},{1,17},{9,25},{17,1},{25,9},{2,18},{10... | collective-permute-start | bytes 1720328 | tf_op jit(solution)/shard_map/ppermute | solution.py:281
  128.0 12.3 %copy-start.29 = (bf16[2,8,16,1024]{3,2,1,0:T(8,128)(2,1)S(1)}, bf16[2,8,16,1024]{3,2,1,0:T(8,128)(2,1)}, u32[]{:S(2)}) copy-start(bf16[2,8,16,1024]{3,2,1,0:T(8,128)(2,1)} %copy-done.28) | copy-start | bytes 1572868
  128.0 12.4 %copy-start.47 = (bf16[2,8,16,1024]{3,2,1,0:T(8,128)(2,1)S(1)}, bf16[2,8,16,1024]{3,2,1,0:T(8,128)(2,1)}, u32[]{:S(2)}) copy-start(bf16[2,8,16,1024]{3,2,1,0:T(8,128)(2,1)} %copy-done.46) | copy-start | bytes 1572868
  143.2 25.5 %collective-permute-start.18 = (f16[80,3584]{1,0:T(8,128)(2,1)}, f16[80,3584]{1,0:T(8,128)(2,1)}, u32[]{:S(2)}, u32[]{:S(2)}) collective-permute-start(f16[80,3584]{1,0:T(8,128)(2,1)} %get-tuple-element.347), channel_id=1, source_target_pairs={{0,16},{8,24},{16,0},{24,8},{1,17},{9,25},{17,1},{25,9},{2,18},{10... | collective-permute-start | bytes 1720328 | tf_op jit(solution)/shard_map/ppermute | solution.py:281
  149.5 21.3 %collective-permute-start.19 = (f16[80,3584]{1,0:T(8,128)(2,1)}, f16[80,3584]{1,0:T(8,128)(2,1)}, u32[]{:S(2)}, u32[]{:S(2)}) collective-permute-start(f16[80,3584]{1,0:T(8,128)(2,1)} %get-tuple-element.430), channel_id=1, source_target_pairs={{0,16},{8,24},{16,0},{24,8},{1,17},{9,25},{17,1},{25,9},{2,18},{10... | collective-permute-start | bytes 1720328 | tf_op jit(solution)/shard_map/ppermute | solution.py:281
  150.0 20.8 %collective-permute-start.20 = (f32[160,2560]{1,0:T(8,128)}, f32[160,2560]{1,0:T(8,128)}, u32[]{:S(2)}, u32[]{:S(2)}) collective-permute-start(f32[160,2560]{1,0:T(8,128)} %get-tuple-element.355), channel_id=1, source_target_pairs={{0,8},{8,0},{16,24},{24,16},{1,9},{9,1},{17,25},{25,17},{2,10},{10... | collective-permute-start | bytes 4915208 | tf_op jit(solution)/shard_map/ppermute | solution.py:278
  167.0 3.7 %copy-start.14 = (f32[160,2560]{1,0:T(8,128)S(1)}, f32[160,2560]{1,0:T(8,128)}, u32[]{:S(2)}) copy-start(f32[160,2560]{1,0:T(8,128)} %copy-done.13) | copy-start | bytes 4915204
  170.7 3.9 %copy-start.16 = (f16[80,3584]{1,0:T(8,128)(2,1)S(1)}, f16[80,3584]{1,0:T(8,128)(2,1)}, u32[]{:S(2)}) copy-start(f16[80,3584]{1,0:T(8,128)(2,1)} %get-tuple-element.400) | copy-start | bytes 1720324
  173.2 5.3 %copy-start.32 = (f16[80,2560]{1,0:T(8,128)(2,1)}, f16[80,2560]{1,0:T(8,128)(2,1)S(1)}, u32[]{:S(2)}) copy-start(f16[80,2560]{1,0:T(8,128)(2,1)S(1)} %get-tuple-element.432) | copy-start | bytes 1228804
  173.2 10.5 %collective-permute-start.21 = (f16[80,2560]{1,0:T(8,128)(2,1)S(1)}, f16[80,2560]{1,0:T(8,128)(2,1)S(1)}, u32[]{:S(2)}, u32[]{:S(2)}) collective-permute-start(f16[80,2560]{1,0:T(8,128)(2,1)S(1)} %get-tuple-element.432), channel_id=1, source_target_pairs={{0,16},{8,24},{16,0},{24,8},{1,17},{9,25},{17,1},{25,9},{2,18},{10... | collective-permute-start | bytes 1228808 | tf_op jit(solution)/shard_map/ppermute | solution.py:281
  183.6 8.1 %copy-start.17 = (f16[80,3584]{1,0:T(8,128)(2,1)S(1)}, f16[80,3584]{1,0:T(8,128)(2,1)}, u32[]{:S(2)}) copy-start(f16[80,3584]{1,0:T(8,128)(2,1)} %get-tuple-element.400) | copy-start | bytes 1720324
  187.7 6.9 %copy-start.19 = (f16[96,3584]{1,0:T(8,128)(2,1)S(1)}, f16[96,3584]{1,0:T(8,128)(2,1)}, u32[]{:S(2)}) copy-start(f16[96,3584]{1,0:T(8,128)(2,1)} %copy-done.18) | copy-start | bytes 2064388
  187.7 6.9 %copy-start.21 = (f16[96,3584]{1,0:T(8,128)(2,1)S(1)}, f16[96,3584]{1,0:T(8,128)(2,1)}, u32[]{:S(2)}) copy-start(f16[96,3584]{1,0:T(8,128)(2,1)} %copy-done.20) | copy-start | bytes 2064388
  187.7 6.9 %copy-start.35 = (f16[96,3584]{1,0:T(8,128)(2,1)S(1)}, f16[96,3584]{1,0:T(8,128)(2,1)}, u32[]{:S(2)}) copy-start(f16[96,3584]{1,0:T(8,128)(2,1)} %copy-done.34) | copy-start | bytes 2064388
  187.7 10.1 %collective-permute-start.25 = (f32[2,2,8,16]{3,2,1,0:T(8,128)S(1)}, f32[2,2,8,16]{3,2,1,0:T(8,128)S(1)}, u32[]{:S(2)}, u32[]{:S(2)}) collective-permute-start(f32[2,2,8,16]{3,2,1,0:T(8,128)S(1)} %pad_maximum_fusion.4), channel_id=1, source_target_pairs={{0,2},{1,3},{2,4},{3,5},{4,6},{5,7},{6,0},{7,1},{8,10},{9,11},{10,... | collective-permute-start | bytes 6152 | tf_op jit(solution)/shard_map/ppermute | solution.py:202
  189.2 8.6 %collective-permute-start.24 = (f32[2,2,8,16]{3,2,1,0:T(8,128)S(1)}, f32[2,2,8,16]{3,2,1,0:T(8,128)S(1)}, u32[]{:S(2)}, u32[]{:S(2)}) collective-permute-start(f32[2,2,8,16]{3,2,1,0:T(8,128)S(1)} %pad_maximum_fusion.4), channel_id=1, source_target_pairs={{0,4},{1,5},{2,6},{3,7},{4,0},{5,1},{6,2},{7,3},{8,12},{9,13},{10,... | collective-permute-start | bytes 6152 | tf_op jit(solution)/shard_map/ppermute | solution.py:202
  190.3 7.5 %collective-permute-start.23 = (f32[2,2,8,16]{3,2,1,0:T(8,128)S(1)}, f32[2,2,8,16]{3,2,1,0:T(8,128)S(1)}, u32[]{:S(2)}, u32[]{:S(2)}) collective-permute-start(f32[2,2,8,16]{3,2,1,0:T(8,128)S(1)} %pad_maximum_fusion.4), channel_id=1, source_target_pairs={{0,6},{1,7},{2,0},{3,1},{4,2},{5,3},{6,4},{7,5},{8,14},{9,15},{10,... | collective-permute-start | bytes 6152 | tf_op jit(solution)/shard_map/ppermute | solution.py:202
  191.7 12.5 %collective-permute-start.22 = (f16[80,3584]{1,0:T(8,128)(2,1)S(1)}, f16[80,3584]{1,0:T(8,128)(2,1)S(1)}, u32[]{:S(2)}, u32[]{:S(2)}) collective-permute-start(f16[80,3584]{1,0:T(8,128)(2,1)S(1)} %copy-done.17), channel_id=1, source_target_pairs={{0,16},{8,24},{16,0},{24,8},{1,17},{9,25},{17,1},{25,9},{2,18},{10... | collective-permute-start | bytes 1720328 | tf_op jit(solution)/shard_map/ppermute | solution.py:281
  204.2 5.1 %copy-start.45 = (bf16[128,896]{0,1:T(8,128)(2,1)S(1)}, bf16[128,896]{0,1:T(8,128)(2,1)}, u32[]{:S(2)}) copy-start(bf16[128,896]{0,1:T(8,128)(2,1)} %get-tuple-element.435) | copy-start | bytes 688132
  204.2 5.3 %collective-permute-start.27 = (f32[2,2,8,16]{3,2,1,0:T(8,128)S(1)}, f32[2,2,8,16]{3,2,1,0:T(8,128)S(1)}, u32[]{:S(2)}, u32[]{:S(2)}) collective-permute-start(f32[2,2,8,16]{3,2,1,0:T(8,128)S(1)} %pad_maximum_fusion.5), channel_id=1, source_target_pairs={{0,1},{1,0},{2,3},{3,2},{4,5},{5,4},{6,7},{7,6},{8,9},{9,8},{10,11... | collective-permute-start | bytes 6152 | tf_op jit(solution)/shard_map/ppermute | solution.py:210
  205.5 24.8 %collective-permute-start.26 = (f16[80,2560]{1,0:T(8,128)(2,1)}, f16[80,2560]{1,0:T(8,128)(2,1)}, u32[]{:S(2)}, u32[]{:S(2)}) collective-permute-start(f16[80,2560]{1,0:T(8,128)(2,1)} %get-tuple-element.433), channel_id=1, source_target_pairs={{0,16},{8,24},{16,0},{24,8},{1,17},{9,25},{17,1},{25,9},{2,18},{10... | collective-permute-start | bytes 1228808 | tf_op jit(solution)/shard_map/ppermute | solution.py:281
  210.0 23.3 %collective-permute-start.28 = (f32[2,128]{1,0:T(2,128)S(1)}, f32[2,128]{1,0:T(2,128)S(1)}, u32[]{:S(2)}, u32[]{:S(2)}) collective-permute-start(f32[2,128]{1,0:T(2,128)S(1)} %pad_maximum_fusion.12), channel_id=1, source_target_pairs={{0,16},{8,24},{16,0},{24,8},{1,17},{9,25},{17,1},{25,9},{2,18},{10... | collective-permute-start | bytes 3080 | tf_op jit(solution)/shard_map/ppermute | solution.py:281
  212.9 7.0 %copy-start.1 = (f32[80,3584]{1,0:T(8,128)S(1)}, f32[80,3584]{1,0:T(8,128)}, u32[]{:S(2)}) copy-start(f32[80,3584]{1,0:T(8,128)} %get-tuple-element.440.refs_3_) | copy-start | bytes 3440644
  212.9 7.0 %copy-start.6 = (f32[48,3584]{1,0:T(8,128)S(1)}, f32[48,3584]{1,0:T(8,128)}, u32[]{:S(2)}) copy-start(f32[48,3584]{1,0:T(8,128)} %get-tuple-element.436.refs_0_) | copy-start | bytes 2064388
  212.9 7.0 %copy-start.7 = (f32[48,3584]{1,0:T(8,128)S(1)}, f32[48,3584]{1,0:T(8,128)}, u32[]{:S(2)}) copy-start(f32[48,3584]{1,0:T(8,128)} %get-tuple-element.437.refs_2_) | copy-start | bytes 2064388
  233.3 13.5 %collective-permute-start.30 = (bf16[128,7168]{1,0:T(8,128)(2,1)}, bf16[128,7168]{1,0:T(8,128)(2,1)}, u32[]{:S(2)}, u32[]{:S(2)}) collective-permute-start(bf16[128,7168]{1,0:T(8,128)(2,1)} %get-tuple-element.452.d_ref), channel_id=1, source_target_pairs={{0,8},{8,0},{16,24},{24,16},{1,9},{9,1},{17,25},{25,17},{2,10},{10... | collective-permute-start | bytes 5505032 | tf_op jit(solution)/shard_map/ppermute | solution.py:278
  234.2 11.4 %collective-permute-start.29 = (f32[4,16,1024]{2,1,0:T(8,128)}, f32[4,16,1024]{2,1,0:T(8,128)}, u32[]{:S(2)}, u32[]{:S(2)}) collective-permute-start(f32[4,16,1024]{2,1,0:T(8,128)} %slice_bitcast_fusion), channel_id=1, source_target_pairs={{0,1},{1,0},{2,3},{3,2},{4,5},{5,4},{6,7},{7,6},{8,9},{9,8},{10,11... | collective-permute-start | bytes 786440 | tf_op jit(solution)/shard_map/ppermute | solution.py:210
  238.8 6.9 %copy-start.27 = (f32[128,1024]{1,0:T(8,128)S(1)}, f32[128,1024]{1,0:T(8,128)}, u32[]{:S(2)}) copy-start(f32[128,1024]{1,0:T(8,128)} %copy-done.26) | copy-start | bytes 1572868
  245.6 6.7 %copy-start.31 = (bf16[128,896]{0,1:T(8,128)(2,1)S(1)}, bf16[128,896]{0,1:T(8,128)(2,1)}, u32[]{:S(2)}) copy-start(bf16[128,896]{0,1:T(8,128)(2,1)} %get-tuple-element.469) | copy-start | bytes 688132
  245.6 6.8 %copy-start.2 = (f32[80,2560]{1,0:T(8,128)S(1)}, f32[80,2560]{1,0:T(8,128)}, u32[]{:S(2)}) copy-start(f32[80,2560]{1,0:T(8,128)} %convert_add_fusion.4.refs_1_) | copy-start | bytes 2457604
  246.7 5.4 %copy-start.41 = (f32[4,16,1024]{2,1,0:T(8,128)}, f32[4,16,1024]{2,1,0:T(8,128)S(1)}, u32[]{:S(2)}) copy-start(f32[4,16,1024]{2,1,0:T(8,128)S(1)} %fusion.1) | copy-start | bytes 786436
  246.8 12.5 %collective-permute-start.35 = (bf16[128,7168]{1,0:T(8,128)(2,1)S(1)}, bf16[128,7168]{1,0:T(8,128)(2,1)}, u32[]{:S(2)}, u32[]{:S(2)}) collective-permute-start(bf16[128,7168]{1,0:T(8,128)(2,1)S(1)} %shard_map.93.c_ref), channel_id=1, source_target_pairs={{0,8},{8,0},{16,24},{24,16},{1,9},{9,1},{17,25},{25,17},{2,10},{10... | collective-permute-start | bytes 5505032 | tf_op jit(solution)/shard_map/ppermute | solution.py:278
  247.1 12.2 %collective-permute-start.34 = (bf16[128,2560]{1,0:T(8,128)(2,1)}, bf16[128,2560]{1,0:T(8,128)(2,1)}, u32[]{:S(2)}, u32[]{:S(2)}) collective-permute-start(bf16[128,2560]{1,0:T(8,128)(2,1)} %get-tuple-element.465.d_ref), channel_id=1, source_target_pairs={{0,8},{8,0},{16,24},{24,16},{1,9},{9,1},{17,25},{25,17},{2,10},{10... | collective-permute-start | bytes 1966088 | tf_op jit(solution)/shard_map/ppermute | solution.py:278
  248.0 10.3 %collective-permute-start.32 = (f32[16,1024]{1,0:T(8,128)}, f32[16,1024]{1,0:T(8,128)S(1)}, u32[]{:S(2)}, u32[]{:S(2)}) collective-permute-start(f32[16,1024]{1,0:T(8,128)} %get-tuple-element.505), channel_id=1, source_target_pairs={{0,4},{1,5},{2,6},{3,7},{4,0},{5,1},{6,2},{7,3},{8,12},{9,13},{10,... | collective-permute-start | bytes 196616 | tf_op jit(solution)/shard_map/ppermute | solution.py:207
  250.1 8.2 %collective-permute-start.33 = (f32[16,1024]{1,0:T(8,128)}, f32[16,1024]{1,0:T(8,128)}, u32[]{:S(2)}, u32[]{:S(2)}) collective-permute-start(f32[16,1024]{1,0:T(8,128)} %get-tuple-element.506), channel_id=1, source_target_pairs={{0,6},{1,7},{2,0},{3,1},{4,2},{5,3},{6,4},{7,5},{8,14},{9,15},{10,... | collective-permute-start | bytes 196616 | tf_op jit(solution)/shard_map/ppermute | solution.py:207
  251.3 7.1 %collective-permute-start.31 = (f32[16,1024]{1,0:T(8,128)}, f32[16,1024]{1,0:T(8,128)}, u32[]{:S(2)}, u32[]{:S(2)}) collective-permute-start(f32[16,1024]{1,0:T(8,128)} %get-tuple-element.507), channel_id=1, source_target_pairs={{0,2},{1,3},{2,4},{3,5},{4,6},{5,7},{6,0},{7,1},{8,10},{9,11},{10,... | collective-permute-start | bytes 196616 | tf_op jit(solution)/shard_map/ppermute | solution.py:207
  259.3 8.6 %collective-permute-start.37 = (bf16[128,2560]{1,0:T(8,128)(2,1)S(1)}, bf16[128,2560]{1,0:T(8,128)(2,1)S(1)}, u32[]{:S(2)}, u32[]{:S(2)}) collective-permute-start(bf16[128,2560]{1,0:T(8,128)(2,1)S(1)} %shard_map.94.c_ref), channel_id=1, source_target_pairs={{0,8},{8,0},{16,24},{24,16},{1,9},{9,1},{17,25},{25,17},{2,10},{10... | collective-permute-start | bytes 1966088 | tf_op jit(solution)/shard_map/ppermute | solution.py:278
  259.4 7.3 %collective-permute-start.36 = (f32[16,1024]{1,0:T(8,128)S(1)}, f32[16,1024]{1,0:T(8,128)S(1)}, u32[]{:S(2)}, u32[]{:S(2)}) collective-permute-start(f32[16,1024]{1,0:T(8,128)S(1)} %bitcast_add_fusion), channel_id=1, source_target_pairs={{0,0},{1,4},{2,8},{3,12},{4,16},{5,20},{6,24},{7,28},{8,1},{9,5},{... | collective-permute-start | bytes 196616 | tf_op jit(solution)/shard_map/ppermute | solution.py:480
  (24 other events, 37.3 us)
